TPU v7x, 32 devices: a whole 2x2x4 slice. The times are simulated.
32 devices in a mesh: tile: 4 (over y, x), src: 8 (over z, core).
Axes of the slice: x: 2, y: 2, z: 4, core: 2. Of those that a mesh axis runs over, the one named last changes fastest.
Arguments:
- log_conductivity: float32 [32, 8, 512], P('src', None, 'tile'), may hold values from -1 to 1
- cluster_labels: int32 [32, 8, 512], P('src', None, 'tile'), may hold values from 0 to 3
- cluster_means: float32 [4], replicated, may hold values from -1 to 1
- cluster_vars: float32 [4], replicated, may hold values from 0.25 to 1
- source_cells: int32 [8, 2], P('src'), may hold values from 0 to 131071
- receiver_cells: int32 [256, 2], replicated, may hold values from 0 to 131071
- observed: float32 [8, 256], P('src'), may hold values from -6 to 6
- warm_potential: float32 [8, 32, 8, 512], P('src', None, None, 'tile'), may hold values from -6 to 6
- warm_adjoint: float32 [8, 32, 8, 512], P('src', None, None, 'tile'), may hold values from -6 to 6
Outputs:
- potentials: float32 [8, 32, 8, 512], P('src', None, None, 'tile')
- adjoints: float32 [8, 32, 8, 512], P('src', None, None, 'tile')
- misfit: float32 [8, 256], P('src')
- gradient: float32 [32, 8, 512], P('src', None, 'tile')
Inputs may be any that keep to these rules, and one draw needn't show every extreme that they name: `source_cells`: flat cell indices. `receiver_cells`: flat cell indices.
All inputs are finite; a program needn't handle non-finite values.
Results may differ from a plain program's by a relative error of at most 0.0003.
Values sent between devices are 32-bit elements; how exact they have to be, the bound alone decides.
No kernel may reach another device: no remote copies, remote signals or barrier semaphores. Data moves between devices by JAX's collectives and lax.ppermute only.
A program may use at most 64 MiB of HBM per device.

v0:
```python
import jax
import jax.numpy as jnp
from jax import lax
from jax.sharding import PartitionSpec as P

SWEEPS = 8
CLUSTERS = 4


LEAKAGE = 0.05
WEIGHT_X = 1.0
WEIGHT_Y = 0.5
WEIGHT_Z = 0.5
SMALLNESS = 1.0


def padded_2(array, sides, width):
    for axis, dim in sides:
        peers, length = (lax.axis_size(axis), array.shape[dim])
        up = [(i, (i + 1) % peers) for i in range(peers - 1)]
        down = [(j, i) for i, j in up]
        last = lax.slice_in_dim(array, length - width, length, axis=dim)
        leading = lax.slice_in_dim(array, 0, width, axis=dim)
        before = lax.ppermute(last, axis, up)
        after = lax.ppermute(leading, axis, down)
        array = jnp.concatenate([before, array, after], axis=dim)
    return array


def shift_down(values, along):
    length = values.shape[along]
    zero_slab = jnp.zeros_like(lax.slice_in_dim(values, 0, 1, axis=along))
    return jnp.concatenate(
        [zero_slab, lax.slice_in_dim(values, 0, length - 1, axis=along)], axis=along
    )


def shift_up(values, along):
    length = values.shape[along]
    zero_slab = jnp.zeros_like(lax.slice_in_dim(values, 0, 1, axis=along))
    return jnp.concatenate([lax.slice_in_dim(values, 1, length, axis=along), zero_slab], axis=along)


def build_faces(sigma_ext, after_row, col_start, total_rows, total_x):
    span = sigma_ext.shape[2] - 2
    centre = sigma_ext[:, :, 1 : span + 1]
    column = col_start + lax.broadcasted_iota(jnp.int32, (1, 1, span), 2)
    right_x = jnp.where(column + 1 < total_x, WEIGHT_X * 0.5 * (centre + sigma_ext[:, :, 2:]), 0.0)
    left_x = jnp.where(column > 0, WEIGHT_X * 0.5 * (sigma_ext[:, :, :span] + centre), 0.0)
    following = jnp.concatenate([centre[1:], after_row], axis=0)
    row_index = lax.broadcasted_iota(jnp.int32, (centre.shape[0], 1, 1), 0)
    next_y = jnp.where(row_index + 1 < total_rows, WEIGHT_Y * 0.5 * (centre + following), 0.0)
    inside_z = WEIGHT_Z * 0.5 * (centre[:, :-1] + centre[:, 1:])
    zero_slab = jnp.zeros_like(centre[:, :1])
    next_z = jnp.concatenate([inside_z, zero_slab], axis=1)
    prev_z = jnp.concatenate([zero_slab, inside_z], axis=1)
    partial_diag = left_x + right_x + next_y + next_z + prev_z + LEAKAGE * centre
    return (left_x, right_x, next_y, next_z, partial_diag)


def relax_wide(field, source_wide, coefs, inside_wide, offset):
    span = field.shape[3] - 2

    def trimmed(values):
        return lax.slice_in_dim(values, offset, offset + span, axis=values.ndim - 1)

    left_x, right_x, next_y, prev_y, next_z, prev_z, diagonal = [trimmed(entry) for entry in coefs]
    centre = field[..., 1:-1]
    neighbours = left_x * field[..., :-2] + right_x * field[..., 2:]
    neighbours = neighbours + prev_y * shift_down(centre, 1) + next_y * shift_up(centre, 1)
    neighbours = neighbours + prev_z * shift_down(centre, 2) + next_z * shift_up(centre, 2)
    updated = (trimmed(source_wide) + neighbours) / diagonal
    return jnp.where(trimmed(inside_wide), updated, 0.0)


def term_rows(padded, row_span, tile_pos, total_rows, total_x):
    field_rows = padded[0]
    adjoint_rows = padded[1]
    tile_width = field_rows.shape[3] - 2
    centre_f = field_rows[:, 1:-1, :, 1:-1]
    centre_a = adjoint_rows[:, 1:-1, :, 1:-1]
    column = tile_pos * tile_width + lax.broadcasted_iota(jnp.int32, (1, 1, 1, tile_width), 3)
    row_index = lax.broadcasted_iota(jnp.int32, (1, row_span, 1, 1), 1)
    right_x = jnp.where(
        column + 1 < total_x,
        (field_rows[:, 1:-1, :, 2:] - centre_f) * (adjoint_rows[:, 1:-1, :, 2:] - centre_a),
        0.0,
    )
    left_x = jnp.where(
        column > 0,
        (centre_f - field_rows[:, 1:-1, :, :-2]) * (centre_a - adjoint_rows[:, 1:-1, :, :-2]),
        0.0,
    )
    next_y = jnp.where(
        row_index + 1 < total_rows,
        (field_rows[:, 2:, :, 1:-1] - centre_f) * (adjoint_rows[:, 2:, :, 1:-1] - centre_a),
        0.0,
    )
    prev_y = jnp.where(
        row_index > 0,
        (centre_f - field_rows[:, :-2, :, 1:-1]) * (centre_a - adjoint_rows[:, :-2, :, 1:-1]),
        0.0,
    )
    product = (centre_f[:, :, 1:] - centre_f[:, :, :-1]) * (
        centre_a[:, :, 1:] - centre_a[:, :, :-1]
    )
    zero_slab = jnp.zeros_like(product[:, :, :1])
    z_pair = jnp.concatenate([zero_slab, product], axis=2) + jnp.concatenate(
        [product, zero_slab], axis=2
    )
    paired = WEIGHT_X * (left_x + right_x) + WEIGHT_Y * (prev_y + next_y) + WEIGHT_Z * z_pair
    inner_term = 0.5 * paired + LEAKAGE * centre_f * centre_a
    return jnp.sum(inner_term, axis=0)


def on_device(
    log_conductivity,
    cluster_labels,
    cluster_means,
    cluster_vars,
    source_cells,
    receiver_cells,
    observed,
    warm_potential,
    warm_adjoint,
):
    tile_pos = lax.axis_index("tile")
    tile_count = lax.axis_size("tile")
    src_count = lax.axis_size("src")
    row_count, depth_cells, tile_width = log_conductivity.shape
    total_rows = row_count * src_count
    total_x = tile_width * tile_count
    sweep_count = SWEEPS
    rim_cols = sweep_count + 2
    extra = rim_cols - 1
    col_start = tile_pos * tile_width - extra
    whole_tile = lax.all_gather(log_conductivity, "src", axis=0, tiled=True)
    sigma_tile = jnp.exp(whole_tile)
    sigma_ext = padded_2(sigma_tile, (("tile", 2),), rim_cols)
    after_zero = jnp.zeros_like(sigma_ext[:1, :, 1:-1])
    left_x, right_x, next_y, next_z, partial_diag = build_faces(
        sigma_ext, after_zero, col_start, total_rows, total_x
    )
    prev_y = shift_down(next_y, 0)
    prev_z = shift_down(next_z, 1)
    diagonal = partial_diag + prev_y
    coefs = (left_x, right_x, next_y, prev_y, next_z, prev_z, diagonal)
    wide = tile_width + 2 * extra
    grid_shape = (total_rows, depth_cells, wide)
    global_col = col_start + lax.broadcasted_iota(jnp.int32, grid_shape, 2)
    inside_grid = (global_col >= 0) & (global_col < total_x)
    cell_index = (
        lax.broadcasted_iota(jnp.int32, grid_shape, 0) * depth_cells
        + lax.broadcasted_iota(jnp.int32, grid_shape, 1)
    ) * total_x + global_col
    cell_index = jnp.where(inside_grid, cell_index, -1)
    positive = source_cells[:, 0][:, None, None, None]
    negative = source_cells[:, 1][:, None, None, None]
    source_term = (cell_index[None] == positive).astype(jnp.float32) - (
        cell_index[None] == negative
    ).astype(jnp.float32)
    inside_wide = inside_grid[None]

    def locate_cells(cells, first_col, span):
        column = cells % total_x - first_col
        inside = (column >= 0) & (column < span)
        return (cells // total_x * span + jnp.clip(column, 0, span - 1), inside)

    def solve(start, right_side):
        current = padded_2(start, (("tile", 3),), sweep_count + 1)
        for sweep_index in range(sweep_count):
            current = relax_wide(current, right_side, coefs, inside_wide, sweep_index + 1)
        return (current[..., 1:-1], current)

    field, field_keep = solve(warm_potential, source_term)
    spot_first, inside_first = locate_cells(receiver_cells[:, 0], tile_pos * tile_width, tile_width)
    spot_second, inside_second = locate_cells(
        receiver_cells[:, 1], tile_pos * tile_width, tile_width
    )
    flat_field = field.reshape(field.shape[0], -1)
    picked_first = jnp.where(inside_first, flat_field[:, spot_first], 0.0)
    picked_second = jnp.where(inside_second, flat_field[:, spot_second], 0.0)
    picked_first, picked_second = lax.psum((picked_first, picked_second), "tile")
    misfit = picked_first - picked_second - observed
    wide_first, in_first = locate_cells(receiver_cells[:, 0], col_start, wide)
    wide_second, in_second = locate_cells(receiver_cells[:, 1], col_start, wide)
    adjoint_source = (
        jnp.zeros((field.shape[0], total_rows * depth_cells * wide), jnp.float32)
        .at[:, wide_first]
        .add(jnp.where(in_first, misfit, 0.0))
    )
    adjoint_source = (
        adjoint_source.at[:, wide_second]
        .add(jnp.where(in_second, -misfit, 0.0))
        .reshape((field.shape[0],) + grid_shape)
    )
    adjoint, adjoint_keep = solve(warm_adjoint, adjoint_source)
    stacked = jnp.stack([field_keep, adjoint_keep])
    padded = jnp.pad(stacked, ((0, 0), (0, 0), (1, 1), (0, 0), (0, 0)))
    summed = lax.psum_scatter(
        term_rows(padded, total_rows, tile_pos, total_rows, total_x),
        "src",
        scatter_dimension=0,
        tiled=True,
    )
    own_sigma = jnp.exp(log_conductivity)
    mean_cell = jnp.zeros(log_conductivity.shape, jnp.float32)
    var_cell = jnp.zeros(log_conductivity.shape, jnp.float32)
    for cluster in range(CLUSTERS):
        mean_cell = mean_cell + jnp.where(cluster_labels == cluster, cluster_means[cluster], 0.0)
        var_cell = var_cell + jnp.where(cluster_labels == cluster, cluster_vars[cluster], 0.0)
    gradient = -own_sigma * summed + SMALLNESS * (log_conductivity - mean_cell) / var_cell
    return (field, adjoint, misfit, gradient)


def solution(mesh):
    in_specs = (
        P("src", None, "tile"),
        P("src", None, "tile"),
        P(),
        P(),
        P("src", None),
        P(),
        P("src", None),
        P("src", None, None, "tile"),
        P("src", None, None, "tile"),
    )
    out_specs = (
        P("src", None, None, "tile"),
        P("src", None, None, "tile"),
        P("src", None),
        P("src", None, "tile"),
    )
    return jax.shard_map(
        on_device, mesh=mesh, in_specs=in_specs, out_specs=out_specs, check_vma=False
    )
```

profile of v0, /device:TPU:0, one launch (start us, length us, event | category | flops | bytes accessed | tf_op | source)
XLA Modules:
  0.0 140.5 jit_solution(9375785314231729953)
XLA Ops:
  7.2 15.9 %all_gather.3 = f32[32,8,128]{2,1,0:T(8,128)S(1)} all-gather(f32[4,8,128]{2,1,0:T(8,128)} %param.9), channel_id=1, replica_groups=mesh['tile'=4,'src'=8] {'src'}, dimensions={0}, use_global_device_ids=true | all-gather | bytes 147456 | tf_op jit(solution)/shard_map/all_gather | solution.py:137
  23.3 3.4 %collective-permute-start = (f32[32,8,10]{2,1,0:T(8,128)S(1)}, f32[32,8,10]{2,1,0:T(8,128)S(1)}, u32[]{:S(2)}, u32[]{:S(2)}) collective-permute-start(f32[32,8,10]{2,1,0:T(8,128)S(1)} %get-tuple-element.89), channel_id=1, source_target_pairs={{0,8},{8,16},{16,24},{1,9},{9,17},{17,25},{2,10},{10,18},{18,26},{... | collective-permute-start | bytes 30728 | tf_op jit(solution)/shard_map/ppermute | solution.py:24
  26.7 1.3 collective-permute-start.1
  28.1 4.6 %collective-permute-start.2 = (f32[1,32,8,9]{3,2,1,0:T(8,128)S(1)}, f32[1,32,8,9]{3,2,1,0:T(8,128)S(1)}, u32[]{:S(2)}, u32[]{:S(2)}) collective-permute-start(f32[1,32,8,9]{3,2,1,0:T(8,128)S(1)} %get-tuple-element.91), channel_id=1, source_target_pairs={{0,8},{8,16},{16,24},{1,9},{9,17},{17,25},{2,10},{10,18},{18,26},{... | collective-permute-start | bytes 27656 | tf_op jit(solution)/shard_map/ppermute | solution.py:24
  32.7 1.3 collective-permute-start.3
  34.1 4.9 %collective-permute-start.4 = (f32[1,32,8,9]{3,2,1,0:T(8,128)S(1)}, f32[1,32,8,9]{3,2,1,0:T(8,128)S(1)}, u32[]{:S(2)}, u32[]{:S(2)}) collective-permute-start(f32[1,32,8,9]{3,2,1,0:T(8,128)S(1)} %get-tuple-element.87), channel_id=1, source_target_pairs={{0,8},{8,16},{16,24},{1,9},{9,17},{17,25},{2,10},{10,18},{18,26},{... | collective-permute-start | bytes 27656 | tf_op jit(solution)/shard_map/ppermute | solution.py:24
  39.1 0.6 add_compare_fusion.1
  39.7 0.6 fusion.198
  40.3 0.6 compare_select_fusion.3
  40.9 1.4 %convert_subtract_fusion = f32[1,32,8,146]{3,2,1,0:T(8,128)S(1)} fusion(s32[]{:T(128)} %bitcast.1, s32[]{:T(128)} %bitcast, s32[146]{0:T(256)S(1)} %iota_add_fusion, s32[32]{0:T(128)S(1)} %iota_multiply_fusion, pred[146]{0:T(512)(128)(4,1)S(1)} %get-tuple-element.110), kind=kLoop, calls=%fused_computation.247 | loop fusion | flops 336384 | bytes 150370 | tf_op jit(solution)/shard_map/sub | solution.py:159
  42.3 0.5 iota_compare_fusion.2
  43.5 1.3 collective-permute-start.5
  45.0 0.2 fusion.192
  45.4 5.9 %collective-permute-done.5 = f32[1,32,8,9]{3,2,1,0:T(8,128)S(1)} collective-permute-done((f32[1,32,8,9]{3,2,1,0:T(8,128)S(1)}, f32[1,32,8,9]{3,2,1,0:T(8,128)S(1)}, u32[]{:S(2)}, u32[]{:S(2)}) %collective-permute-start.5) | collective-permute-done | bytes 9248 | tf_op jit(solution)/shard_map/ppermute | solution.py:25
  51.4 0.2 fusion.176
  52.1 0.2 fusion.106
  52.5 0.2 add_add_fusion
  52.8 0.7 fusion.120
  53.5 0.2 fusion.190
  53.9 0.7 fusion.121
  54.7 0.2 fusion.188
  55.1 0.7 fusion.122
  55.8 0.2 fusion.186
  56.2 0.7 fusion.123
  56.9 0.2 fusion.184
  57.3 0.7 fusion.124
  58.5 0.7 fusion.125
  59.6 0.7 fusion.126
  60.7 0.7 fusion.127
  61.5 1.7 %gather_fusion.1 = f32[256]{0:T(256)S(1)} fusion(f32[32768]{0:T(1024)S(1)} %slice_bitcast_fusion.34, s32[1024]{0:T(1024)S(1)} %pad_clamp_fusion), kind=kCustom, calls=%fused_computation.1 | custom fusion | bytes 3072 | tf_op jit(solution)/shard_map/gather | solution.py:182
  63.3 1.7 %gather_fusion = f32[256]{0:T(256)S(1)} fusion(f32[32768]{0:T(1024)S(1)} %slice_bitcast_fusion.34, s32[1024]{0:T(1024)S(1)} %pad_clamp_fusion.1), kind=kCustom, calls=%fused_computation | custom fusion | bytes 3072 | tf_op jit(solution)/shard_map/gather | solution.py:181
  65.0 10.6 %all-reduce.71 = (f32[1,256]{1,0:T(1,128)S(1)}, f32[1,256]{1,0:T(1,128)S(1)}) all-reduce(f32[1,256]{1,0:T(1,128)S(1)} %get-tuple-element.13, f32[1,256]{1,0:T(1,128)S(1)} %get-tuple-element.93), channel_id=1, replica_groups=mesh['tile'=4,'src'=8] {'tile'}, use_global_device_ids=true, to_apply=%region_0.1 | all-reduce | flops 512 | bytes 4096 | tf_op jit(solution)/shard_map/psum | solution.py:183
  75.6 0.7 copy-done.25
  76.3 0.6 copy-done.7
  76.8 2.1 %scatter_custom_fusion = f32[37376]{0:T(1024)S(1)} fusion(s32[256]{0:T(256)} %bitcast.498, f32[256]{0:T(256)S(1)} %bitcast.499, f32[]{:T(128)} %constant.54.clone.1), kind=kCustom, calls=%fused_computation.294 | custom fusion | flops 256 | bytes 150016 | tf_op jit(solution)/shard_map/scatter-add | solution.py:190
  78.9 2.0 %scatter_fusion = f32[37376]{0:T(1024)S(1)} fusion(f32[37376]{0:T(1024)S(1)} %scatter_custom_fusion, s32[256]{0:T(256)S(1)} %bitcast.492, f32[256]{0:T(256)S(1)} %bitcast.493), kind=kCustom, calls=%fused_computation.3 | custom fusion | flops 256 | bytes 4096 | tf_op jit(solution)/shard_map/scatter-add | solution.py:194
  81.0 0.3 reshape.297
  81.3 0.6 copy-done.24
  81.9 0.7 fusion.128
  83.1 0.7 copy-done.22
  83.7 0.7 fusion.129
  84.8 0.6 copy-done.20
  85.4 0.7 fusion.130
  86.6 0.7 copy-done.18
  87.2 0.7 fusion.131
  88.4 0.6 copy-done.16
  89.0 0.7 fusion.132
  90.1 0.7 copy-done.14
  90.8 0.7 fusion.133
  91.9 0.6 copy-done.12
  92.5 0.7 fusion.134
  93.3 0.2 fusion.162
  93.5 0.2 fusion.161
  93.7 0.6 copy-done.10
  94.3 0.7 fusion.135
  95.1 0.2 fusion.136
  95.3 0.6 copy-done.26
  95.9 1.1 fusion.145
  97.1 0.7 fusion.196
  97.7 0.7 fusion.197
  98.4 0.8 slice.1195
  99.1 0.8 slice.1138
  99.9 27.5 %reduce-scatter.2.cloned.1.call-done = f32[4,8,128]{2,1,0:T(8,128)} async-done(((f32[32,8,128]{2,1,0:T(8,128)}), f32[4,8,128]{2,1,0:T(8,128)}) %reduce-scatter.2.cloned.1.call-update) | async-done | bytes 16400 | tf_op jit(solution)/shard_map/reduce_scatter | solution.py:200
  127.3 6.3 %divide_add_fusion = f32[4,8,128]{2,1,0:T(8,128)} fusion(f32[4,8,128]{2,1,0:T(8,128)S(1)} %copy-done.2, f32[4,8,128]{2,1,0:T(8,128)} %reduce-scatter.2.cloned.1.call-done, s32[4,8,128]{2,1,0:T(8,128)S(1)} %copy-done.3, f32[]{:T(128)} %bitcast.81, f32[]{:T(128)} %bitcast.80, f32[]{:T(128)} %bitcast.79, f32[]{:T(128)} %bitcast.78, f32[]{:T(128)} %bitcast.77, ...), kind=kLoop, calls=%fused_computation.296 | loop fusion | flops 94208 | bytes 65568 | tf_op jit(solution)/shard_map/add | solution.py:212
  (111 shorter events, 6.8 us)
Async XLA Ops:
  7.2 120.2 %reduce-scatter.2.cloned.1.call-start = ((), (), s32[]{:S(2)}) async-start(), calls=%async_computation.1 | async-start | bytes 147456 | tf_op jit(solution)/shard_map/reduce_scatter | solution.py:200
  23.2 4.8 %copy-start = (f32[1,32,8,128]{3,2,1,0:T(8,128)S(1)}, f32[1,32,8,128]{3,2,1,0:T(8,128)}, u32[]{:S(2)}) copy-start(f32[1,32,8,128]{3,2,1,0:T(8,128)} %param.16) | copy-start | bytes 393220
  23.3 28.5 %collective-permute-start = (f32[32,8,10]{2,1,0:T(8,128)S(1)}, f32[32,8,10]{2,1,0:T(8,128)S(1)}, u32[]{:S(2)}, u32[]{:S(2)}) collective-permute-start(f32[32,8,10]{2,1,0:T(8,128)S(1)} %get-tuple-element.89), channel_id=1, source_target_pairs={{0,8},{8,16},{16,24},{1,9},{9,17},{17,25},{2,10},{10,18},{18,26},{... | collective-permute-start | bytes 30728 | tf_op jit(solution)/shard_map/ppermute | solution.py:24
  26.7 25.1 %collective-permute-start.1 = (f32[32,8,10]{2,1,0:T(8,128)S(1)}, f32[32,8,10]{2,1,0:T(8,128)S(1)}, u32[]{:S(2)}, u32[]{:S(2)}) collective-permute-start(f32[32,8,10]{2,1,0:T(8,128)S(1)} %get-tuple-element.90), channel_id=1, source_target_pairs={{8,0},{16,8},{24,16},{9,1},{17,9},{25,17},{10,2},{18,10},{26,18},{... | collective-permute-start | bytes 30728 | tf_op jit(solution)/shard_map/ppermute | solution.py:25
  28.0 6.0 %copy-start.1 = (f32[1,32,8,128]{3,2,1,0:T(8,128)S(1)}, f32[1,32,8,128]{3,2,1,0:T(8,128)}, u32[]{:S(2)}) copy-start(f32[1,32,8,128]{3,2,1,0:T(8,128)} %param.17) | copy-start | bytes 393220
  28.1 15.4 %collective-permute-start.2 = (f32[1,32,8,9]{3,2,1,0:T(8,128)S(1)}, f32[1,32,8,9]{3,2,1,0:T(8,128)S(1)}, u32[]{:S(2)}, u32[]{:S(2)}) collective-permute-start(f32[1,32,8,9]{3,2,1,0:T(8,128)S(1)} %get-tuple-element.91), channel_id=1, source_target_pairs={{0,8},{8,16},{16,24},{1,9},{9,17},{17,25},{2,10},{10,18},{18,26},{... | collective-permute-start | bytes 27656 | tf_op jit(solution)/shard_map/ppermute | solution.py:24
  32.7 12.1 %collective-permute-start.3 = (f32[1,32,8,9]{3,2,1,0:T(8,128)S(1)}, f32[1,32,8,9]{3,2,1,0:T(8,128)S(1)}, u32[]{:S(2)}, u32[]{:S(2)}) collective-permute-start(f32[1,32,8,9]{3,2,1,0:T(8,128)S(1)} %get-tuple-element.92), channel_id=1, source_target_pairs={{8,0},{16,8},{24,16},{9,1},{17,9},{25,17},{10,2},{18,10},{26,18},{... | collective-permute-start | bytes 27656 | tf_op jit(solution)/shard_map/ppermute | solution.py:25
  34.1 11.3 %collective-permute-start.4 = (f32[1,32,8,9]{3,2,1,0:T(8,128)S(1)}, f32[1,32,8,9]{3,2,1,0:T(8,128)S(1)}, u32[]{:S(2)}, u32[]{:S(2)}) collective-permute-start(f32[1,32,8,9]{3,2,1,0:T(8,128)S(1)} %get-tuple-element.87), channel_id=1, source_target_pairs={{0,8},{8,16},{16,24},{1,9},{9,17},{17,25},{2,10},{10,18},{18,26},{... | collective-permute-start | bytes 27656 | tf_op jit(solution)/shard_map/ppermute | solution.py:24
  39.0 0.7 copy-start.8
  39.1 1.2 copy-start.4
  42.9 9.9 %copy-start.23 = (pred[144]{0:T(512)(128)(4,1)}, pred[144]{0:T(512)(128)(4,1)S(1)}, u32[]{:S(2)}) copy-start(pred[144]{0:T(512)(128)(4,1)S(1)} %slice.845) | copy-start | bytes 436
  43.0 10.9 %copy-start.21 = (pred[142]{0:T(512)(128)(4,1)}, pred[142]{0:T(512)(128)(4,1)S(1)}, u32[]{:S(2)}) copy-start(pred[142]{0:T(512)(128)(4,1)S(1)} %slice.842) | copy-start | bytes 430
  43.1 12.0 %copy-start.19 = (pred[140]{0:T(512)(128)(4,1)}, pred[140]{0:T(512)(128)(4,1)S(1)}, u32[]{:S(2)}) copy-start(pred[140]{0:T(512)(128)(4,1)S(1)} %slice.839) | copy-start | bytes 424
  43.2 13.0 %copy-start.17 = (pred[138]{0:T(512)(128)(4,1)}, pred[138]{0:T(512)(128)(4,1)S(1)}, u32[]{:S(2)}) copy-start(pred[138]{0:T(512)(128)(4,1)S(1)} %slice.836) | copy-start | bytes 418
  43.2 14.1 %copy-start.15 = (pred[136]{0:T(512)(128)(4,1)}, pred[136]{0:T(512)(128)(4,1)S(1)}, u32[]{:S(2)}) copy-start(pred[136]{0:T(512)(128)(4,1)S(1)} %slice.833) | copy-start | bytes 412
  43.3 15.1 %copy-start.13 = (pred[134]{0:T(512)(128)(4,1)}, pred[134]{0:T(512)(128)(4,1)S(1)}, u32[]{:S(2)}) copy-start(pred[134]{0:T(512)(128)(4,1)S(1)} %slice.830) | copy-start | bytes 406
  43.4 16.2 %copy-start.11 = (pred[132]{0:T(512)(128)(4,1)}, pred[132]{0:T(512)(128)(4,1)S(1)}, u32[]{:S(2)}) copy-start(pred[132]{0:T(512)(128)(4,1)S(1)} %slice.827) | copy-start | bytes 400
  43.5 17.2 %copy-start.9 = (pred[130]{0:T(512)(128)(4,1)}, pred[130]{0:T(512)(128)(4,1)S(1)}, u32[]{:S(2)}) copy-start(pred[130]{0:T(512)(128)(4,1)S(1)} %slice.818) | copy-start | bytes 394
  43.5 7.7 %collective-permute-start.5 = (f32[1,32,8,9]{3,2,1,0:T(8,128)S(1)}, f32[1,32,8,9]{3,2,1,0:T(8,128)S(1)}, u32[]{:S(2)}, u32[]{:S(2)}) collective-permute-start(f32[1,32,8,9]{3,2,1,0:T(8,128)S(1)} %get-tuple-element.88), channel_id=1, source_target_pairs={{8,0},{16,8},{24,16},{9,1},{17,9},{25,17},{10,2},{18,10},{26,18},{... | collective-permute-start | bytes 27656 | tf_op jit(solution)/shard_map/ppermute | solution.py:25
  75.6 0.7 copy-start.25
  76.3 0.6 copy-start.7
  81.3 0.7 copy-start.24
  83.0 0.7 copy-start.22
  84.8 0.6 copy-start.20
  86.6 0.7 copy-start.18
  88.4 0.6 copy-start.16
  90.1 0.7 copy-start.14
  91.9 0.6 copy-start.12
  93.7 0.6 copy-start.10
  95.3 0.6 copy-start.26
  95.3 0.6 copy-start.27
  95.3 0.6 copy-start.28
  95.9 1.1 copy-start.5
  95.9 1.8 %copy-start.6 = (f32[4]{0:T(128)S(1)}, f32[4]{0:T(128)}, u32[]{:S(2)}) copy-start(f32[4]{0:T(128)} %param.12) | copy-start | bytes 52
  99.1 28.2 %copy-start.3 = (s32[4,8,128]{2,1,0:T(8,128)S(1)}, s32[4,8,128]{2,1,0:T(8,128)}, u32[]{:S(2)}) copy-start(s32[4,8,128]{2,1,0:T(8,128)} %param.10) | copy-start | bytes 49156
  99.9 27.5 %copy-start.2 = (f32[4,8,128]{2,1,0:T(8,128)S(1)}, f32[4,8,128]{2,1,0:T(8,128)}, u32[]{:S(2)}) copy-start(f32[4,8,128]{2,1,0:T(8,128)} %param.9) | copy-start | bytes 49156
Sparse Core Ops, SparseCore 0:
  97.2 30.1 reduce-scatter.1
where the time goes:
time: 141 us
  waiting for transfers between devices  33.4 us (24%)
  other arithmetic  27.5 us (20%)
  blocking collectives  26.5 us (19%)
  local copies, waits for them, and re-layouts  21.6 us (15%)
  starting transfers between devices  16.8 us (12%)
  between operations  14.8 us (10%)
    reduce_scatter x1, waiting for transfers between devices, on_device(): lax.psum_scatter(term_rows(padded, total_rows, tile_pos, total_rows, tota...  27.5 us
    all_gather x1, blocking collectives, on_device(): whole_tile = lax.all_gather(log_conductivity, 'src', axis=0, tiled=True)  15.9 us
    ppermute x3, starting transfers between devices, padded_2(): before = lax.ppermute(last, axis, up)  12.9 us
    select_n x16, other arithmetic, relax_wide(): return jnp.where(trimmed(inside_wide), updated, 0.0)  11.4 us
    psum x1, blocking collectives, on_device(): lax.psum((picked_first, picked_second), 'tile')  10.6 us
    unnamed x58, local copies, waits for them, and re-layouts  7.02 us
    add x1, other arithmetic, on_device(): -own_sigma * summed + SMALLNESS * (log_conductivity - mean_cell) / var_cell  6.34 us
    slice x33, local copies, waits for them, and re-layouts, shift_down(): lax.slice_in_dim(values, 0, length - 1, axis=along)  6.29 us
  transfers between devices with their start and end apart: 7, of which 2 were waited for; matrix products, arithmetic and copies ran while one was open for 6% of the time, Pallas kernels for 0%

commit v1 on v0

v1 whole, which is shorter than its diff:
```python
import functools

import jax
import jax.numpy as jnp
from jax import lax
from jax.experimental import pallas as pl
from jax.experimental.pallas import tpu as pltpu
from jax.sharding import PartitionSpec as P

SWEEPS = 8
CLUSTERS = 4
HALO = SWEEPS + 1

LEAKAGE = 0.05
WEIGHT_X = 1.0
WEIGHT_Y = 0.5
WEIGHT_Z = 0.5
SMALLNESS = 1.0

F32 = jnp.float32
BF16 = jnp.bfloat16
VMEM = pl.BlockSpec(memory_space=pltpu.VMEM)
SMEM = pl.BlockSpec(memory_space=pltpu.SMEM)
PARAMS = pltpu.CompilerParams(vmem_limit_bytes=24 * 1024 * 1024)


def xor_pairs(count, bit):
    return [(i, i ^ bit) for i in range(count)]


def lanes(shape):
    return lax.broadcasted_iota(jnp.int32, shape, len(shape) - 1)


def wide_columns(shape):
    lane = lanes(shape)
    width = shape[-1]
    return jnp.where(lane < width - width // 4, lane, lane - width)


def turn(values, shift):
    return pltpu.roll(values, shift % values.shape[-1], values.ndim - 1)


def pack_kernel(order, info, gathered, own_v, own_a, other_v, other_a, payload, model):
    peers, rows_own = gathered.shape[:2]
    rows = model.shape[0]
    half = rows // 2
    me, right = info[0], info[1]
    for i in range(peers):
        j = sum(((i >> n) & 1) << bit for n, bit in enumerate(order))
        model[pl.ds((me ^ j) * rows_own, rows_own)] = gathered[i]
    lane = lanes((8, 128))

    def fill(start):
        sources = (own_v, own_a, model, other_v, other_a, model)
        for row in range(half):
            out = jnp.zeros((8, 128), F32)
            for group in range(2):
                for k, ref in enumerate(sources):
                    place = 64 * group + HALO * k
                    piece = turn(ref[row + half * group], place - start)
                    out = jnp.where((lane >= place) & (lane < place + HALO), piece, out)
            payload[row] = out

    @pl.when(right == 1)
    def _():
        fill(128 - HALO)

    @pl.when(right == 0)
    def _():
        fill(0)


def side_buffers(right, mine, theirs, row):
    near = mine[row]
    far = turn(theirs[row], -3 * HALO)
    on_right = jnp.full((8, 128), right, jnp.int32) == 1
    return jnp.where(on_right, near, far), jnp.where(on_right, far, near)


def halo_row(after, before, base, slot):
    lane = lanes((8, 128))
    first = turn(after, -(base + HALO * slot))
    last = turn(before, 128 - HALO - base - HALO * slot)
    return jnp.where(lane < HALO, first, jnp.where(lane >= 128 - HALO, last, 0.0))


def sweep(source, target, right_side, fx, fy, fz, inverse):
    rows = source.shape[0]
    for y in range(rows):
        v = source[y]
        face_x = fx[y]
        face_z = fz[y]
        total = right_side[y] + face_x * turn(v, -1) + turn(face_x * v, 1)
        total = total + (face_z * pltpu.roll(v, 7, 0) + pltpu.roll(face_z * v, 1, 0))
        if y + 1 < rows:
            total = total + fy[y] * source[y + 1]
        if y > 0:
            total = total + fy[y - 1] * source[y - 1]
        target[y] = total * inverse[y]


def relax(first, second, right_side, fx, fy, fz, inverse):
    def two(_, carry):
        sweep(first, second, right_side, fx, fy, fz, inverse)
        sweep(second, first, right_side, fx, fy, fz, inverse)
        return carry

    lax.fori_loop(0, SWEEPS // 2, two, 0)


def three_parts(values):
    high = values.astype(BF16)
    rest = values - high.astype(F32)
    middle = rest.astype(BF16)
    low = (rest - middle.astype(F32)).astype(BF16)
    return high, middle, low


def field_kernel(
    total_x, info, cells, model, mine, theirs, warm, spots,
    field_out, picked, wide, fx, fy, fz, inverse, other, right_side,
):
    rows, depth, width = model.shape
    span = 2 * width
    half = rows // 2
    right, first_col = info[1], info[2]
    col = first_col + wide_columns((depth, span))
    depth_at = lax.broadcasted_iota(jnp.int32, (depth, span), 0)
    closed_x = (col == total_x - 1) | (col == -1)
    wide_sigma = other
    for row in range(half):
        after, before = side_buffers(right, mine, theirs, row)
        for group in range(2):
            y = row + half * group
            wide[y, :, :width] = warm[y]
            wide[y, :, width:] = halo_row(after, before, 64 * group, 0)
            wide_sigma[y, :, :width] = jnp.exp(model[y])
            wide_sigma[y, :, width:] = jnp.exp(halo_row(after, before, 64 * group, 2))
    previous = jnp.zeros((depth, span), F32)
    for y in range(rows):
        s = wide_sigma[y]
        face_x = jnp.where(closed_x, 0.0, WEIGHT_X * 0.5 * (s + turn(s, -1)))
        face_z = jnp.where(depth_at == depth - 1, 0.0, WEIGHT_Z * 0.5 * (s + pltpu.roll(s, depth - 1, 0)))
        if y + 1 < rows:
            face_y = WEIGHT_Y * 0.5 * (s + wide_sigma[y + 1])
        else:
            face_y = jnp.zeros((depth, span), F32)
        diagonal = face_x + turn(face_x, 1) + face_z + pltpu.roll(face_z, 1, 0) + LEAKAGE * s + face_y + previous
        fx[y] = face_x
        fy[y] = face_y
        fz[y] = face_z
        inverse[y] = 1.0 / diagonal
        previous = face_y
        right_side[y] = jnp.zeros((depth, span), F32)
    for k, sign in ((0, 1.0), (1, -1.0)):
        cell = cells[0, k]
        line = cell // total_x
        y = line // depth
        hit = (col == cell - line * total_x) & (depth_at == line - y * depth)
        right_side[y] = right_side[y] + jnp.where(hit, sign, 0.0)
    relax(wide, other, right_side, fx, fy, fz, inverse)
    field = wide[:, :, :width]
    field_out[0] = field
    count = spots.shape[1]
    x_row = spots[0:1, :] - first_col
    line_row = spots[1:2, :]
    hit_x = jnp.where(lax.broadcasted_iota(jnp.int32, (width, count), 0) == x_row, 1.0, 0.0).astype(BF16)
    flat = field.reshape(rows * depth, width)
    lines = sum(jnp.dot(part, hit_x, preferred_element_type=F32) for part in three_parts(flat))
    hit_line = lax.broadcasted_iota(jnp.int32, (rows * depth, count), 0) == line_row
    got = jnp.sum(jnp.where(hit_line, lines, 0.0), axis=0, keepdims=True)
    picked[...] = got[:, : count // 2] - got[:, count // 2 :]


def adjoint_kernel(
    total_x, places, info, picked, observed, spots, mine, theirs, warm, wide_v, fx, fy, fz, inverse,
    adjoint_out, misfit_out, terms, wide, other, right_side,
):
    rows, depth, span = wide_v.shape
    width = span // 2
    half = rows // 2
    me, right, first_col = info[0], info[1], info[2]
    count = spots.shape[1]
    col = first_col + wide_columns((depth, span))
    misfit = picked[...] - observed[...]
    misfit_out[...] = misfit
    weights = jnp.concatenate([misfit, -misfit], axis=1)
    hit_line = lax.broadcasted_iota(jnp.int32, (rows * depth, count), 0) == spots[1:2, :]
    at = lax.broadcasted_iota(jnp.int32, (span, count), 0)
    at = first_col + jnp.where(at < span - span // 4, at, at - span)
    hit_x = jnp.where(at == spots[0:1, :], 1.0, 0.0).astype(BF16)
    flat = jnp.zeros((rows * depth, span), F32)
    for part in three_parts(weights):
        left = jnp.where(hit_line, part.astype(F32), 0.0).astype(BF16)
        flat = flat + lax.dot_general(left, hit_x, (((1,), (1,)), ((), ())), preferred_element_type=F32)
    right_side[...] = flat.reshape(rows, depth, span)
    for row in range(half):
        after, before = side_buffers(right, mine, theirs, row)
        for group in range(2):
            y = row + half * group
            wide[y, :, :width] = warm[y]
            wide[y, :, width:] = halo_row(after, before, 64 * group, 1)
    relax(wide, other, right_side, fx, fy, fz, inverse)
    adjoint_out[0] = wide[:, :, :width]
    closed_x = (col == total_x - 1) | (col == -1)
    depth_at = lax.broadcasted_iota(jnp.int32, (depth, width), 0)
    peers, rows_own = terms.shape[:2]
    py_prev = jnp.zeros((depth, width), F32)
    for y in range(rows):
        f, a = wide_v[y], wide[y]
        px = jnp.where(closed_x, 0.0, (turn(f, -1) - f) * (turn(a, -1) - a))
        px = (px + turn(px, 1))[:, :width]
        f, a = f[:, :width], a[:, :width]
        pz = (pltpu.roll(f, depth - 1, 0) - f) * (pltpu.roll(a, depth - 1, 0) - a)
        pz = jnp.where(depth_at == depth - 1, 0.0, pz)
        pz = pz + pltpu.roll(pz, 1, 0)
        if y + 1 < rows:
            py = (wide_v[y + 1, :, :width] - f) * (wide[y + 1, :, :width] - a)
        else:
            py = jnp.zeros((depth, width), F32)
        paired = WEIGHT_X * px + WEIGHT_Y * (py_prev + py) + WEIGHT_Z * pz
        py_prev = py
        j = me ^ (y // rows_own)
        place = sum(((j >> bit) & 1) << n for n, bit in enumerate(reversed(places)))
        terms[place, y % rows_own] = 0.5 * paired + LEAKAGE * f * a


def gradient_kernel(means, variances, labels, model, kept, came, gradient):
    m = model[...]
    label = labels[...]
    mean_cell = jnp.zeros(m.shape, F32)
    var_cell = jnp.zeros(m.shape, F32)
    for cluster in range(CLUSTERS):
        mean_cell = jnp.where(label == cluster, means[cluster], mean_cell)
        var_cell = jnp.where(label == cluster, variances[cluster], var_cell)
    gradient[...] = -jnp.exp(m) * (kept[...] + came[...]) + SMALLNESS * (m - mean_cell) / var_cell


def on_device(
    log_conductivity,
    cluster_labels,
    cluster_means,
    cluster_vars,
    source_cells,
    receiver_cells,
    observed,
    warm_potential,
    warm_adjoint,
):
    tile, src = lax.axis_index("tile"), lax.axis_index("src")
    tiles, peers = lax.axis_size("tile"), lax.axis_size("src")
    rows_own, depth, width = log_conductivity.shape
    rows = rows_own * peers
    total_x = width * tiles
    receivers = receiver_cells.shape[0]
    bits = [1 << n for n in range(peers.bit_length() - 1)]
    levels = list(range(len(bits)))
    right = 1 - (tile + src) % 2
    info = jnp.stack([src, right, tile * width]).astype(jnp.int32)
    spots = receiver_cells.T.reshape(1, 2 * receivers)
    spots = jnp.concatenate([spots % total_x, spots // total_x], axis=0)
    spots = jnp.pad(spots, ((0, 6), (0, 0)), constant_values=-1)
    start_v, start_a = warm_potential[0], warm_adjoint[0]

    gathered = log_conductivity[None]
    order = levels[1:] + [0]
    for level in order:
        came = lax.ppermute(gathered, "src", xor_pairs(peers, bits[level]))
        gathered = jnp.concatenate([gathered, came], axis=0)
    other_v = lax.ppermute(start_v, "src", xor_pairs(peers, 1))
    other_a = lax.ppermute(start_a, "src", xor_pairs(peers, 1))
    block = jax.ShapeDtypeStruct((rows // 2, depth, width), F32)
    tile_field = jax.ShapeDtypeStruct((rows, depth, width), F32)
    wide_field = jax.ShapeDtypeStruct((rows, depth, 2 * width), F32)
    payload, model = pl.pallas_call(
        functools.partial(pack_kernel, order),
        out_shape=(block, tile_field),
        in_specs=[SMEM] + [VMEM] * 5,
        out_specs=(VMEM, VMEM),
        compiler_params=PARAMS,
    )(info, gathered, start_v, start_a, other_v, other_a)
    pairs = []
    for t in range(tiles):
        for s in range(peers):
            t_to = (t + 1) % tiles if (t + s) % 2 == 0 else (t - 1) % tiles
            pairs.append((t * peers + s, t_to * peers + s))
    mine = lax.ppermute(payload, ("tile", "src"), pairs)
    theirs = lax.ppermute(mine, "src", xor_pairs(peers, 1))

    field, picked, wide_v, fx, fy, fz, inverse = pl.pallas_call(
        functools.partial(field_kernel, total_x),
        out_shape=(
            jax.ShapeDtypeStruct(warm_potential.shape, F32),
            jax.ShapeDtypeStruct((1, receivers), F32),
        )
        + (wide_field,) * 5,
        in_specs=[SMEM, SMEM] + [VMEM] * 5,
        out_specs=(VMEM,) * 7,
        scratch_shapes=[pltpu.VMEM(wide_field.shape, F32)] * 2,
        compiler_params=PARAMS,
    )(info, source_cells, model, mine, theirs, start_v, spots)

    step = 1
    while step < tiles:
        picked = picked + lax.ppermute(picked, "tile", xor_pairs(tiles, step))
        step *= 2

    places = [0] + levels[:0:-1]
    adjoint, misfit, terms = pl.pallas_call(
        functools.partial(adjoint_kernel, total_x, places),
        out_shape=(
            jax.ShapeDtypeStruct(warm_adjoint.shape, F32),
            jax.ShapeDtypeStruct(observed.shape, F32),
            jax.ShapeDtypeStruct((peers, rows_own, depth, width), F32),
        ),
        in_specs=[SMEM] + [VMEM] * 11,
        out_specs=(VMEM,) * 3,
        scratch_shapes=[pltpu.VMEM(wide_field.shape, F32)] * 3,
        compiler_params=PARAMS,
    )(info, picked, observed, spots, mine, theirs, start_a, wide_v, fx, fy, fz, inverse)

    for level in places[:-1]:
        keep = terms.shape[0] // 2
        terms = terms[:keep] + lax.ppermute(terms[keep:], "src", xor_pairs(peers, bits[level]))
    came = lax.ppermute(terms[1], "src", xor_pairs(peers, bits[places[-1]]))
    gradient = pl.pallas_call(
        gradient_kernel,
        out_shape=jax.ShapeDtypeStruct(log_conductivity.shape, F32),
        in_specs=[SMEM, SMEM] + [VMEM] * 4,
        out_specs=VMEM,
        compiler_params=PARAMS,
    )(cluster_means, cluster_vars, cluster_labels, log_conductivity, terms[0], came)
    return (field, adjoint, misfit, gradient)


def solution(mesh):
    in_specs = (
        P("src", None, "tile"),
        P("src", None, "tile"),
        P(),
        P(),
        P("src", None),
        P(),
        P("src", None),
        P("src", None, None, "tile"),
        P("src", None, None, "tile"),
    )
    out_specs = (
        P("src", None, None, "tile"),
        P("src", None, None, "tile"),
        P("src", None),
        P("src", None, "tile"),
    )
    return jax.shard_map(
        on_device, mesh=mesh, in_specs=in_specs, out_specs=out_specs, check_vma=False
    )
```

time: 141 us -> 47.1 us (0.33)
  other arithmetic: 27.5 us -> 0.87 us
  blocking collectives: 26.5 us -> 0 us
  local copies, waits for them, and re-layouts: 21.6 us -> 0.91 us
  waiting for transfers between devices: 33.4 us -> 16.6 us
  between operations: 14.8 us -> 0.8 us
  Pallas kernels: 0 us -> 10.1 us
    reduce_scatter x1 -> x0, waiting for transfers between devices: 27.5 us -> none  [on_device(): lax.psum_scatter(term_rows(padded, total_rows, tile_pos, total_rows, tota...]
    all_gather x1 -> x0, blocking collectives: 15.9 us -> none  [on_device(): whole_tile = lax.all_gather(log_conductivity, 'src', axis=0, tiled=True)]
    select_n x23 -> x2, other arithmetic: 12.2 us -> 0.02 us  [on_device(): spots = jnp.concatenate([spots % total_x, spots // total_x], axis=0)]
    ppermute x6 -> x12, waiting for transfers between devices: 5.87 us -> 16.6 us  [the longest x3 4.25 us: on_device(): came = lax.ppermute(gathered, 'src', xor_pairs(peers, bits[level]))]
    slice x50 -> x2, local copies, waits for them, and re-layouts: 10.7 us -> 0.01 us  [on_device(): terms[keep:]]
    psum x1 -> x0, blocking collectives: 10.6 us -> none  [on_device(): lax.psum((picked_first, picked_second), 'tile')]
    pallas_call x0 -> x4, Pallas kernels: none -> 10.1 us  [the longest x1 4.42 us: on_device(): pl.pallas_call(functools.partial(adjoint_kernel, total_x, places), out_sh...]
    add x3 -> x4, other arithmetic: 6.59 us -> 0.02 us  [the longest x2 0.02 us: on_device(): terms[:keep]]
  transfers between devices with their start and end apart: 7 -> 12, of which waited for: 2 -> 10; matrix products, arithmetic and copies ran while one was open for 6% -> 2% of each run, Pallas kernels for 0% -> 0%
where the time goes in v1:
time: 47.1 us; the launch traced here: 46.8 us
  starting transfers between devices  17.5 us (37%)
  waiting for transfers between devices  16.6 us (35%)
  Pallas kernels  10.1 us (21%)
  local copies, waits for them, and re-layouts  0.91 us (2%)
  other arithmetic  0.87 us (2%)
  between operations  0.8 us (2%)
    ppermute x3, starting transfers between devices, on_device(): came = lax.ppermute(gathered, 'src', xor_pairs(peers, bits[level]))  6.19 us
    pallas_call x1, Pallas kernels, on_device(): pl.pallas_call(functools.partial(adjoint_kernel, total_x, places), out_sh...  4.42 us
    ppermute x3, waiting for transfers between devices, on_device(): came = lax.ppermute(gathered, 'src', xor_pairs(peers, bits[level]))  4.25 us
    pallas_call x1, Pallas kernels, on_device(): pl.pallas_call(functools.partial(field_kernel, total_x), out_shape=(jax.S...  3.68 us
    ppermute x2, starting transfers between devices, on_device(): picked = picked + lax.ppermute(picked, 'tile', xor_pairs(tiles, step))  3.65 us
    ppermute x2, waiting for transfers between devices, on_device(): picked = picked + lax.ppermute(picked, 'tile', xor_pairs(tiles, step))  3.49 us
    ppermute x2, starting transfers between devices, on_device(): lax.ppermute(terms[keep:], 'src', xor_pairs(peers, bits[level]))  3.34 us
    ppermute x2, waiting for transfers between devices, on_device(): lax.ppermute(terms[keep:], 'src', xor_pairs(peers, bits[level]))  3.14 us
  transfers between devices with their start and end apart: 12, of which 10 were waited for; matrix products, arithmetic and copies ran while one was open for 2% of the time, Pallas kernels for 0%

profile of v1, /device:TPU:0, one launch (start us, length us, event | category | flops | bytes accessed | tf_op | source)
XLA Modules:
  0.0 46.8 jit_solution(8795717998687196158)
XLA Ops:
  0.6 3.1 %collective-permute-start = (f32[1,4,8,128]{3,2,1,0:T(8,128)}, f32[1,4,8,128]{3,2,1,0:T(8,128)S(1)}, u32[]{:S(2)}, u32[]{:S(2)}) collective-permute-start(f32[1,4,8,128]{3,2,1,0:T(8,128)} %bitcast.20), channel_id=1, source_target_pairs={{0,2},{1,3},{2,0},{3,1},{4,6},{5,7},{6,4},{7,5},{8,10},{9,11},{10,... | collective-permute-start | bytes 49160 | tf_op jit(solution)/shard_map/ppermute | solution.py:270
  3.7 0.0 copy-start.8
  3.7 0.0 collective-permute-start.3
  3.7 0.5 %collective-permute-start.4 = (f32[32,8,128]{2,1,0:T(8,128)}, f32[32,8,128]{2,1,0:T(8,128)S(1)}, u32[]{:S(2)}, u32[]{:S(2)}) collective-permute-start(f32[32,8,128]{2,1,0:T(8,128)} %bitcast.17), channel_id=1, source_target_pairs={{0,1},{1,0},{2,3},{3,2},{4,5},{5,4},{6,7},{7,6},{8,9},{9,8},{10,11... | collective-permute-start | bytes 393224 | tf_op jit(solution)/shard_map/ppermute | solution.py:273
  4.2 0.2 copy-done.8
  4.4 1.2 %collective-permute-done = f32[1,4,8,128]{3,2,1,0:T(8,128)S(1)} collective-permute-done((f32[1,4,8,128]{3,2,1,0:T(8,128)}, f32[1,4,8,128]{3,2,1,0:T(8,128)S(1)}, u32[]{:S(2)}, u32[]{:S(2)}) %collective-permute-start) | collective-permute-done | bytes 16416 | tf_op jit(solution)/shard_map/ppermute | solution.py:270
  5.7 0.7 %pad_maximum_fusion.2 = f32[2,4,8,128]{3,2,1,0:T(8,128)S(1)} fusion(f32[1,4,8,128]{3,2,1,0:T(8,128)S(1)} %collective-permute-done, f32[1,4,8,128]{3,2,1,0:T(8,128)} %bitcast.21), kind=kLoop, calls=%fused_computation.4 | loop fusion | flops 8192 | bytes 65536 | tf_op jit(solution)/shard_map/concatenate | solution.py:271
  6.4 3.0 %collective-permute-start.1 = (f32[2,4,8,128]{3,2,1,0:T(8,128)S(1)}, f32[2,4,8,128]{3,2,1,0:T(8,128)S(1)}, u32[]{:S(2)}, u32[]{:S(2)}) collective-permute-start(f32[2,4,8,128]{3,2,1,0:T(8,128)S(1)} %pad_maximum_fusion.2), channel_id=1, source_target_pairs={{0,4},{1,5},{2,6},{3,7},{4,0},{5,1},{6,2},{7,3},{8,12},{9,13},{10,... | collective-permute-start | bytes 98312 | tf_op jit(solution)/shard_map/ppermute | solution.py:270
  9.4 0.0 copy-start.2
  9.4 1.9 %collective-permute-done.1 = f32[2,4,8,128]{3,2,1,0:T(8,128)S(1)} collective-permute-done((f32[2,4,8,128]{3,2,1,0:T(8,128)S(1)}, f32[2,4,8,128]{3,2,1,0:T(8,128)S(1)}, u32[]{:S(2)}, u32[]{:S(2)}) %collective-permute-start.1) | collective-permute-done | bytes 32800 | tf_op jit(solution)/shard_map/ppermute | solution.py:270
  11.3 0.0 copy-done.2
  11.3 0.1 collective-permute-start.2
  11.4 0.1 pad_add_fusion.1.info
  11.5 0.0 copy-start
  11.5 0.0 copy-start.1
  11.5 1.2 %collective-permute-done.2 = f32[4,4,8,128]{3,2,1,0:T(8,128)S(1)} collective-permute-done((f32[4,4,8,128]{3,2,1,0:T(8,128)S(1)}, f32[4,4,8,128]{3,2,1,0:T(8,128)S(1)}, u32[]{:S(2)}, u32[]{:S(2)}) %collective-permute-start.2) | collective-permute-done | bytes 65568 | tf_op jit(solution)/shard_map/ppermute | solution.py:270
  12.6 0.0 collective-permute-done.3.other_v
  12.6 0.0 collective-permute-done.4.other_a
  12.7 0.0 copy-done
  12.7 0.0 copy-done.1
  12.7 0.8 %shard_map.120 = (f32[16,8,128]{2,1,0:T(8,128)S(1)}, f32[32,8,128]{2,1,0:T(8,128)S(1)}) custom-call(s32[3]{0:T(128)S(1)} %pad_add_fusion.1.info, f32[8,4,8,128]{3,2,1,0:T(8,128)S(1)} %pad_maximum_fusion.gathered, f32[32,8,128]{2,1,0:T(8,128)S(1)} %bitcast.15, f32[32,8,128]{2,1,0:T(8,128)S(1)} %bitcast.18, f32[32,8,128]{2,1,0:T(8,128)S(1)} %collective-permute-done.3.other_v, ...), custom_call_target="tpu_custom_call" | custom-call | tf_op jit(solution)/shard_map/pallas_call | solution.py:277
  13.5 1.9 %collective-permute-start.5 = (f32[16,8,128]{2,1,0:T(8,128)S(1)}, f32[16,8,128]{2,1,0:T(8,128)S(1)}, u32[]{:S(2)}, u32[]{:S(2)}) collective-permute-start(f32[16,8,128]{2,1,0:T(8,128)S(1)} %get-tuple-element.17), channel_id=1, source_target_pairs={{0,8},{1,25},{2,10},{3,27},{4,12},{5,29},{6,14},{7,31},{8,0},{9,17... | collective-permute-start | bytes 196616 | tf_op jit(solution)/shard_map/ppermute | solution.py:289
  15.4 2.7 %collective-permute-done.5.mine = f32[16,8,128]{2,1,0:T(8,128)S(1)} collective-permute-done((f32[16,8,128]{2,1,0:T(8,128)S(1)}, f32[16,8,128]{2,1,0:T(8,128)S(1)}, u32[]{:S(2)}, u32[]{:S(2)}) %collective-permute-start.5) | collective-permute-done | bytes 65568 | tf_op jit(solution)/shard_map/ppermute | solution.py:289
  18.1 0.0 collective-permute-start.6
  18.1 0.0 copy-start.5
  18.1 1.2 %collective-permute-done.6.theirs = f32[16,8,128]{2,1,0:T(8,128)S(1)} collective-permute-done((f32[16,8,128]{2,1,0:T(8,128)S(1)}, f32[16,8,128]{2,1,0:T(8,128)S(1)}, u32[]{:S(2)}, u32[]{:S(2)}) %collective-permute-start.6) | collective-permute-done | bytes 65568 | tf_op jit(solution)/shard_map/ppermute | solution.py:290
  19.3 0.0 copy-done.5
  19.3 3.7 %shard_map.121 = (f32[1,32,8,128]{3,2,1,0:T(8,128)}, f32[1,256]{1,0:T(1,128)S(1)}, f32[32,8,256]{2,1,0:T(8,128)S(1)}, f32[32,8,256]{2,1,0:T(8,128)S(1)}, f32[32,...) custom-call(s32[3]{0:T(128)S(1)} %pad_add_fusion.1.info, s32[1,2]{1,0:T(1,128)S(1)} %copy-done.5, ...), custom_call_target="tpu_custom_call" | custom-call | tf_op jit(solution)/shard_map/pallas_call | solution.py:292
  23.0 2.0 %collective-permute-start.7 = (f32[1,256]{1,0:T(1,128)S(1)}, f32[1,256]{1,0:T(1,128)S(1)}, u32[]{:S(2)}, u32[]{:S(2)}) collective-permute-start(f32[1,256]{1,0:T(1,128)S(1)} %get-tuple-element.19), channel_id=1, source_target_pairs={{0,8},{8,0},{16,24},{24,16},{1,9},{9,1},{17,25},{25,17},{2,10},{10... | collective-permute-start | bytes 3080 | tf_op jit(solution)/shard_map/ppermute | solution.py:307
  25.0 1.5 %collective-permute-done.7 = f32[1,256]{1,0:T(1,128)S(1)} collective-permute-done((f32[1,256]{1,0:T(1,128)S(1)}, f32[1,256]{1,0:T(1,128)S(1)}, u32[]{:S(2)}, u32[]{:S(2)}) %collective-permute-start.7) | collective-permute-done | bytes 1056 | tf_op jit(solution)/shard_map/ppermute | solution.py:307
  26.6 1.6 %collective-permute-start.8 = (f32[1,256]{1,0:T(1,128)S(1)}, f32[1,256]{1,0:T(1,128)S(1)}, u32[]{:S(2)}, u32[]{:S(2)}) collective-permute-start(f32[1,256]{1,0:T(1,128)S(1)} %add.47), channel_id=1, source_target_pairs={{0,16},{8,24},{16,0},{24,8},{1,17},{9,25},{17,1},{25,9},{2,18},{10... | collective-permute-start | bytes 3080 | tf_op jit(solution)/shard_map/ppermute | solution.py:307
  28.2 1.9 %collective-permute-done.8 = f32[1,256]{1,0:T(1,128)S(1)} collective-permute-done((f32[1,256]{1,0:T(1,128)S(1)}, f32[1,256]{1,0:T(1,128)S(1)}, u32[]{:S(2)}, u32[]{:S(2)}) %collective-permute-start.8) | collective-permute-done | bytes 1056 | tf_op jit(solution)/shard_map/ppermute | solution.py:307
  30.2 0.0 copy-start.4
  30.2 0.7 %copy-done.4 = f32[1,256]{1,0:T(1,128)S(1)} copy-done((f32[1,256]{1,0:T(1,128)S(1)}, f32[1,256]{1,0:T(1,128)}, u32[]{:S(2)}) %copy-start.4) | copy-done | bytes 1048
  30.8 4.4 %shard_map.122 = (f32[1,32,8,128]{3,2,1,0:T(8,128)}, f32[1,256]{1,0:T(1,128)}, f32[8,4,8,128]{3,2,1,0:T(8,128)S(1)}) custom-call(s32[3]{0:T(128)S(1)} %pad_add_fusion.1.info, f32[1,256]{1,0:T(1,128)S(1)} %add.48.picked, f32[1,256]{1,0:T(1,128)S(1)} %copy-done.4, s32[8,512]{1,0:T(8,128)S(1)} %pad.4.spots, f32[16,8,128]{2,1,0:T(8,128)S(1)} %collective-permute-done.5.mine, ...), custom_call_target="tpu_custom_call" | custom-call | tf_op jit(solution)/shard_map/pallas_call | solution.py:311
  35.3 0.1 collective-permute-start.9
  35.4 1.2 %collective-permute-done.9 = f32[4,4,8,128]{3,2,1,0:T(8,128)S(1)} collective-permute-done((f32[4,4,8,128]{3,2,1,0:T(8,128)S(1)}, f32[4,4,8,128]{3,2,1,0:T(8,128)S(1)}, u32[]{:S(2)}, u32[]{:S(2)}) %collective-permute-start.9) | collective-permute-done | bytes 65568 | tf_op jit(solution)/shard_map/ppermute | solution.py:326
  36.6 3.3 %collective-permute-start.10 = (f32[2,4,8,128]{3,2,1,0:T(8,128)S(1)}, f32[2,4,8,128]{3,2,1,0:T(8,128)S(1)}, u32[]{:S(2)}, u32[]{:S(2)}) collective-permute-start(f32[2,4,8,128]{3,2,1,0:T(8,128)S(1)} %slice.25), channel_id=1, source_target_pairs={{0,4},{1,5},{2,6},{3,7},{4,0},{5,1},{6,2},{7,3},{8,12},{9,13},{10,... | collective-permute-start | bytes 98312 | tf_op jit(solution)/shard_map/ppermute | solution.py:326
  39.9 1.9 %collective-permute-done.10 = f32[2,4,8,128]{3,2,1,0:T(8,128)S(1)} collective-permute-done((f32[2,4,8,128]{3,2,1,0:T(8,128)S(1)}, f32[2,4,8,128]{3,2,1,0:T(8,128)S(1)}, u32[]{:S(2)}, u32[]{:S(2)}) %collective-permute-start.10) | collective-permute-done | bytes 32800 | tf_op jit(solution)/shard_map/ppermute | solution.py:326
  41.8 0.0 copy-start.3
  41.8 0.0 copy-start.6
  41.8 0.0 copy-start.7
  41.8 2.0 %collective-permute-start.11 = (f32[4,8,128]{2,1,0:T(8,128)S(1)}, f32[4,8,128]{2,1,0:T(8,128)S(1)}, u32[]{:S(2)}, u32[]{:S(2)}) collective-permute-start(f32[4,8,128]{2,1,0:T(8,128)S(1)} %get-tuple-element.30), channel_id=1, source_target_pairs={{0,2},{1,3},{2,0},{3,1},{4,6},{5,7},{6,4},{7,5},{8,10},{9,11},{10,... | collective-permute-start | bytes 49160 | tf_op jit(solution)/shard_map/ppermute | solution.py:327
  43.8 1.9 %collective-permute-done.11.came = f32[4,8,128]{2,1,0:T(8,128)S(1)} collective-permute-done((f32[4,8,128]{2,1,0:T(8,128)S(1)}, f32[4,8,128]{2,1,0:T(8,128)S(1)}, u32[]{:S(2)}, u32[]{:S(2)}) %collective-permute-start.11) | collective-permute-done | bytes 16416 | tf_op jit(solution)/shard_map/ppermute | solution.py:327
  45.6 0.0 copy-done.3
  45.6 0.0 copy-done.6
  45.6 0.0 copy-done.7
  45.7 1.2 %shard_map.123 = f32[4,8,128]{2,1,0:T(8,128)} custom-call(f32[4]{0:T(128)S(1)} %copy-done.6, f32[4]{0:T(128)S(1)} %copy-done.7, s32[4,8,128]{2,1,0:T(8,128)S(1)} %copy-done.3, f32[4,8,128]{2,1,0:T(8,128)S(1)} %copy-done.2, f32[4,8,128]{2,1,0:T(8,128)S(1)} %get-tuple-element.31.kept, f32[4,8,128]{2,1,0:T(8,128)S(1)} %collective-permute-done.11.came), custom_call_target="tpu_custom_call" | custom-call | tf_op jit(solution)/shard_map/pallas_call | solution.py:328
  (14 shorter events, 0.1 us)
Async XLA Ops:
  0.6 5.0 %collective-permute-start = (f32[1,4,8,128]{3,2,1,0:T(8,128)}, f32[1,4,8,128]{3,2,1,0:T(8,128)S(1)}, u32[]{:S(2)}, u32[]{:S(2)}) collective-permute-start(f32[1,4,8,128]{3,2,1,0:T(8,128)} %bitcast.20), channel_id=1, source_target_pairs={{0,2},{1,3},{2,0},{3,1},{4,6},{5,7},{6,4},{7,5},{8,10},{9,11},{10,... | collective-permute-start | bytes 49160 | tf_op jit(solution)/shard_map/ppermute | solution.py:270
  3.7 0.7 %copy-start.8 = (s32[256,2]{0,1:T(2,128)S(1)}, s32[256,2]{0,1:T(2,128)}, u32[]{:S(2)}) copy-start(s32[256,2]{0,1:T(2,128)} %param.14) | copy-start | bytes 6148
  3.7 8.9 %collective-permute-start.3 = (f32[32,8,128]{2,1,0:T(8,128)}, f32[32,8,128]{2,1,0:T(8,128)S(1)}, u32[]{:S(2)}, u32[]{:S(2)}) collective-permute-start(f32[32,8,128]{2,1,0:T(8,128)} %bitcast.14), channel_id=1, source_target_pairs={{0,1},{1,0},{2,3},{3,2},{4,5},{5,4},{6,7},{7,6},{8,9},{9,8},{10,11... | collective-permute-start | bytes 393224 | tf_op jit(solution)/shard_map/ppermute | solution.py:272
  3.7 8.9 %collective-permute-start.4 = (f32[32,8,128]{2,1,0:T(8,128)}, f32[32,8,128]{2,1,0:T(8,128)S(1)}, u32[]{:S(2)}, u32[]{:S(2)}) collective-permute-start(f32[32,8,128]{2,1,0:T(8,128)} %bitcast.17), channel_id=1, source_target_pairs={{0,1},{1,0},{2,3},{3,2},{4,5},{5,4},{6,7},{7,6},{8,9},{9,8},{10,11... | collective-permute-start | bytes 393224 | tf_op jit(solution)/shard_map/ppermute | solution.py:273
  6.4 4.9 %collective-permute-start.1 = (f32[2,4,8,128]{3,2,1,0:T(8,128)S(1)}, f32[2,4,8,128]{3,2,1,0:T(8,128)S(1)}, u32[]{:S(2)}, u32[]{:S(2)}) collective-permute-start(f32[2,4,8,128]{3,2,1,0:T(8,128)S(1)} %pad_maximum_fusion.2), channel_id=1, source_target_pairs={{0,4},{1,5},{2,6},{3,7},{4,0},{5,1},{6,2},{7,3},{8,12},{9,13},{10,... | collective-permute-start | bytes 98312 | tf_op jit(solution)/shard_map/ppermute | solution.py:270
  9.4 1.9 %copy-start.2 = (f32[4,8,128]{2,1,0:T(8,128)S(1)}, f32[4,8,128]{2,1,0:T(8,128)}, u32[]{:S(2)}) copy-start(f32[4,8,128]{2,1,0:T(8,128)} %model.1) | copy-start | bytes 49156
  11.3 1.3 %collective-permute-start.2 = (f32[4,4,8,128]{3,2,1,0:T(8,128)S(1)}, f32[4,4,8,128]{3,2,1,0:T(8,128)S(1)}, u32[]{:S(2)}, u32[]{:S(2)}) collective-permute-start(f32[4,4,8,128]{3,2,1,0:T(8,128)S(1)} %pad_maximum_fusion.1), channel_id=1, source_target_pairs={{0,1},{1,0},{2,3},{3,2},{4,5},{5,4},{6,7},{7,6},{8,9},{9,8},{10,11... | collective-permute-start | bytes 196616 | tf_op jit(solution)/shard_map/ppermute | solution.py:270
  11.5 1.2 %copy-start = (f32[1,32,8,128]{3,2,1,0:T(8,128)S(1)}, f32[1,32,8,128]{3,2,1,0:T(8,128)}, u32[]{:S(2)}) copy-start(f32[1,32,8,128]{3,2,1,0:T(8,128)} %param.16) | copy-start | bytes 393220
  11.5 1.2 %copy-start.1 = (f32[1,32,8,128]{3,2,1,0:T(8,128)S(1)}, f32[1,32,8,128]{3,2,1,0:T(8,128)}, u32[]{:S(2)}) copy-start(f32[1,32,8,128]{3,2,1,0:T(8,128)} %param.17) | copy-start | bytes 393220
  13.5 4.6 %collective-permute-start.5 = (f32[16,8,128]{2,1,0:T(8,128)S(1)}, f32[16,8,128]{2,1,0:T(8,128)S(1)}, u32[]{:S(2)}, u32[]{:S(2)}) collective-permute-start(f32[16,8,128]{2,1,0:T(8,128)S(1)} %get-tuple-element.17), channel_id=1, source_target_pairs={{0,8},{1,25},{2,10},{3,27},{4,12},{5,29},{6,14},{7,31},{8,0},{9,17... | collective-permute-start | bytes 196616 | tf_op jit(solution)/shard_map/ppermute | solution.py:289
  18.1 1.3 %collective-permute-start.6 = (f32[16,8,128]{2,1,0:T(8,128)S(1)}, f32[16,8,128]{2,1,0:T(8,128)S(1)}, u32[]{:S(2)}, u32[]{:S(2)}) collective-permute-start(f32[16,8,128]{2,1,0:T(8,128)S(1)} %collective-permute-done.5.mine), channel_id=1, source_target_pairs={{0,1},{1,0},{2,3},{3,2},{4,5},{5,4},{6,7},{7,6},{8,9},{9,8},{10,11... | collective-permute-start | bytes 196616 | tf_op jit(solution)/shard_map/ppermute | solution.py:290
  18.1 1.2 %copy-start.5 = (s32[1,2]{1,0:T(1,128)S(1)}, s32[1,2]{1,0:T(1,128)}, u32[]{:S(2)}) copy-start(s32[1,2]{1,0:T(1,128)} %cells.1) | copy-start | bytes 28
  23.0 3.6 %collective-permute-start.7 = (f32[1,256]{1,0:T(1,128)S(1)}, f32[1,256]{1,0:T(1,128)S(1)}, u32[]{:S(2)}, u32[]{:S(2)}) collective-permute-start(f32[1,256]{1,0:T(1,128)S(1)} %get-tuple-element.19), channel_id=1, source_target_pairs={{0,8},{8,0},{16,24},{24,16},{1,9},{9,1},{17,25},{25,17},{2,10},{10... | collective-permute-start | bytes 3080 | tf_op jit(solution)/shard_map/ppermute | solution.py:307
  26.6 3.6 %collective-permute-start.8 = (f32[1,256]{1,0:T(1,128)S(1)}, f32[1,256]{1,0:T(1,128)S(1)}, u32[]{:S(2)}, u32[]{:S(2)}) collective-permute-start(f32[1,256]{1,0:T(1,128)S(1)} %add.47), channel_id=1, source_target_pairs={{0,16},{8,24},{16,0},{24,8},{1,17},{9,25},{17,1},{25,9},{2,18},{10... | collective-permute-start | bytes 3080 | tf_op jit(solution)/shard_map/ppermute | solution.py:307
  30.2 0.7 %copy-start.4 = (f32[1,256]{1,0:T(1,128)S(1)}, f32[1,256]{1,0:T(1,128)}, u32[]{:S(2)}) copy-start(f32[1,256]{1,0:T(1,128)} %observed.1) | copy-start | bytes 3076
  35.3 1.3 %collective-permute-start.9 = (f32[4,4,8,128]{3,2,1,0:T(8,128)S(1)}, f32[4,4,8,128]{3,2,1,0:T(8,128)S(1)}, u32[]{:S(2)}, u32[]{:S(2)}) collective-permute-start(f32[4,4,8,128]{3,2,1,0:T(8,128)S(1)} %slice.19), channel_id=1, source_target_pairs={{0,1},{1,0},{2,3},{3,2},{4,5},{5,4},{6,7},{7,6},{8,9},{9,8},{10,11... | collective-permute-start | bytes 196616 | tf_op jit(solution)/shard_map/ppermute | solution.py:326
  36.6 5.2 %collective-permute-start.10 = (f32[2,4,8,128]{3,2,1,0:T(8,128)S(1)}, f32[2,4,8,128]{3,2,1,0:T(8,128)S(1)}, u32[]{:S(2)}, u32[]{:S(2)}) collective-permute-start(f32[2,4,8,128]{3,2,1,0:T(8,128)S(1)} %slice.25), channel_id=1, source_target_pairs={{0,4},{1,5},{2,6},{3,7},{4,0},{5,1},{6,2},{7,3},{8,12},{9,13},{10,... | collective-permute-start | bytes 98312 | tf_op jit(solution)/shard_map/ppermute | solution.py:326
  41.8 3.8 %copy-start.3 = (s32[4,8,128]{2,1,0:T(8,128)S(1)}, s32[4,8,128]{2,1,0:T(8,128)}, u32[]{:S(2)}) copy-start(s32[4,8,128]{2,1,0:T(8,128)} %labels.1) | copy-start | bytes 49156
  41.8 3.8 %copy-start.6 = (f32[4]{0:T(128)S(1)}, f32[4]{0:T(128)}, u32[]{:S(2)}) copy-start(f32[4]{0:T(128)} %means.1) | copy-start | bytes 52
  41.8 3.8 %copy-start.7 = (f32[4]{0:T(128)S(1)}, f32[4]{0:T(128)}, u32[]{:S(2)}) copy-start(f32[4]{0:T(128)} %variances.1) | copy-start | bytes 52
  41.8 3.8 %collective-permute-start.11 = (f32[4,8,128]{2,1,0:T(8,128)S(1)}, f32[4,8,128]{2,1,0:T(8,128)S(1)}, u32[]{:S(2)}, u32[]{:S(2)}) collective-permute-start(f32[4,8,128]{2,1,0:T(8,128)S(1)} %get-tuple-element.30), channel_id=1, source_target_pairs={{0,2},{1,3},{2,0},{3,1},{4,6},{5,7},{6,4},{7,5},{8,10},{9,11},{10,... | collective-permute-start | bytes 49160 | tf_op jit(solution)/shard_map/ppermute | solution.py:327

commit v2 on v1

v2 whole, which is shorter than its diff:
```python
import functools

import jax
import jax.numpy as jnp
from jax import lax
from jax.experimental import pallas as pl
from jax.experimental.pallas import tpu as pltpu
from jax.sharding import PartitionSpec as P

SWEEPS = 8
CLUSTERS = 4

LEAKAGE = 0.05
WEIGHT_X = 1.0
WEIGHT_Y = 0.5
WEIGHT_Z = 0.5
SMALLNESS = 1.0

GROUPS = 4
SLOT = 32
HALF = SLOT // 2
PACK_AT = 1
DEPTH = 8

F32 = jnp.float32
BF16 = jnp.bfloat16
VMEM = pl.BlockSpec(memory_space=pltpu.VMEM)
SMEM = pl.BlockSpec(memory_space=pltpu.SMEM)
HBM = pl.BlockSpec(memory_space=pl.ANY)
BESIDE = pl.CostEstimate(flops=0, bytes_accessed=4_000_000, transcendentals=0)
PARAMS = pltpu.CompilerParams(vmem_limit_bytes=24 * 1024 * 1024)


def xor_pairs(count, bit):
    return [(i, i ^ bit) for i in range(count)]


def lane_of(shape):
    return lax.broadcasted_iota(jnp.int32, shape, len(shape) - 1)


def depth_of(shape):
    return lax.broadcasted_iota(jnp.int32, shape, 0)


def turn(values, shift):
    return pltpu.roll(values, shift % 128, 1)


def up_depth(values):
    return pltpu.roll(values, values.shape[0] - 1, 0)


def down_depth(values):
    return pltpu.roll(values, 1, 0)


def full(value, shape):
    return jnp.full(shape, value, jnp.int32)


def each(count, body, unroll):
    def step(k, carry):
        body(k)
        return carry

    lax.fori_loop(0, count, step, 0, unroll=unroll)


def swap_halves(values):
    upper = lane_of(values.shape) % SLOT >= HALF
    return jnp.where(upper, turn(values, HALF), turn(values, -HALF))


def merge(pieces):
    group = lane_of(pieces[0].shape) // SLOT
    out = pieces[0]
    for g in range(1, GROUPS):
        out = jnp.where(group == g, pieces[g], out)
    return out


def rim_columns(shape, width):
    slot = lane_of(shape) % SLOT
    return HALF - 1 - slot + jnp.where(slot < HALF, width, 0)


def edges(row_of, k, per, shape):
    index = (HALF - 1 - lane_of(shape) % SLOT) & 127
    return merge([jnp.take_along_axis(row_of(k + per * g), index, axis=1) for g in range(GROUPS)])


def upper_is(right, shape):
    return (lane_of(shape) % SLOT) // HALF == full(right, shape)


def pack_fields_kernel(info, own_v, own_a, other_v, other_a, passed, payload, passed_on):
    del passed, passed_on
    per = own_v.shape[0] // GROUPS
    shape = own_v.shape[1:]
    mask = upper_is(info[1], shape)

    def body(k):
        for n, (own, other) in enumerate(((own_v, other_v), (own_a, other_a))):
            far = swap_halves(edges(lambda y: other[y], k, per, shape))
            payload[n * per + k] = jnp.where(mask, edges(lambda y: own[y], k, per, shape), far)

    each(per, body, 4)


def pack_model_kernel(order, info, gathered, part, payload, model):
    del part
    peers, rows_own = gathered.shape[:2]
    per = model.shape[0] // GROUPS
    shape = gathered.shape[2:]
    mask = upper_is(info[1], shape)
    for i in range(peers):
        j = sum(((i >> n) & 1) << bit for n, bit in enumerate(order))
        model[pl.ds((info[0] ^ j) * rows_own, rows_own)] = gathered[i]
    for k in range(per // 2):
        first, second = edges(lambda y: model[y], k, per, shape), edges(lambda y: model[y], k + per // 2, per, shape)
        payload[2 * per + k] = jnp.where(mask, first, swap_halves(second))


def own_field_kernel(
    total_x, info, cells, means, variances, labels, own_model, model, warm, observed,
    scale, prior, main, main_2, b_m, b_r, measured, nothing,
):
    rows, depth, width = warm.shape
    shape = (depth, width)
    per = rows // GROUPS
    first_col = info[2]
    nothing[...] = jnp.zeros(nothing.shape, F32)
    measured[...] = jnp.where(full(first_col, observed.shape) == 0, observed[...], 0.0)
    m = own_model[...]
    label = labels[...]
    mean_cell = jnp.zeros(m.shape, F32)
    var_cell = jnp.zeros(m.shape, F32)
    for cluster in range(CLUSTERS):
        mean_cell = jnp.where(label == cluster, means[cluster], mean_cell)
        var_cell = jnp.where(label == cluster, variances[cluster], var_cell)
    scale[...] = -jnp.exp(m)
    prior[...] = SMALLNESS * (m - mean_cell) / var_cell

    def body(k):
        for g in range(GROUPS):
            y = k + per * g
            r = k + (per + 2) * g
            shift = SLOT * g + HALF
            put_row(main, r, turn(warm[y], shift))
            put_row(main_2, r, turn(jnp.exp(model[y]), shift))
            b_m[y] = jnp.zeros(shape, F32)
        b_r[k] = jnp.zeros(shape, F32)

    each(per, body, 2)
    clear_ends(main, per)
    clear_ends(main_2, per)
    lane, depth_at = lane_of(shape), depth_of(shape)
    for n, sign in ((0, 1.0), (1, -1.0)):
        cell = cells[0, n]
        line = cell // total_x
        x = cell - line * total_x
        y = line // depth
        g = y // per
        k = y - g * per
        at_depth = depth_at == line - y * depth
        col_m = first_col + ((lane - (SLOT * g + HALF)) & 127)
        b_m[y] = b_m[y] + jnp.where((col_m == x) & at_depth, sign, 0.0)
        at_slot = (first_col + columns(GROUPS, shape) == x) & (lane // SLOT == g)
        b_r[k] = b_r[k] + jnp.where(at_slot & at_depth, sign, 0.0)


def own_adjoint_kernel(info, mine, theirs, warm, spots, main, rim, hit_x):
    rows, depth, width = warm.shape
    per = rows // GROUPS
    mask = ~upper_is(info[1], (depth, width))

    def body(k):
        for g in range(GROUPS):
            put_row(main, k + (per + 2) * g, turn(warm[k + per * g], SLOT * g + HALF))
        put_row(rim, k, jnp.where(mask, mine[per + k], swap_halves(theirs[per + k])))

    each(per, body, 2)
    clear_ends(main, per)
    at = depth_of((2 * width, spots.shape[1]))
    slot = at % SLOT
    at = info[2] + jnp.where(at < width, at, HALF - 1 - slot + jnp.where(slot < HALF, width, 0))
    hit_x[...] = jnp.where(at == spots[0:1, :], 1.0, 0.0).astype(BF16)


def save_kernel(value, out, sem):
    copy = pltpu.make_async_copy(value, out.at[0], sem)
    copy.start()
    copy.wait()


def at_row(ref, y, shift=0):
    return ref[(y + 1) * DEPTH + shift : (y + 2) * DEPTH + shift, :]


def put_row(ref, y, values):
    start = (y + 1) * DEPTH
    if not isinstance(y, int):
        start = pl.multiple_of(start, DEPTH)
    ref[pl.ds(start, DEPTH), :] = values


def neighbours(main, rim, k, per):
    packed = at_row(rim, k)
    shape = packed.shape
    lane = lane_of(shape)
    slot = lane % SLOT
    own = [at_row(main, g * (per + 2) + k) for g in range(GROUPS)]
    before, after = [], []
    for g in range(GROUPS):
        last = SLOT * g + HALF - 1
        after.append(jnp.where(lane == last, packed, turn(own[g], -1)))
        before.append(jnp.where(lane == last + 1, packed, turn(own[g], 1)))
    inner = merge(own)
    before.append(jnp.where(slot == HALF - 1, inner, turn(packed, -1)))
    after.append(jnp.where(slot == HALF, inner, turn(packed, 1)))
    own.append(packed)
    return own, before, after


def wrap(main, rim, per):
    put_row(rim, -1, turn(at_row(rim, per - 1), SLOT))
    put_row(rim, per, turn(at_row(rim, 0), -SLOT))
    for g in range(1, GROUPS):
        start = g * (per + 2)
        put_row(main, start - 1, turn(at_row(main, start - 3), SLOT))
        put_row(main, start - 2, turn(at_row(main, start), -SLOT))


def clear_ends(main, per):
    put_row(main, -1, jnp.zeros((DEPTH, main.shape[1]), F32))
    put_row(main, GROUPS * (per + 2) - 2, jnp.zeros((DEPTH, main.shape[1]), F32))


def sweep(old, new, face_m, face_r, b_m, b_r):
    per = b_r.shape[0]
    rows = per * GROUPS
    main, rim = old
    main_new, rim_new = new
    for k in range(per):
        own, before, after = neighbours(main, rim, k, per)
        for g in range(GROUPS + 1):
            n = min(g, GROUPS) // GROUPS
            field, face, b = (old[n], (face_m, face_r)[n], (b_m, b_r)[n])
            y = k if n else k + per * g
            r = k if n else k + (per + 2) * g
            c = k if n else k + (per + 1) * g
            total = b[y] + face[0, c + 1] * after[g] + face[1, c + 1] * before[g]
            total = total + (face[3, c + 1] * at_row(field, r, 1) + face[4, c + 1] * at_row(field, r, -1))
            if n or y + 1 < rows:
                total = total + face[2, c + 1] * at_row(field, r + 1)
            if n or y > 0:
                total = total + face[2, c] * at_row(field, r - 1)
            put_row(new[n], r, total * face[5, c + 1])
    wrap(main_new, rim_new, per)


def relax(first, second, face_m, face_r, b_m, b_r):
    per = b_r.shape[0]
    clear_ends(second[0], per)
    wrap(*first, per)

    def two(_, carry):
        sweep(first, second, face_m, face_r, b_m, b_r)
        sweep(second, first, face_m, face_r, b_m, b_r)
        return carry

    lax.fori_loop(0, SWEEPS // 2, two, 0)


def three_parts(values):
    high = values.astype(BF16)
    rest = values - high.astype(F32)
    middle = rest.astype(BF16)
    low = (rest - middle.astype(F32)).astype(BF16)
    return high, middle, low


def columns(g, shape):
    if g == GROUPS:
        return rim_columns(shape, shape[1])
    return (lane_of(shape) - (SLOT * g + HALF)) & 127


def coefficients(total_x, first_col, main, rim, face_m, face_r):
    per = face_r.shape[1] - 1
    rows = per * GROUPS
    shape = face_r.shape[2:]
    group = lane_of(shape) // SLOT
    bottom = depth_of(shape) == shape[0] - 1
    for k in range(per):
        own, before, after = neighbours(main, rim, k, per)
        for g in range(GROUPS + 1):
            n = g // GROUPS
            field, face = ((main, rim)[n], (face_m, face_r)[n])
            y = k if n else k + per * g
            r = k if n else k + (per + 2) * g
            c = k if n else k + (per + 1) * g
            col = first_col + columns(g, shape)
            s = own[g]
            fx = jnp.where((col == total_x - 1) | (col == -1), 0.0, WEIGHT_X * 0.5 * (s + after[g]))
            bx = jnp.where((col == 0) | (col == total_x), 0.0, WEIGHT_X * 0.5 * (before[g] + s))
            fz = jnp.where(bottom, 0.0, WEIGHT_Z * 0.5 * (s + up_depth(s)))
            bz = down_depth(fz)
            fy = WEIGHT_Y * 0.5 * (s + at_row(field, r + 1))
            by = WEIGHT_Y * 0.5 * (at_row(field, r - 1) + s)
            if n and k == 0:
                by = jnp.where(group == 0, 0.0, by)
            if n and k == per - 1:
                fy = jnp.where(group == GROUPS - 1, 0.0, fy)
            if not n and y == 0:
                by = jnp.zeros(shape, F32)
            if not n and y == rows - 1:
                fy = jnp.zeros(shape, F32)
            diagonal = fx + bx + fy + by + fz + bz + LEAKAGE * s
            face[0, c + 1] = fx
            face[1, c + 1] = bx
            face[2, c + 1] = fy
            if not n and k == 0:
                face[2, c] = by
            face[3, c + 1] = fz
            face[4, c + 1] = bz
            face[5, c + 1] = 1.0 / diagonal
    face_r[2, 0] = turn(face_r[2, per], SLOT)


def field_kernel(
    total_x, info, mine, theirs, main_in, sigma_in, b_m, b_r, spots, measured,
    picked, plain, main, rim, face_m, face_r, main_2, rim_2,
):
    del main_in, sigma_in
    rows, depth, width = plain.shape
    shape = (depth, width)
    per = rows // GROUPS
    right, first_col = info[1], info[2]
    mask = ~upper_is(right, shape)
    for k in range(per):
        put_row(rim, k, jnp.where(mask, mine[k], swap_halves(theirs[k])))
    for k in range(per // 2):
        near, far = mine[2 * per + k], theirs[2 * per + k]
        put_row(rim_2, k, jnp.exp(jnp.where(mask, near, far)))
        put_row(rim_2, k + per // 2, jnp.exp(swap_halves(jnp.where(mask, far, near))))
    wrap(main_2, rim_2, per)
    coefficients(total_x, first_col, main_2, rim_2, face_m, face_r)
    relax((main, rim), (main_2, rim_2), face_m, face_r, b_m, b_r)
    for y in range(rows):
        plain[y] = turn(at_row(main, y + 2 * (y // per)), -(SLOT * (y // per) + HALF))
    count = spots.shape[1]
    x_row = spots[0:1, :] - first_col
    line_row = spots[1:2, :]
    hit_x = jnp.where(depth_of((width, count)) == x_row, 1.0, 0.0).astype(BF16)
    flat = plain[...].reshape(rows * depth, width)
    lines = sum(jnp.dot(part, hit_x, preferred_element_type=F32) for part in three_parts(flat))
    hit_line = depth_of((rows * depth, count)) == line_row
    got = jnp.sum(jnp.where(hit_line, lines, 0.0), axis=0, keepdims=True)
    picked[...] = got[:, : count // 2] - got[:, count // 2 :] - measured[...]


def adjoint_kernel(
    total_x, places, info, picked, spots, main_in, rim_in, hit_x, main_v, rim_v, face_m, face_r,
    misfit_out, terms, plain, main, rim, main_2, rim_2, b_m, b_r,
):
    del main_in, rim_in
    rows, depth, width = plain.shape
    shape = (depth, width)
    per = rows // GROUPS
    me, first_col = info[0], info[2]
    count = spots.shape[1]
    misfit = picked[...]
    misfit_out[...] = misfit
    weights = jnp.concatenate([misfit, -misfit], axis=1)
    hit_line = depth_of((rows * depth, count)) == spots[1:2, :]
    flat = jnp.zeros((rows * depth, 2 * width), F32)
    for part in three_parts(weights):
        left = jnp.where(hit_line, part.astype(F32), 0.0).astype(BF16)
        flat = flat + lax.dot_general(left, hit_x[...], (((1,), (1,)), ((), ())), preferred_element_type=F32)
    flat = flat.reshape(rows, depth, 2 * width)
    for y in range(rows):
        b_m[y] = turn(flat[y, :, :width], SLOT * (y // per) + HALF)
    for k in range(per):
        b_r[k] = merge([flat[k + per * g, :, width:] for g in range(GROUPS)])
    relax((main, rim), (main_2, rim_2), face_m, face_r, b_m, b_r)
    for y in range(rows):
        plain[y] = turn(at_row(main, y + 2 * (y // per)), -(SLOT * (y // per) + HALF))
    rows_own = terms.shape[1]
    bottom = depth_of(shape) == depth - 1
    for k in range(per):
        f_own, f_before, f_after = neighbours(main_v, rim_v, k, per)
        a_own, a_before, a_after = neighbours(main, rim, k, per)
        for g in range(GROUPS):
            y, r = k + per * g, k + (per + 2) * g
            col = first_col + columns(g, shape)
            f, a = f_own[g], a_own[g]
            px_next = jnp.where(col == total_x - 1, 0.0, (f_after[g] - f) * (a_after[g] - a))
            px_prev = jnp.where(col == 0, 0.0, (f - f_before[g]) * (a - a_before[g]))
            py = jnp.zeros(shape, F32)
            if y + 1 < rows:
                py = py + (at_row(main_v, r + 1) - f) * (at_row(main, r + 1) - a)
            if y > 0:
                py = py + (f - at_row(main_v, r - 1)) * (a - at_row(main, r - 1))
            pz = jnp.where(bottom, 0.0, (at_row(main_v, r, 1) - f) * (at_row(main, r, 1) - a))
            pz = pz + down_depth(pz)
            paired = WEIGHT_X * (px_prev + px_next) + WEIGHT_Y * py + WEIGHT_Z * pz
            j = me ^ (y // rows_own)
            place = sum(((j >> bit) & 1) << n for n, bit in enumerate(reversed(places)))
            term = 0.5 * paired + LEAKAGE * f * a
            terms[place, y % rows_own] = turn(term, -(SLOT * g + HALF))


def gradient_kernel(scale, prior, kept, came, gradient):
    gradient[...] = scale[...] * (kept[...] + came[...]) + prior[...]


def on_device(
    log_conductivity,
    cluster_labels,
    cluster_means,
    cluster_vars,
    source_cells,
    receiver_cells,
    observed,
    warm_potential,
    warm_adjoint,
):
    tile, src = lax.axis_index("tile"), lax.axis_index("src")
    tiles, peers = lax.axis_size("tile"), lax.axis_size("src")
    rows_own, depth, width = log_conductivity.shape
    rows = rows_own * peers
    per = rows // GROUPS
    total_x = width * tiles
    receivers = receiver_cells.shape[0]
    bits = [1 << n for n in range(peers.bit_length() - 1)]
    levels = list(range(len(bits)))
    right = 1 - (tile + src) % 2
    info = jnp.stack([src, right, tile * width]).astype(jnp.int32)
    spots = receiver_cells.T.reshape(1, 2 * receivers)
    spots = jnp.concatenate([spots % total_x, spots // total_x], axis=0)
    spots = jnp.pad(spots, ((0, 6), (0, 0)), constant_values=-1)
    start_v, start_a = warm_potential[0], warm_adjoint[0]

    def shaped(*sizes):
        return jax.ShapeDtypeStruct(sizes, F32)

    other_v = lax.ppermute(start_v, "src", xor_pairs(peers, 1))
    other_a = lax.ppermute(start_a, "src", xor_pairs(peers, 1))
    order = levels[:0:-1] + [0]
    own = log_conductivity[None]
    gathered = lax.optimization_barrier(jnp.pad(own, ((0, peers - 1), (0, 0), (0, 0), (0, 0))))
    for n, level in enumerate(order):
        sent = own if n == 0 else gathered[: 1 << n]
        came = lax.ppermute(sent, "src", xor_pairs(peers, bits[level]))
        if n == PACK_AT:
            payload, gathered = pl.pallas_call(
                pack_fields_kernel,
                out_shape=(shaped(5 * per // 2, depth, width), shaped(*gathered.shape)),
                in_specs=[SMEM] + [VMEM] * 5,
                out_specs=(VMEM, VMEM),
                input_output_aliases={5: 1},
                cost_estimate=BESIDE,
                compiler_params=PARAMS,
            )(info, start_v, start_a, other_v, other_a, gathered)
        gathered = lax.dynamic_update_slice(gathered, came, (1 << n, 0, 0, 0))
    payload, model = pl.pallas_call(
        functools.partial(pack_model_kernel, order),
        out_shape=(shaped(*payload.shape), shaped(rows, depth, width)),
        in_specs=[SMEM, VMEM, VMEM],
        out_specs=(VMEM, VMEM),
        input_output_aliases={2: 0},
        compiler_params=PARAMS,
    )(info, gathered, payload)
    pairs = []
    for t in range(tiles):
        for s in range(peers):
            t_to = (t + 1) % tiles if (t + s) % 2 == 0 else (t - 1) % tiles
            pairs.append((t * peers + s, t_to * peers + s))
    mine = lax.ppermute(payload, ("tile", "src"), pairs)
    main_shape, rim_shape = ((rows + 2 * GROUPS) * depth, width), ((per + 2) * depth, width)
    scale, prior, main_v, sigma, b_m, b_r, measured, nothing = pl.pallas_call(
        functools.partial(own_field_kernel, total_x),
        out_shape=(shaped(*log_conductivity.shape),) * 2
        + (shaped(*main_shape),) * 2
        + (
            shaped(rows, depth, width),
            shaped(per, depth, width),
            shaped(*observed.shape),
            shaped(1, depth, width),
        ),
        in_specs=[SMEM] * 4 + [VMEM] * 5,
        out_specs=(VMEM,) * 8,
        cost_estimate=BESIDE,
        compiler_params=PARAMS,
    )(
        info, source_cells, cluster_means, cluster_vars, cluster_labels, log_conductivity,
        model, start_v, observed,
    )
    theirs = lax.ppermute(mine + nothing, "src", xor_pairs(peers, 1))
    picked, plain_v, main_v, rim_v, face_m, face_r, _ = pl.pallas_call(
        functools.partial(field_kernel, total_x),
        out_shape=(
            shaped(1, receivers),
            shaped(rows, depth, width),
            shaped(*main_shape),
            shaped(*rim_shape),
            shaped(6, rows + GROUPS, depth, width),
            shaped(6, per + 1, depth, width),
            shaped(*main_shape),
        ),
        in_specs=[SMEM] + [VMEM] * 8,
        out_specs=(VMEM,) * 7,
        input_output_aliases={3: 2, 4: 6},
        scratch_shapes=[pltpu.VMEM(rim_shape, F32)],
        compiler_params=PARAMS,
    )(info, mine, theirs, main_v, sigma, b_m, b_r, spots, measured)
    main_a, rim_a, hit_x = pl.pallas_call(
        own_adjoint_kernel,
        out_shape=(
            shaped(*main_shape),
            shaped(*rim_shape),
            jax.ShapeDtypeStruct((2 * width, 2 * receivers), BF16),
        ),
        in_specs=[SMEM] + [VMEM] * 4,
        out_specs=(VMEM,) * 3,
        cost_estimate=BESIDE,
        compiler_params=PARAMS,
    )(info, mine, theirs, start_a, spots)

    def saved(value, shape):
        return pl.pallas_call(
            save_kernel,
            out_shape=shaped(*shape),
            in_specs=[VMEM],
            out_specs=HBM,
            scratch_shapes=[pltpu.SemaphoreType.DMA],
            cost_estimate=BESIDE,
            compiler_params=PARAMS,
        )(value)

    field = saved(plain_v, warm_potential.shape)
    step = 1
    while step < tiles:
        picked = picked + lax.ppermute(picked, "tile", xor_pairs(tiles, step))
        step *= 2

    misfit, terms, plain_a, _, _ = pl.pallas_call(
        functools.partial(adjoint_kernel, total_x, levels),
        out_shape=(
            shaped(*observed.shape),
            shaped(peers, rows_own, depth, width),
            shaped(rows, depth, width),
            shaped(*main_shape),
            shaped(*rim_shape),
        ),
        in_specs=[SMEM] + [VMEM] * 9,
        out_specs=(VMEM,) * 5,
        input_output_aliases={3: 3, 4: 4},
        scratch_shapes=[
            pltpu.VMEM(main_shape, F32),
            pltpu.VMEM(rim_shape, F32),
            pltpu.VMEM((rows, depth, width), F32),
            pltpu.VMEM((per, depth, width), F32),
        ],
        compiler_params=PARAMS,
    )(info, picked, spots, main_a, rim_a, hit_x, main_v, rim_v, face_m, face_r)
    adjoint = saved(plain_a, warm_adjoint.shape)

    for level in levels[:-1]:
        keep = terms.shape[0] // 2
        terms = terms[:keep] + lax.ppermute(terms[keep:], "src", xor_pairs(peers, bits[level]))
    came = lax.ppermute(terms[1], "src", xor_pairs(peers, bits[-1]))
    gradient = pl.pallas_call(
        gradient_kernel,
        out_shape=shaped(*log_conductivity.shape),
        in_specs=[VMEM] * 4,
        out_specs=VMEM,
        compiler_params=PARAMS,
    )(scale, prior, terms[0], came)
    return (field, adjoint, misfit, gradient)


def solution(mesh):
    in_specs = (
        P("src", None, "tile"),
        P("src", None, "tile"),
        P(),
        P(),
        P("src", None),
        P(),
        P("src", None),
        P("src", None, None, "tile"),
        P("src", None, None, "tile"),
    )
    out_specs = (
        P("src", None, None, "tile"),
        P("src", None, None, "tile"),
        P("src", None),
        P("src", None, "tile"),
    )
    return jax.shard_map(
        on_device, mesh=mesh, in_specs=in_specs, out_specs=out_specs, check_vma=False
    )
```

time: 47.1 us -> 43.5 us (0.924)
  waiting for transfers between devices: 16.6 us -> 11.8 us
  Pallas kernels: 10.1 us -> 11.6 us
  other arithmetic: 0.87 us -> 0.14 us
  local copies, waits for them, and re-layouts: 0.91 us -> 1.43 us
    ppermute x5, waiting for transfers between devices: 7.32 us -> 4.46 us  [the longest x3 2.85 us: on_device(): came = lax.ppermute(sent, 'src', xor_pairs(peers, bits[level]))]
    pallas_call x4 -> x9, Pallas kernels: 10.1 us -> 11.6 us  [the longest x1 3.25 us: on_device(): pl.pallas_call(functools.partial(adjoint_kernel, total_x, levels), out_sh...]
    ppermute x1, waiting for transfers between devices: 2.67 us -> 1.32 us  [on_device(): mine = lax.ppermute(payload, ('tile', 'src'), pairs)]
    ppermute x2, starting transfers between devices: 3.34 us -> 2.12 us  [on_device(): lax.ppermute(terms[keep:], 'src', xor_pairs(peers, bits[level]))]
    ppermute x5, starting transfers between devices: 8.14 us -> 9.27 us  [the longest x3 6.08 us: on_device(): came = lax.ppermute(sent, 'src', xor_pairs(peers, bits[level]))]
    concatenate x3 -> x0, other arithmetic: 0.73 us -> none  [on_device(): gathered = jnp.concatenate([gathered, came], axis=0)]
    ppermute x2, waiting for transfers between devices: 3.49 us -> 2.9 us  [on_device(): picked = picked + lax.ppermute(picked, 'tile', xor_pairs(tiles, step))]
    unnamed x19, local copies, waits for them, and re-layouts: 0.89 us -> 1.38 us
  transfers between devices with their start and end apart: 12 -> 12, of which waited for: 10 -> 10; matrix products, arithmetic and copies ran while one was open for 2% -> 0% of each run, Pallas kernels for 0% -> 10%
where the time goes in v2:
time: 43.5 us; the launch traced here: 43.2 us
  starting transfers between devices  17.4 us (40%)
  waiting for transfers between devices  11.8 us (27%)
  Pallas kernels  11.6 us (27%)
  local copies, waits for them, and re-layouts  1.43 us (3%)
  between operations  0.84 us (2%)
    ppermute x3, starting transfers between devices, on_device(): came = lax.ppermute(sent, 'src', xor_pairs(peers, bits[level]))  6.08 us
    ppermute x2, starting transfers between devices, on_device(): picked = picked + lax.ppermute(picked, 'tile', xor_pairs(tiles, step))  3.56 us
    pallas_call x1, Pallas kernels, on_device(): pl.pallas_call(functools.partial(adjoint_kernel, total_x, levels), out_sh...  3.25 us
    ppermute x2, waiting for transfers between devices, on_device(): lax.ppermute(terms[keep:], 'src', xor_pairs(peers, bits[level]))  3.14 us
    ppermute x1, starting transfers between devices, on_device(): came = lax.ppermute(terms[1], 'src', xor_pairs(peers, bits[-1]))  3.11 us
    ppermute x2, waiting for transfers between devices, on_device(): picked = picked + lax.ppermute(picked, 'tile', xor_pairs(tiles, step))  2.9 us
    pallas_call x1, Pallas kernels, on_device(): pl.pallas_call(functools.partial(field_kernel, total_x), out_shape=(shape...  2.87 us
    ppermute x3, waiting for transfers between devices, on_device(): came = lax.ppermute(sent, 'src', xor_pairs(peers, bits[level]))  2.85 us
  transfers between devices with their start and end apart: 12, of which 10 were waited for; matrix products, arithmetic and copies ran while one was open for 0% of the time, Pallas kernels for 10%

profile of v2, /device:TPU:0, one launch (start us, length us, event | category | flops | bytes accessed | tf_op | source)
XLA Modules:
  0.0 43.2 jit_solution(16552112944314291769)
XLA Ops:
  0.6 4.1 %collective-permute-start.2 = (f32[1,4,8,128]{3,2,1,0:T(8,128)}, f32[1,4,8,128]{3,2,1,0:T(8,128)S(1)}, u32[]{:S(2)}, u32[]{:S(2)}) collective-permute-start(f32[1,4,8,128]{3,2,1,0:T(8,128)} %bitcast.21), channel_id=1, source_target_pairs={{0,4},{1,5},{2,6},{3,7},{4,0},{5,1},{6,2},{7,3},{8,12},{9,13},{10,... | collective-permute-start | bytes 49160 | tf_op jit(solution)/shard_map/ppermute | solution.py:456
  4.7 0.0 collective-permute-start
  4.7 0.5 %collective-permute-start.1 = (f32[32,8,128]{2,1,0:T(8,128)}, f32[32,8,128]{2,1,0:T(8,128)S(1)}, u32[]{:S(2)}, u32[]{:S(2)}) collective-permute-start(f32[32,8,128]{2,1,0:T(8,128)} %bitcast.18), channel_id=1, source_target_pairs={{0,1},{1,0},{2,3},{3,2},{4,5},{5,4},{6,7},{7,6},{8,9},{9,8},{10,11... | collective-permute-start | bytes 393224 | tf_op jit(solution)/shard_map/ppermute | solution.py:450
  5.2 0.0 copy-start.2
  5.2 0.0 copy-start.8
  5.2 0.0 copy-start.1
  5.3 0.0 copy-start
  5.3 0.7 %copy-done.2 = f32[4,8,128]{2,1,0:T(8,128)S(1)} copy-done((f32[4,8,128]{2,1,0:T(8,128)S(1)}, f32[4,8,128]{2,1,0:T(8,128)}, u32[]{:S(2)}) %copy-start.2) | copy-done | bytes 16408
  6.0 0.7 %collective-permute-done.2 = f32[1,4,8,128]{3,2,1,0:T(8,128)S(1)} collective-permute-done((f32[1,4,8,128]{3,2,1,0:T(8,128)}, f32[1,4,8,128]{3,2,1,0:T(8,128)S(1)}, u32[]{:S(2)}, u32[]{:S(2)}) %collective-permute-start.2) | collective-permute-done | bytes 16416 | tf_op jit(solution)/shard_map/ppermute | solution.py:456
  6.7 1.9 %collective-permute-start.3 = (f32[2,4,8,128]{3,2,1,0:T(8,128)S(1)}, f32[2,4,8,128]{3,2,1,0:T(8,128)S(1)}, u32[]{:S(2)}, u32[]{:S(2)}) collective-permute-start(f32[2,4,8,128]{3,2,1,0:T(8,128)S(1)} %slice.32), channel_id=1, source_target_pairs={{0,2},{1,3},{2,0},{3,1},{4,6},{5,7},{6,4},{7,5},{8,10},{9,11},{10,... | collective-permute-start | bytes 98312 | tf_op jit(solution)/shard_map/ppermute | solution.py:456
  8.6 0.1 pad_add_fusion.1.info
  8.7 0.0 copy-done.8
  8.7 0.0 collective-permute-done.other_v
  8.7 0.0 collective-permute-done.1.other_a
  8.7 0.0 copy-done.1
  8.7 0.0 copy-done
  8.7 0.9 %shard_map.120 = (f32[20,8,128]{2,1,0:T(8,128)S(1)}, f32[8,4,8,128]{3,2,1,0:T(8,128)S(1)}) custom-call(s32[3]{0:T(128)S(1)} %pad_add_fusion.1.info, f32[32,8,128]{2,1,0:T(8,128)S(1)} %bitcast.16, f32[32,8,128]{2,1,0:T(8,128)S(1)} %bitcast.19, f32[32,8,128]{2,1,0:T(8,128)S(1)} %collective-permute-done.other_v, ...), custom_call_target="tpu_custom_call", output_to_operand_aliasing={{1}: (5, {})} | custom-call | bytes 4000000 | tf_op jit(solution)/shard_map/pallas_call | solution.py:458
  9.6 0.9 %collective-permute-done.3 = f32[2,4,8,128]{3,2,1,0:T(8,128)S(1)} collective-permute-done((f32[2,4,8,128]{3,2,1,0:T(8,128)S(1)}, f32[2,4,8,128]{3,2,1,0:T(8,128)S(1)}, u32[]{:S(2)}, u32[]{:S(2)}) %collective-permute-start.3) | collective-permute-done | bytes 32800 | tf_op jit(solution)/shard_map/ppermute | solution.py:456
  10.6 0.1 collective-permute-start.4
  10.7 1.2 %collective-permute-done.4 = f32[4,4,8,128]{3,2,1,0:T(8,128)S(1)} collective-permute-done((f32[4,4,8,128]{3,2,1,0:T(8,128)S(1)}, f32[4,4,8,128]{3,2,1,0:T(8,128)S(1)}, u32[]{:S(2)}, u32[]{:S(2)}) %collective-permute-start.4) | collective-permute-done | bytes 65568 | tf_op jit(solution)/shard_map/ppermute | solution.py:456
  11.9 0.0 copy-start.3
  11.9 0.0 copy-start.6
  11.9 0.0 copy-start.7
  12.0 0.7 %shard_map.121 = (f32[20,8,128]{2,1,0:T(8,128)S(1)}, f32[32,8,128]{2,1,0:T(8,128)S(1)}) custom-call(s32[3]{0:T(128)S(1)} %pad_add_fusion.1.info, f32[8,4,8,128]{3,2,1,0:T(8,128)S(1)} %constant_dynamic-update-slice_fusion.gathered, f32[20,8,128]{2,1,0:T(8,128)S(1)} %get-tuple-element.29.part), custom_call_target="tpu_custom_call", output_to_operand_aliasing={{0}: (2, {})} | custom-call | tf_op jit(solution)/shard_map/pallas_call | solution.py:468
  12.7 1.9 %collective-permute-start.5 = (f32[20,8,128]{2,1,0:T(8,128)S(1)}, f32[20,8,128]{2,1,0:T(8,128)S(1)}, u32[]{:S(2)}, u32[]{:S(2)}) collective-permute-start(f32[20,8,128]{2,1,0:T(8,128)S(1)} %get-tuple-element.30), channel_id=1, source_target_pairs={{0,8},{1,25},{2,10},{3,27},{4,12},{5,29},{6,14},{7,31},{8,0},{9,17... | collective-permute-start | bytes 245768 | tf_op jit(solution)/shard_map/ppermute | solution.py:481
  14.6 0.0 copy-start.4
  14.6 0.0 copy-start.5
  14.6 0.0 copy-done.3
  14.6 0.0 copy-done.6
  14.7 0.0 copy-done.7
  14.7 0.6 %copy-done.4 = f32[1,256]{1,0:T(1,128)S(1)} copy-done((f32[1,256]{1,0:T(1,128)S(1)}, f32[1,256]{1,0:T(1,128)}, u32[]{:S(2)}) %copy-start.4) | copy-done | bytes 1048
  15.3 0.0 copy-done.5
  15.3 1.0 %shard_map.122 = (f32[4,8,128]{2,1,0:T(8,128)S(1)}, f32[4,8,128]{2,1,0:T(8,128)S(1)}, f32[320,128]{1,0:T(8,128)S(1)}, f32[320,128]{1,0:T(8,128)S(1)}, f32[32,8,1...) custom-call(s32[3]{0:T(128)S(1)} %pad_add_fusion.1.info, ...), custom_call_target="tpu_custom_call" | custom-call | bytes 4000000 | tf_op jit(solution)/shard_map/pallas_call | solution.py:483
  16.3 1.3 %collective-permute-done.5.mine = f32[20,8,128]{2,1,0:T(8,128)S(1)} collective-permute-done((f32[20,8,128]{2,1,0:T(8,128)S(1)}, f32[20,8,128]{2,1,0:T(8,128)S(1)}, u32[]{:S(2)}, u32[]{:S(2)}) %collective-permute-start.5) | collective-permute-done | bytes 81952 | tf_op jit(solution)/shard_map/ppermute | solution.py:481
  17.6 0.1 collective-permute-start.6
  17.7 1.2 %collective-permute-done.6.theirs = f32[20,8,128]{2,1,0:T(8,128)S(1)} collective-permute-done((f32[20,8,128]{2,1,0:T(8,128)S(1)}, f32[20,8,128]{2,1,0:T(8,128)S(1)}, u32[]{:S(2)}, u32[]{:S(2)}) %collective-permute-start.6) | collective-permute-done | bytes 81952 | tf_op jit(solution)/shard_map/ppermute | solution.py:501
  18.9 2.9 %shard_map.123 = (f32[1,256]{1,0:T(1,128)S(1)}, f32[32,8,128]{2,1,0:T(8,128)S(1)}, f32[320,128]{1,0:T(8,128)S(1)}, f32[80,128]{1,0:T(8,128)S(1)}, f32[6,36,8,128...) custom-call(s32[3]{0:T(128)S(1)} %pad_add_fusion.1.info, ...), custom_call_target="tpu_custom_call", output_to_operand_aliasing={{2}: (3, {}), {6}: (4, {})} | custom-call | tf_op jit(solution)/shard_map/pallas_call | solution.py:502
  21.8 2.3 %collective-permute-start.7 = (f32[1,256]{1,0:T(1,128)S(1)}, f32[1,256]{1,0:T(1,128)S(1)}, u32[]{:S(2)}, u32[]{:S(2)}) collective-permute-start(f32[1,256]{1,0:T(1,128)S(1)} %get-tuple-element.39), channel_id=1, source_target_pairs={{0,8},{8,0},{16,24},{24,16},{1,9},{9,1},{17,25},{25,17},{2,10},{10... | collective-permute-start | bytes 3080 | tf_op jit(solution)/shard_map/ppermute | solution.py:546
  24.1 1.5 %collective-permute-done.7 = f32[1,256]{1,0:T(1,128)S(1)} collective-permute-done((f32[1,256]{1,0:T(1,128)S(1)}, f32[1,256]{1,0:T(1,128)S(1)}, u32[]{:S(2)}, u32[]{:S(2)}) %collective-permute-start.7) | collective-permute-done | bytes 1056 | tf_op jit(solution)/shard_map/ppermute | solution.py:546
  25.6 1.3 %collective-permute-start.8 = (f32[1,256]{1,0:T(1,128)S(1)}, f32[1,256]{1,0:T(1,128)S(1)}, u32[]{:S(2)}, u32[]{:S(2)}) collective-permute-start(f32[1,256]{1,0:T(1,128)S(1)} %add.62), channel_id=1, source_target_pairs={{0,16},{8,24},{16,0},{24,8},{1,17},{9,25},{17,1},{25,9},{2,18},{10... | collective-permute-start | bytes 3080 | tf_op jit(solution)/shard_map/ppermute | solution.py:546
  26.9 0.9 %shard_map.125 = (f32[320,128]{1,0:T(8,128)S(1)}, f32[80,128]{1,0:T(8,128)S(1)}, bf16[256,512]{1,0:T(8,128)(2,1)S(1)}) custom-call(s32[3]{0:T(128)S(1)} %pad_add_fusion.1.info, f32[20,8,128]{2,1,0:T(8,128)S(1)} %collective-permute-done.5.mine, f32[20,8,128]{2,1,0:T(8,128)S(1)} %collective-permute-done.6.theirs, f32[32,8,128]{2,1,0:T(8,128)S(1)} %bitcast.20, ...), custom_call_target="tpu_custom_call" | custom-call | bytes 4000000 | tf_op jit(solution)/shard_map/pallas_call | solution.py:519
  27.8 1.4 %collective-permute-done.8 = f32[1,256]{1,0:T(1,128)S(1)} collective-permute-done((f32[1,256]{1,0:T(1,128)S(1)}, f32[1,256]{1,0:T(1,128)S(1)}, u32[]{:S(2)}, u32[]{:S(2)}) %collective-permute-start.8) | collective-permute-done | bytes 1056 | tf_op jit(solution)/shard_map/ppermute | solution.py:546
  29.2 3.3 %shard_map.126 = (f32[1,256]{1,0:T(1,128)}, f32[8,4,8,128]{3,2,1,0:T(8,128)S(1)}, f32[32,8,128]{2,1,0:T(8,128)S(1)}, f32[320,128]{1,0:T(8,128)S(1)}, f32[80,128]{1,0:T(8,128)S(1)}) custom-call(s32[3]{0:T(128)S(1)} %pad_add_fusion.1.info, f32[1,256]{1,0:T(1,128)S(1)} %add.63.picked, ...), custom_call_target="tpu_custom_call", output_to_operand_aliasing={{3}: (3, {}), {4}: (4, {})} | custom-call | tf_op jit(solution)/shard_map/pallas_call | solution.py:549
  32.5 0.0 collective-permute-start.9
  32.5 1.2 %collective-permute-done.9 = f32[4,4,8,128]{3,2,1,0:T(8,128)S(1)} collective-permute-done((f32[4,4,8,128]{3,2,1,0:T(8,128)S(1)}, f32[4,4,8,128]{3,2,1,0:T(8,128)S(1)}, u32[]{:S(2)}, u32[]{:S(2)}) %collective-permute-start.9) | collective-permute-done | bytes 65568 | tf_op jit(solution)/shard_map/ppermute | solution.py:573
  33.7 2.1 %collective-permute-start.10 = (f32[2,4,8,128]{3,2,1,0:T(8,128)S(1)}, f32[2,4,8,128]{3,2,1,0:T(8,128)S(1)}, u32[]{:S(2)}, u32[]{:S(2)}) collective-permute-start(f32[2,4,8,128]{3,2,1,0:T(8,128)S(1)} %slice.35), channel_id=1, source_target_pairs={{0,2},{1,3},{2,0},{3,1},{4,6},{5,7},{6,4},{7,5},{8,10},{9,11},{10,... | collective-permute-start | bytes 98312 | tf_op jit(solution)/shard_map/ppermute | solution.py:573
  35.9 1.9 %collective-permute-done.10 = f32[2,4,8,128]{3,2,1,0:T(8,128)S(1)} collective-permute-done((f32[2,4,8,128]{3,2,1,0:T(8,128)S(1)}, f32[2,4,8,128]{3,2,1,0:T(8,128)S(1)}, u32[]{:S(2)}, u32[]{:S(2)}) %collective-permute-start.10) | collective-permute-done | bytes 32800 | tf_op jit(solution)/shard_map/ppermute | solution.py:573
  37.8 3.1 %collective-permute-start.11 = (f32[4,8,128]{2,1,0:T(8,128)S(1)}, f32[4,8,128]{2,1,0:T(8,128)S(1)}, u32[]{:S(2)}, u32[]{:S(2)}) collective-permute-start(f32[4,8,128]{2,1,0:T(8,128)S(1)} %get-tuple-element.54), channel_id=1, source_target_pairs={{0,4},{1,5},{2,6},{3,7},{4,0},{5,1},{6,2},{7,3},{8,12},{9,13},{10,... | collective-permute-start | bytes 49160 | tf_op jit(solution)/shard_map/ppermute | solution.py:574
  40.9 0.7 %shard_map.124 = f32[1,32,8,128]{3,2,1,0:T(8,128)} custom-call(f32[32,8,128]{2,1,0:T(8,128)S(1)} %get-tuple-element.38.value), custom_call_target="tpu_custom_call" | custom-call | bytes 4000000 | tf_op jit(solution)/shard_map/pallas_call | solution.py:533
  41.5 0.7 %shard_map.127 = f32[1,32,8,128]{3,2,1,0:T(8,128)} custom-call(f32[32,8,128]{2,1,0:T(8,128)S(1)} %get-tuple-element.47.value), custom_call_target="tpu_custom_call" | custom-call | bytes 4000000 | tf_op jit(solution)/shard_map/pallas_call | solution.py:533
  42.2 0.4 collective-permute-done.11.came
  42.6 0.6 %shard_map.128 = f32[4,8,128]{2,1,0:T(8,128)} custom-call(f32[4,8,128]{2,1,0:T(8,128)S(1)} %get-tuple-element.49.scale, f32[4,8,128]{2,1,0:T(8,128)S(1)} %get-tuple-element.50.prior, f32[4,8,128]{2,1,0:T(8,128)S(1)} %get-tuple-element.55.kept, f32[4,8,128]{2,1,0:T(8,128)S(1)} %collective-permute-done.11.came), custom_call_target="tpu_custom_call" | custom-call | tf_op jit(solution)/shard_map/pallas_call | solution.py:575
  (19 shorter events, 0.1 us)
Async XLA Ops:
  0.6 6.0 %collective-permute-start.2 = (f32[1,4,8,128]{3,2,1,0:T(8,128)}, f32[1,4,8,128]{3,2,1,0:T(8,128)S(1)}, u32[]{:S(2)}, u32[]{:S(2)}) collective-permute-start(f32[1,4,8,128]{3,2,1,0:T(8,128)} %bitcast.21), channel_id=1, source_target_pairs={{0,4},{1,5},{2,6},{3,7},{4,0},{5,1},{6,2},{7,3},{8,12},{9,13},{10,... | collective-permute-start | bytes 49160 | tf_op jit(solution)/shard_map/ppermute | solution.py:456
  4.7 3.9 %collective-permute-start = (f32[32,8,128]{2,1,0:T(8,128)}, f32[32,8,128]{2,1,0:T(8,128)S(1)}, u32[]{:S(2)}, u32[]{:S(2)}) collective-permute-start(f32[32,8,128]{2,1,0:T(8,128)} %bitcast.15), channel_id=1, source_target_pairs={{0,1},{1,0},{2,3},{3,2},{4,5},{5,4},{6,7},{7,6},{8,9},{9,8},{10,11... | collective-permute-start | bytes 393224 | tf_op jit(solution)/shard_map/ppermute | solution.py:449
  4.7 3.9 %collective-permute-start.1 = (f32[32,8,128]{2,1,0:T(8,128)}, f32[32,8,128]{2,1,0:T(8,128)S(1)}, u32[]{:S(2)}, u32[]{:S(2)}) collective-permute-start(f32[32,8,128]{2,1,0:T(8,128)} %bitcast.18), channel_id=1, source_target_pairs={{0,1},{1,0},{2,3},{3,2},{4,5},{5,4},{6,7},{7,6},{8,9},{9,8},{10,11... | collective-permute-start | bytes 393224 | tf_op jit(solution)/shard_map/ppermute | solution.py:450
  5.2 0.7 %copy-start.2 = (f32[4,8,128]{2,1,0:T(8,128)S(1)}, f32[4,8,128]{2,1,0:T(8,128)}, u32[]{:S(2)}) copy-start(f32[4,8,128]{2,1,0:T(8,128)} %own_model.1) | copy-start | bytes 49156
  5.2 3.4 %copy-start.8 = (s32[256,2]{0,1:T(2,128)S(1)}, s32[256,2]{0,1:T(2,128)}, u32[]{:S(2)}) copy-start(s32[256,2]{0,1:T(2,128)} %param.14) | copy-start | bytes 6148
  5.2 3.4 %copy-start.1 = (f32[1,32,8,128]{3,2,1,0:T(8,128)S(1)}, f32[1,32,8,128]{3,2,1,0:T(8,128)}, u32[]{:S(2)}) copy-start(f32[1,32,8,128]{3,2,1,0:T(8,128)} %param.17) | copy-start | bytes 393220
  5.3 3.4 %copy-start = (f32[1,32,8,128]{3,2,1,0:T(8,128)S(1)}, f32[1,32,8,128]{3,2,1,0:T(8,128)}, u32[]{:S(2)}) copy-start(f32[1,32,8,128]{3,2,1,0:T(8,128)} %param.16) | copy-start | bytes 393220
  6.7 3.9 %collective-permute-start.3 = (f32[2,4,8,128]{3,2,1,0:T(8,128)S(1)}, f32[2,4,8,128]{3,2,1,0:T(8,128)S(1)}, u32[]{:S(2)}, u32[]{:S(2)}) collective-permute-start(f32[2,4,8,128]{3,2,1,0:T(8,128)S(1)} %slice.32), channel_id=1, source_target_pairs={{0,2},{1,3},{2,0},{3,1},{4,6},{5,7},{6,4},{7,5},{8,10},{9,11},{10,... | collective-permute-start | bytes 98312 | tf_op jit(solution)/shard_map/ppermute | solution.py:456
  10.6 1.3 %collective-permute-start.4 = (f32[4,4,8,128]{3,2,1,0:T(8,128)S(1)}, f32[4,4,8,128]{3,2,1,0:T(8,128)S(1)}, u32[]{:S(2)}, u32[]{:S(2)}) collective-permute-start(f32[4,4,8,128]{3,2,1,0:T(8,128)S(1)} %slice.33), channel_id=1, source_target_pairs={{0,1},{1,0},{2,3},{3,2},{4,5},{5,4},{6,7},{7,6},{8,9},{9,8},{10,11... | collective-permute-start | bytes 196616 | tf_op jit(solution)/shard_map/ppermute | solution.py:456
  11.9 2.7 %copy-start.3 = (s32[4,8,128]{2,1,0:T(8,128)S(1)}, s32[4,8,128]{2,1,0:T(8,128)}, u32[]{:S(2)}) copy-start(s32[4,8,128]{2,1,0:T(8,128)} %labels.1) | copy-start | bytes 49156
  11.9 2.7 %copy-start.6 = (f32[4]{0:T(128)S(1)}, f32[4]{0:T(128)}, u32[]{:S(2)}) copy-start(f32[4]{0:T(128)} %means.1) | copy-start | bytes 52
  11.9 2.7 %copy-start.7 = (f32[4]{0:T(128)S(1)}, f32[4]{0:T(128)}, u32[]{:S(2)}) copy-start(f32[4]{0:T(128)} %variances.1) | copy-start | bytes 52
  12.7 4.9 %collective-permute-start.5 = (f32[20,8,128]{2,1,0:T(8,128)S(1)}, f32[20,8,128]{2,1,0:T(8,128)S(1)}, u32[]{:S(2)}, u32[]{:S(2)}) collective-permute-start(f32[20,8,128]{2,1,0:T(8,128)S(1)} %get-tuple-element.30), channel_id=1, source_target_pairs={{0,8},{1,25},{2,10},{3,27},{4,12},{5,29},{6,14},{7,31},{8,0},{9,17... | collective-permute-start | bytes 245768 | tf_op jit(solution)/shard_map/ppermute | solution.py:481
  14.6 0.7 %copy-start.4 = (f32[1,256]{1,0:T(1,128)S(1)}, f32[1,256]{1,0:T(1,128)}, u32[]{:S(2)}) copy-start(f32[1,256]{1,0:T(1,128)} %observed.1) | copy-start | bytes 3076
  14.6 0.7 %copy-start.5 = (s32[1,2]{1,0:T(1,128)S(1)}, s32[1,2]{1,0:T(1,128)}, u32[]{:S(2)}) copy-start(s32[1,2]{1,0:T(1,128)} %cells.1) | copy-start | bytes 28
  17.6 1.3 %collective-permute-start.6 = (f32[20,8,128]{2,1,0:T(8,128)S(1)}, f32[20,8,128]{2,1,0:T(8,128)S(1)}, u32[]{:S(2)}, u32[]{:S(2)}) collective-permute-start(f32[20,8,128]{2,1,0:T(8,128)S(1)} %broadcast_add_fusion), channel_id=1, source_target_pairs={{0,1},{1,0},{2,3},{3,2},{4,5},{5,4},{6,7},{7,6},{8,9},{9,8},{10,11... | collective-permute-start | bytes 245768 | tf_op jit(solution)/shard_map/ppermute | solution.py:501
  21.8 3.8 %collective-permute-start.7 = (f32[1,256]{1,0:T(1,128)S(1)}, f32[1,256]{1,0:T(1,128)S(1)}, u32[]{:S(2)}, u32[]{:S(2)}) collective-permute-start(f32[1,256]{1,0:T(1,128)S(1)} %get-tuple-element.39), channel_id=1, source_target_pairs={{0,8},{8,0},{16,24},{24,16},{1,9},{9,1},{17,25},{25,17},{2,10},{10... | collective-permute-start | bytes 3080 | tf_op jit(solution)/shard_map/ppermute | solution.py:546
  25.6 3.6 %collective-permute-start.8 = (f32[1,256]{1,0:T(1,128)S(1)}, f32[1,256]{1,0:T(1,128)S(1)}, u32[]{:S(2)}, u32[]{:S(2)}) collective-permute-start(f32[1,256]{1,0:T(1,128)S(1)} %add.62), channel_id=1, source_target_pairs={{0,16},{8,24},{16,0},{24,8},{1,17},{9,25},{17,1},{25,9},{2,18},{10... | collective-permute-start | bytes 3080 | tf_op jit(solution)/shard_map/ppermute | solution.py:546
  32.5 1.3 %collective-permute-start.9 = (f32[4,4,8,128]{3,2,1,0:T(8,128)S(1)}, f32[4,4,8,128]{3,2,1,0:T(8,128)S(1)}, u32[]{:S(2)}, u32[]{:S(2)}) collective-permute-start(f32[4,4,8,128]{3,2,1,0:T(8,128)S(1)} %slice.27), channel_id=1, source_target_pairs={{0,1},{1,0},{2,3},{3,2},{4,5},{5,4},{6,7},{7,6},{8,9},{9,8},{10,11... | collective-permute-start | bytes 196616 | tf_op jit(solution)/shard_map/ppermute | solution.py:573
  33.7 4.0 %collective-permute-start.10 = (f32[2,4,8,128]{3,2,1,0:T(8,128)S(1)}, f32[2,4,8,128]{3,2,1,0:T(8,128)S(1)}, u32[]{:S(2)}, u32[]{:S(2)}) collective-permute-start(f32[2,4,8,128]{3,2,1,0:T(8,128)S(1)} %slice.35), channel_id=1, source_target_pairs={{0,2},{1,3},{2,0},{3,1},{4,6},{5,7},{6,4},{7,5},{8,10},{9,11},{10,... | collective-permute-start | bytes 98312 | tf_op jit(solution)/shard_map/ppermute | solution.py:573
  37.8 4.8 %collective-permute-start.11 = (f32[4,8,128]{2,1,0:T(8,128)S(1)}, f32[4,8,128]{2,1,0:T(8,128)S(1)}, u32[]{:S(2)}, u32[]{:S(2)}) collective-permute-start(f32[4,8,128]{2,1,0:T(8,128)S(1)} %get-tuple-element.54), channel_id=1, source_target_pairs={{0,4},{1,5},{2,6},{3,7},{4,0},{5,1},{6,2},{7,3},{8,12},{9,13},{10,... | collective-permute-start | bytes 49160 | tf_op jit(solution)/shard_map/ppermute | solution.py:574

commit v3 on v2

--- a/solution.py
+++ b/solution.py
@@ -17,6 +17,7 @@
 SMALLNESS = 1.0
 
 GROUPS = 4
+EDGE = SWEEPS + 1
 SLOT = 32
 HALF = SLOT // 2
 PACK_AT = 1
@@ -31,6 +32,10 @@
 PARAMS = pltpu.CompilerParams(vmem_limit_bytes=24 * 1024 * 1024)
 
 
+def facing():
+    return 1 - (lax.axis_index("tile") + lax.axis_index("src")) % 2
+
+
 def xor_pairs(count, bit):
     return [(i, i ^ bit) for i in range(count)]
 
@@ -67,9 +72,16 @@
     lax.fori_loop(0, count, step, 0, unroll=unroll)
 
 
-def swap_halves(values):
-    upper = lane_of(values.shape) % SLOT >= HALF
-    return jnp.where(upper, turn(values, HALF), turn(values, -HALF))
+def window(side, offset, shape):
+    slot = ((lane_of(shape) - offset) & 127) % SLOT
+    low = full(HALF - EDGE + EDGE * side, shape)
+    return (slot >= low) & (slot < low + EDGE)
+
+
+def joined(side, first, second, third):
+    shape = first.shape
+    out = jnp.where(window(side, 0, shape), first, turn(second, EDGE))
+    return jnp.where(window(side, -EDGE, shape), turn(third, -EDGE), out)
 
 
 def merge(pieces):
@@ -90,46 +102,59 @@
     return merge([jnp.take_along_axis(row_of(k + per * g), index, axis=1) for g in range(GROUPS)])
 
 
-def upper_is(right, shape):
-    return (lane_of(shape) % SLOT) // HALF == full(right, shape)
-
-
-def pack_fields_kernel(info, own_v, own_a, other_v, other_a, passed, payload, passed_on):
+def message_rows(per):
+    return per + per // 2 + -(-(per // 2) // 3)
+
+
+def model_place(k, per):
+    if k < per // 2:
+        return per + k, -EDGE
+    k -= per // 2
+    return per + per // 2 + k // 3, (0, EDGE, -EDGE)[k % 3]
+
+
+def pack_fields_kernel(own_v, own_a, other_v, other_a, passed, payload, passed_on):
     del passed, passed_on
     per = own_v.shape[0] // GROUPS
     shape = own_v.shape[1:]
-    mask = upper_is(info[1], shape)
-
-    def body(k):
-        for n, (own, other) in enumerate(((own_v, other_v), (own_a, other_a))):
-            far = swap_halves(edges(lambda y: other[y], k, per, shape))
-            payload[n * per + k] = jnp.where(mask, edges(lambda y: own[y], k, per, shape), far)
-
-    each(per, body, 4)
-
-
-def pack_model_kernel(order, info, gathered, part, payload, model):
-    del part
+    side = facing()
+
+    def part(ref, k):
+        return edges(lambda y: ref[y], k, per, shape)
+
+    def body(h):
+        for k in (2 * h, 2 * h + 1):
+            payload[k] = joined(side, part(own_v, k), part(other_v, k), part(own_a, k))
+        first, second = part(other_a, 2 * h), part(other_a, 2 * h + 1)
+        payload[per + h] = jnp.where(window(side, 0, shape), first, turn(second, EDGE))
+
+    each(per // 2, body, 2)
+
+
+def pack_model_kernel(order, gathered, part, payload, model):
     peers, rows_own = gathered.shape[:2]
     per = model.shape[0] // GROUPS
     shape = gathered.shape[2:]
-    mask = upper_is(info[1], shape)
+    side = facing()
     for i in range(peers):
         j = sum(((i >> n) & 1) << bit for n, bit in enumerate(order))
-        model[pl.ds((info[0] ^ j) * rows_own, rows_own)] = gathered[i]
-    for k in range(per // 2):
-        first, second = edges(lambda y: model[y], k, per, shape), edges(lambda y: model[y], k + per // 2, per, shape)
-        payload[2 * per + k] = jnp.where(mask, first, swap_halves(second))
+        model[pl.ds((lax.axis_index("src") ^ j) * rows_own, rows_own)] = gathered[i]
+    packed = [edges(lambda y: model[y], k, per, shape) for k in range(per)]
+    half = per // 2
+    for h in range(half):
+        payload[per + h] = jnp.where(window(side, -EDGE, shape), turn(packed[h], -EDGE), part[per + h])
+    for n, k in enumerate(range(half, per, 3)):
+        payload[per + half + n] = joined(side, *[packed[min(k + m, per - 1)] for m in range(3)])
 
 
 def own_field_kernel(
-    total_x, info, cells, means, variances, labels, own_model, model, warm, observed,
+    total_x, cells, means, variances, labels, own_model, model, warm, observed,
     scale, prior, main, main_2, b_m, b_r, measured, nothing,
 ):
     rows, depth, width = warm.shape
     shape = (depth, width)
     per = rows // GROUPS
-    first_col = info[2]
+    first_col = lax.axis_index("tile") * width
     nothing[...] = jnp.zeros(nothing.shape, F32)
     measured[...] = jnp.where(full(first_col, observed.shape) == 0, observed[...], 0.0)
     m = own_model[...]
@@ -170,28 +195,34 @@
         b_r[k] = b_r[k] + jnp.where(at_slot & at_depth, sign, 0.0)
 
 
-def own_adjoint_kernel(info, mine, theirs, warm, spots, main, rim, hit_x):
+def own_adjoint_kernel(mine, theirs, warm, spots, main, rim, hit_x):
     rows, depth, width = warm.shape
     per = rows // GROUPS
-    mask = ~upper_is(info[1], (depth, width))
-
-    def body(k):
-        for g in range(GROUPS):
-            put_row(main, k + (per + 2) * g, turn(warm[k + per * g], SLOT * g + HALF))
-        put_row(rim, k, jnp.where(mask, mine[per + k], swap_halves(theirs[per + k])))
-
-    each(per, body, 2)
+    mask = window(1 - facing(), 0, (depth, width))
+
+    def body(h):
+        for n in range(2):
+            k = 2 * h + n
+            for g in range(GROUPS):
+                put_row(main, k + (per + 2) * g, turn(warm[k + per * g], SLOT * g + HALF))
+            far = turn(theirs[per + h], -EDGE * n)
+            put_row(rim, k, jnp.where(mask, turn(mine[k], EDGE), far))
+
+    each(per // 2, body, 1)
     clear_ends(main, per)
     at = depth_of((2 * width, spots.shape[1]))
     slot = at % SLOT
-    at = info[2] + jnp.where(at < width, at, HALF - 1 - slot + jnp.where(slot < HALF, width, 0))
+    at = lax.axis_index("tile") * width + jnp.where(at < width, at, HALF - 1 - slot + jnp.where(slot < HALF, width, 0))
     hit_x[...] = jnp.where(at == spots[0:1, :], 1.0, 0.0).astype(BF16)
 
 
-def save_kernel(value, out, sem):
-    copy = pltpu.make_async_copy(value, out.at[0], sem)
-    copy.start()
-    copy.wait()
+def save_kernel(field, adjoint, misfit, field_out, adjoint_out, misfit_out, sems):
+    pairs = ((field, field_out.at[0]), (adjoint, adjoint_out.at[0]), (misfit, misfit_out))
+    copies = [pltpu.make_async_copy(a, b, sems.at[n]) for n, (a, b) in enumerate(pairs)]
+    for copy in copies:
+        copy.start()
+    for copy in copies:
+        copy.wait()
 
 
 def at_row(ref, y, shift=0):
@@ -205,22 +236,23 @@
     ref[pl.ds(start, DEPTH), :] = values
 
 
-def neighbours(main, rim, k, per):
-    packed = at_row(rim, k)
-    shape = packed.shape
-    lane = lane_of(shape)
+def row_set(main, rim, k, per):
+    return [at_row(main, g * (per + 2) + k) for g in range(GROUPS)] + [at_row(rim, k)]
+
+
+def beside(own):
+    packed = own[GROUPS]
+    lane = lane_of(packed.shape)
     slot = lane % SLOT
-    own = [at_row(main, g * (per + 2) + k) for g in range(GROUPS)]
     before, after = [], []
     for g in range(GROUPS):
         last = SLOT * g + HALF - 1
         after.append(jnp.where(lane == last, packed, turn(own[g], -1)))
         before.append(jnp.where(lane == last + 1, packed, turn(own[g], 1)))
-    inner = merge(own)
+    inner = merge(own[:GROUPS])
     before.append(jnp.where(slot == HALF - 1, inner, turn(packed, -1)))
     after.append(jnp.where(slot == HALF, inner, turn(packed, 1)))
-    own.append(packed)
-    return own, before, after
+    return before, after
 
 
 def wrap(main, rim, per):
@@ -239,24 +271,25 @@
 
 def sweep(old, new, face_m, face_r, b_m, b_r):
     per = b_r.shape[0]
-    rows = per * GROUPS
-    main, rim = old
     main_new, rim_new = new
+    above, own = row_set(*old, -1, per), row_set(*old, 0, per)
+    face_above = [face_m[2, (per + 1) * g] for g in range(GROUPS)] + [face_r[2, 0]]
     for k in range(per):
-        own, before, after = neighbours(main, rim, k, per)
+        below = row_set(*old, k + 1, per)
+        before, after = beside(own)
         for g in range(GROUPS + 1):
-            n = min(g, GROUPS) // GROUPS
+            n = g // GROUPS
             field, face, b = (old[n], (face_m, face_r)[n], (b_m, b_r)[n])
             y = k if n else k + per * g
             r = k if n else k + (per + 2) * g
             c = k if n else k + (per + 1) * g
+            fy, fz = face[2, c + 1], face[3, c + 1]
             total = b[y] + face[0, c + 1] * after[g] + face[1, c + 1] * before[g]
-            total = total + (face[3, c + 1] * at_row(field, r, 1) + face[4, c + 1] * at_row(field, r, -1))
-            if n or y + 1 < rows:
-                total = total + face[2, c + 1] * at_row(field, r + 1)
-            if n or y > 0:
-                total = total + face[2, c] * at_row(field, r - 1)
+            total = total + (fz * up_depth(own[g]) + down_depth(fz * own[g]))
+            total = total + (fy * below[g] + face_above[g] * above[g])
+            face_above[g] = fy
             put_row(new[n], r, total * face[5, c + 1])
+        above, own = own, below
     wrap(main_new, rim_new, per)
 
 
@@ -294,7 +327,8 @@
     group = lane_of(shape) // SLOT
     bottom = depth_of(shape) == shape[0] - 1
     for k in range(per):
-        own, before, after = neighbours(main, rim, k, per)
+        own = row_set(main, rim, k, per)
+        before, after = beside(own)
         for g in range(GROUPS + 1):
             n = g // GROUPS
             field, face = ((main, rim)[n], (face_m, face_r)[n])
@@ -330,21 +364,21 @@
 
 
 def field_kernel(
-    total_x, info, mine, theirs, main_in, sigma_in, b_m, b_r, spots, measured,
+    total_x, mine, theirs, main_in, sigma_in, b_m, b_r, spots, measured,
     picked, plain, main, rim, face_m, face_r, main_2, rim_2,
 ):
     del main_in, sigma_in
     rows, depth, width = plain.shape
     shape = (depth, width)
     per = rows // GROUPS
-    right, first_col = info[1], info[2]
-    mask = ~upper_is(right, shape)
+    first_col = lax.axis_index("tile") * width
+    mask = window(1 - facing(), 0, shape)
+    filled = mask | window(facing(), 0, shape)
     for k in range(per):
-        put_row(rim, k, jnp.where(mask, mine[k], swap_halves(theirs[k])))
-    for k in range(per // 2):
-        near, far = mine[2 * per + k], theirs[2 * per + k]
-        put_row(rim_2, k, jnp.exp(jnp.where(mask, near, far)))
-        put_row(rim_2, k + per // 2, jnp.exp(swap_halves(jnp.where(mask, far, near))))
+        put_row(rim, k, jnp.where(mask, mine[k], turn(theirs[k], -EDGE)))
+        row, offset = model_place(k, per)
+        beyond = turn(jnp.where(window(1 - facing(), offset, shape), mine[row], theirs[row]), -offset)
+        put_row(rim_2, k, jnp.exp(jnp.where(filled, beyond, 0.0)))
     wrap(main_2, rim_2, per)
     coefficients(total_x, first_col, main_2, rim_2, face_m, face_r)
     relax((main, rim), (main_2, rim_2), face_m, face_r, b_m, b_r)
@@ -362,17 +396,17 @@
 
 
 def adjoint_kernel(
-    total_x, places, info, picked, spots, main_in, rim_in, hit_x, main_v, rim_v, face_m, face_r,
-    misfit_out, terms, plain, main, rim, main_2, rim_2, b_m, b_r,
+    total_x, places, picked, spots, main_in, rim_in, hit_x, main_v, rim_v, face_m, face_r,
+    terms, plain, main, rim, main_2, rim_2, b_m, b_r,
 ):
     del main_in, rim_in
     rows, depth, width = plain.shape
     shape = (depth, width)
     per = rows // GROUPS
-    me, first_col = info[0], info[2]
+    me = lax.axis_index("src")
+    first_col = lax.axis_index("tile") * width
     count = spots.shape[1]
     misfit = picked[...]
-    misfit_out[...] = misfit
     weights = jnp.concatenate([misfit, -misfit], axis=1)
     hit_line = depth_of((rows * depth, count)) == spots[1:2, :]
     flat = jnp.zeros((rows * depth, 2 * width), F32)
@@ -390,8 +424,9 @@
     rows_own = terms.shape[1]
     bottom = depth_of(shape) == depth - 1
     for k in range(per):
-        f_own, f_before, f_after = neighbours(main_v, rim_v, k, per)
-        a_own, a_before, a_after = neighbours(main, rim, k, per)
+        f_own, a_own = row_set(main_v, rim_v, k, per), row_set(main, rim, k, per)
+        f_before, f_after = beside(f_own)
+        a_before, a_after = beside(a_own)
         for g in range(GROUPS):
             y, r = k + per * g, k + (per + 2) * g
             col = first_col + columns(g, shape)
@@ -436,8 +471,6 @@
     receivers = receiver_cells.shape[0]
     bits = [1 << n for n in range(peers.bit_length() - 1)]
     levels = list(range(len(bits)))
-    right = 1 - (tile + src) % 2
-    info = jnp.stack([src, right, tile * width]).astype(jnp.int32)
     spots = receiver_cells.T.reshape(1, 2 * receivers)
     spots = jnp.concatenate([spots % total_x, spots // total_x], axis=0)
     spots = jnp.pad(spots, ((0, 6), (0, 0)), constant_values=-1)
@@ -457,22 +490,22 @@
         if n == PACK_AT:
             payload, gathered = pl.pallas_call(
                 pack_fields_kernel,
-                out_shape=(shaped(5 * per // 2, depth, width), shaped(*gathered.shape)),
-                in_specs=[SMEM] + [VMEM] * 5,
+                out_shape=(shaped(message_rows(per), depth, width), shaped(*gathered.shape)),
+                in_specs=[VMEM] * 5,
                 out_specs=(VMEM, VMEM),
-                input_output_aliases={5: 1},
+                input_output_aliases={4: 1},
                 cost_estimate=BESIDE,
                 compiler_params=PARAMS,
-            )(info, start_v, start_a, other_v, other_a, gathered)
+            )(start_v, start_a, other_v, other_a, gathered)
         gathered = lax.dynamic_update_slice(gathered, came, (1 << n, 0, 0, 0))
     payload, model = pl.pallas_call(
         functools.partial(pack_model_kernel, order),
         out_shape=(shaped(*payload.shape), shaped(rows, depth, width)),
-        in_specs=[SMEM, VMEM, VMEM],
+        in_specs=[VMEM, VMEM],
         out_specs=(VMEM, VMEM),
-        input_output_aliases={2: 0},
+        input_output_aliases={1: 0},
         compiler_params=PARAMS,
-    )(info, gathered, payload)
+    )(gathered, payload)
     pairs = []
     for t in range(tiles):
         for s in range(peers):
@@ -490,12 +523,12 @@
             shaped(*observed.shape),
             shaped(1, depth, width),
         ),
-        in_specs=[SMEM] * 4 + [VMEM] * 5,
+        in_specs=[SMEM] * 3 + [VMEM] * 5,
         out_specs=(VMEM,) * 8,
         cost_estimate=BESIDE,
         compiler_params=PARAMS,
     )(
-        info, source_cells, cluster_means, cluster_vars, cluster_labels, log_conductivity,
+        source_cells, cluster_means, cluster_vars, cluster_labels, log_conductivity,
         model, start_v, observed,
     )
     theirs = lax.ppermute(mine + nothing, "src", xor_pairs(peers, 1))
@@ -510,12 +543,12 @@
             shaped(6, per + 1, depth, width),
             shaped(*main_shape),
         ),
-        in_specs=[SMEM] + [VMEM] * 8,
+        in_specs=[VMEM] * 8,
         out_specs=(VMEM,) * 7,
-        input_output_aliases={3: 2, 4: 6},
+        input_output_aliases={2: 2, 3: 6},
         scratch_shapes=[pltpu.VMEM(rim_shape, F32)],
         compiler_params=PARAMS,
-    )(info, mine, theirs, main_v, sigma, b_m, b_r, spots, measured)
+    )(mine, theirs, main_v, sigma, b_m, b_r, spots, measured)
     main_a, rim_a, hit_x = pl.pallas_call(
         own_adjoint_kernel,
         out_shape=(
@@ -523,41 +556,28 @@
             shaped(*rim_shape),
             jax.ShapeDtypeStruct((2 * width, 2 * receivers), BF16),
         ),
-        in_specs=[SMEM] + [VMEM] * 4,
+        in_specs=[VMEM] * 4,
         out_specs=(VMEM,) * 3,
         cost_estimate=BESIDE,
         compiler_params=PARAMS,
-    )(info, mine, theirs, start_a, spots)
-
-    def saved(value, shape):
-        return pl.pallas_call(
-            save_kernel,
-            out_shape=shaped(*shape),
-            in_specs=[VMEM],
-            out_specs=HBM,
-            scratch_shapes=[pltpu.SemaphoreType.DMA],
-            cost_estimate=BESIDE,
-            compiler_params=PARAMS,
-        )(value)
-
-    field = saved(plain_v, warm_potential.shape)
+    )(mine, theirs, start_a, spots)
+
     step = 1
     while step < tiles:
         picked = picked + lax.ppermute(picked, "tile", xor_pairs(tiles, step))
         step *= 2
 
-    misfit, terms, plain_a, _, _ = pl.pallas_call(
+    terms, plain_a, _, _ = pl.pallas_call(
         functools.partial(adjoint_kernel, total_x, levels),
         out_shape=(
-            shaped(*observed.shape),
             shaped(peers, rows_own, depth, width),
             shaped(rows, depth, width),
             shaped(*main_shape),
             shaped(*rim_shape),
         ),
-        in_specs=[SMEM] + [VMEM] * 9,
-        out_specs=(VMEM,) * 5,
-        input_output_aliases={3: 3, 4: 4},
+        in_specs=[VMEM] * 9,
+        out_specs=(VMEM,) * 4,
+        input_output_aliases={2: 2, 3: 3},
         scratch_shapes=[
             pltpu.VMEM(main_shape, F32),
             pltpu.VMEM(rim_shape, F32),
@@ -565,8 +585,16 @@
             pltpu.VMEM((per, depth, width), F32),
         ],
         compiler_params=PARAMS,
-    )(info, picked, spots, main_a, rim_a, hit_x, main_v, rim_v, face_m, face_r)
-    adjoint = saved(plain_a, warm_adjoint.shape)
+    )(picked, spots, main_a, rim_a, hit_x, main_v, rim_v, face_m, face_r)
+    field, adjoint, misfit = pl.pallas_call(
+        save_kernel,
+        out_shape=(shaped(*warm_potential.shape), shaped(*warm_adjoint.shape), shaped(*observed.shape)),
+        in_specs=[VMEM] * 3,
+        out_specs=(HBM,) * 3,
+        scratch_shapes=[pltpu.SemaphoreType.DMA((3,))],
+        cost_estimate=BESIDE,
+        compiler_params=PARAMS,
+    )(plain_v, plain_a, picked)
 
     for level in levels[:-1]:
         keep = terms.shape[0] // 2

time: 43.5 us -> 40.8 us (0.938)
  Pallas kernels: 11.6 us -> 7.73 us
  local copies, waits for them, and re-layouts: 1.43 us -> 2.34 us
    pallas_call x3 -> x2, Pallas kernels: 2.27 us -> 1.12 us  [the longest x1 0.72 us: on_device(): pl.pallas_call(save_kernel, out_shape=(shaped(*warm_potential.shape), sha...]
    pallas_call x1, Pallas kernels: 3.25 us -> 2.42 us  [on_device(): pl.pallas_call(functools.partial(adjoint_kernel, total_x, levels), out_sh...]
    pallas_call x1, Pallas kernels: 2.87 us -> 2.09 us  [on_device(): pl.pallas_call(functools.partial(field_kernel, total_x), out_shape=(shape...]
    pad x1, local copies, waits for them, and re-layouts: 0.01 us -> 0.73 us  [on_device(): jnp.pad(own, ((0, peers - 1), (0, 0), (0, 0), (0, 0)))]
    ppermute x1, waiting for transfers between devices: 0.37 us -> 0.99 us  [on_device(): came = lax.ppermute(terms[1], 'src', xor_pairs(peers, bits[-1]))]
    pallas_call x1, Pallas kernels: 0.9 us -> 0.36 us  [on_device(): pl.pallas_call(own_adjoint_kernel, out_shape=(shaped(*main_shape), shaped...]
    pallas_call x1, Pallas kernels: 0.71 us -> 0.18 us  [on_device(): pl.pallas_call(functools.partial(pack_model_kernel, order), out_shape=(sh...]
    ppermute x1, waiting for transfers between devices: 1.32 us -> 0.81 us  [on_device(): mine = lax.ppermute(payload, ('tile', 'src'), pairs)]
  transfers between devices with their start and end apart: 12 -> 12, of which waited for: 10 -> 10; matrix products, arithmetic and copies ran while one was open for 0% -> 2% of each run, Pallas kernels for 10% -> 6%
where the time goes in v3:
time: 40.8 us; the launch traced here: 40.5 us
  starting transfers between devices  17.8 us (44%)
  waiting for transfers between devices  11.8 us (29%)
  Pallas kernels  7.73 us (19%)
  local copies, waits for them, and re-layouts  2.34 us (6%)
  between operations  0.83 us (2%)
    ppermute x3, starting transfers between devices, on_device(): came = lax.ppermute(sent, 'src', xor_pairs(peers, bits[level]))  6.14 us
    ppermute x2, starting transfers between devices, on_device(): picked = picked + lax.ppermute(picked, 'tile', xor_pairs(tiles, step))  3.82 us
    ppermute x2, waiting for transfers between devices, on_device(): picked = picked + lax.ppermute(picked, 'tile', xor_pairs(tiles, step))  3.18 us
    ppermute x2, waiting for transfers between devices, on_device(): lax.ppermute(terms[keep:], 'src', xor_pairs(peers, bits[level]))  3.14 us
    ppermute x1, starting transfers between devices, on_device(): came = lax.ppermute(terms[1], 'src', xor_pairs(peers, bits[-1]))  3.11 us
    ppermute x3, waiting for transfers between devices, on_device(): came = lax.ppermute(sent, 'src', xor_pairs(peers, bits[level]))  2.59 us
    pallas_call x1, Pallas kernels, on_device(): pl.pallas_call(functools.partial(adjoint_kernel, total_x, levels), out_sh...  2.42 us
    ppermute x2, starting transfers between devices, on_device(): lax.ppermute(terms[keep:], 'src', xor_pairs(peers, bits[level]))  2.18 us
  transfers between devices with their start and end apart: 12, of which 10 were waited for; matrix products, arithmetic and copies ran while one was open for 2% of the time, Pallas kernels for 6%

profile of v3, /device:TPU:0, one launch (start us, length us, event | category | flops | bytes accessed | tf_op | source)
XLA Modules:
  0.0 40.5 jit_solution(1480915404889065806)
XLA Ops:
  0.6 0.0 copy-start
  0.6 4.1 %collective-permute-start.2 = (f32[1,4,8,128]{3,2,1,0:T(8,128)}, f32[1,4,8,128]{3,2,1,0:T(8,128)S(1)}, u32[]{:S(2)}, u32[]{:S(2)}) collective-permute-start(f32[1,4,8,128]{3,2,1,0:T(8,128)} %bitcast.18), channel_id=1, source_target_pairs={{0,4},{1,5},{2,6},{3,7},{4,0},{5,1},{6,2},{7,3},{8,12},{9,13},{10,... | collective-permute-start | bytes 49160 | tf_op jit(solution)/shard_map/ppermute | solution.py:489
  4.7 0.0 collective-permute-start
  4.7 0.5 %collective-permute-start.1 = (f32[32,8,128]{2,1,0:T(8,128)}, f32[32,8,128]{2,1,0:T(8,128)S(1)}, u32[]{:S(2)}, u32[]{:S(2)}) collective-permute-start(f32[32,8,128]{2,1,0:T(8,128)} %bitcast.15), channel_id=1, source_target_pairs={{0,1},{1,0},{2,3},{3,2},{4,5},{5,4},{6,7},{7,6},{8,9},{9,8},{10,11... | collective-permute-start | bytes 393224 | tf_op jit(solution)/shard_map/ppermute | solution.py:483
  5.3 0.7 %pad.8 = f32[8,4,8,128]{3,2,1,0:T(8,128)S(1)} pad(f32[1,4,8,128]{3,2,1,0:T(8,128)} %bitcast.19, f32[]{:T(128)} %constant.28.clone.1), padding=0_7x0_0x0_0x0_0 | pad | bytes 147460 | tf_op jit(solution)/shard_map/jit(_pad)/pad | solution.py:486
  6.0 0.7 %collective-permute-done.2 = f32[1,4,8,128]{3,2,1,0:T(8,128)S(1)} collective-permute-done((f32[1,4,8,128]{3,2,1,0:T(8,128)}, f32[1,4,8,128]{3,2,1,0:T(8,128)S(1)}, u32[]{:S(2)}, u32[]{:S(2)}) %collective-permute-start.2) | collective-permute-done | bytes 16416 | tf_op jit(solution)/shard_map/ppermute | solution.py:489
  6.7 0.0 copy-start.9
  6.7 2.0 %collective-permute-start.3 = (f32[2,4,8,128]{3,2,1,0:T(8,128)S(1)}, f32[2,4,8,128]{3,2,1,0:T(8,128)S(1)}, u32[]{:S(2)}, u32[]{:S(2)}) collective-permute-start(f32[2,4,8,128]{3,2,1,0:T(8,128)S(1)} %slice.32), channel_id=1, source_target_pairs={{0,2},{1,3},{2,0},{3,1},{4,6},{5,7},{6,4},{7,5},{8,10},{9,11},{10,... | collective-permute-start | bytes 98312 | tf_op jit(solution)/shard_map/ppermute | solution.py:489
  8.7 0.0 copy-done.9
  8.7 0.0 collective-permute-done.other_v
  8.7 0.0 collective-permute-done.1.other_a
  8.7 0.0 copy-done
  8.7 0.0 copy-start.1
  8.7 0.9 %copy-done.1 = f32[1,32,8,128]{3,2,1,0:T(8,128)S(1)} copy-done((f32[1,32,8,128]{3,2,1,0:T(8,128)S(1)}, f32[1,32,8,128]{3,2,1,0:T(8,128)}, u32[]{:S(2)}) %copy-start.1) | copy-done | bytes 131096
  9.6 0.4 shard_map.120
  10.0 0.7 %collective-permute-done.3 = f32[2,4,8,128]{3,2,1,0:T(8,128)S(1)} collective-permute-done((f32[2,4,8,128]{3,2,1,0:T(8,128)S(1)}, f32[2,4,8,128]{3,2,1,0:T(8,128)S(1)}, u32[]{:S(2)}, u32[]{:S(2)}) %collective-permute-start.3) | collective-permute-done | bytes 32800 | tf_op jit(solution)/shard_map/ppermute | solution.py:489
  10.7 0.1 collective-permute-start.4
  10.8 1.2 %collective-permute-done.4 = f32[4,4,8,128]{3,2,1,0:T(8,128)S(1)} collective-permute-done((f32[4,4,8,128]{3,2,1,0:T(8,128)S(1)}, f32[4,4,8,128]{3,2,1,0:T(8,128)S(1)}, u32[]{:S(2)}, u32[]{:S(2)}) %collective-permute-start.4) | collective-permute-done | bytes 65568 | tf_op jit(solution)/shard_map/ppermute | solution.py:489
  12.0 0.0 copy-start.3
  12.0 0.0 copy-start.4
  12.0 0.0 copy-start.7
  12.0 0.0 copy-start.8
  12.0 0.2 shard_map.121
  12.2 1.9 %collective-permute-start.5 = (f32[14,8,128]{2,1,0:T(8,128)S(1)}, f32[14,8,128]{2,1,0:T(8,128)S(1)}, u32[]{:S(2)}, u32[]{:S(2)}) collective-permute-start(f32[14,8,128]{2,1,0:T(8,128)S(1)} %get-tuple-element.32), channel_id=1, source_target_pairs={{0,8},{1,25},{2,10},{3,27},{4,12},{5,29},{6,14},{7,31},{8,0},{9,17... | collective-permute-start | bytes 172040 | tf_op jit(solution)/shard_map/ppermute | solution.py:514
  14.1 0.0 copy-start.5
  14.2 0.0 copy-start.6
  14.2 0.0 copy-done.3
  14.2 0.0 copy-done.4
  14.2 0.0 copy-done.7
  14.2 0.0 copy-done.8
  14.2 0.6 %copy-done.5 = f32[1,256]{1,0:T(1,128)S(1)} copy-done((f32[1,256]{1,0:T(1,128)S(1)}, f32[1,256]{1,0:T(1,128)}, u32[]{:S(2)}) %copy-start.5) | copy-done | bytes 1048
  14.8 0.0 copy-done.6
  14.8 1.0 %shard_map.122 = (f32[4,8,128]{2,1,0:T(8,128)S(1)}, f32[4,8,128]{2,1,0:T(8,128)S(1)}, f32[320,128]{1,0:T(8,128)S(1)}, f32[320,128]{1,0:T(8,128)S(1)}, f32[32,8,1...) custom-call(s32[1,2]{1,0:T(1,128)S(1)} %copy-done.6, ...), custom_call_target="tpu_custom_call" | custom-call | bytes 4000000 | tf_op jit(solution)/shard_map/pallas_call | solution.py:516
  15.8 0.8 %collective-permute-done.5.mine = f32[14,8,128]{2,1,0:T(8,128)S(1)} collective-permute-done((f32[14,8,128]{2,1,0:T(8,128)S(1)}, f32[14,8,128]{2,1,0:T(8,128)S(1)}, u32[]{:S(2)}, u32[]{:S(2)}) %collective-permute-start.5) | collective-permute-done | bytes 57376 | tf_op jit(solution)/shard_map/ppermute | solution.py:514
  16.6 0.1 collective-permute-start.6
  16.7 1.1 %collective-permute-done.6.theirs = f32[14,8,128]{2,1,0:T(8,128)S(1)} collective-permute-done((f32[14,8,128]{2,1,0:T(8,128)S(1)}, f32[14,8,128]{2,1,0:T(8,128)S(1)}, u32[]{:S(2)}, u32[]{:S(2)}) %collective-permute-start.6) | collective-permute-done | bytes 57376 | tf_op jit(solution)/shard_map/ppermute | solution.py:534
  17.9 0.0 copy-start.2
  17.9 2.1 %shard_map.123 = (f32[1,256]{1,0:T(1,128)S(1)}, f32[32,8,128]{2,1,0:T(8,128)S(1)}, f32[320,128]{1,0:T(8,128)S(1)}, f32[80,128]{1,0:T(8,128)S(1)}, f32[6,36,8,128...) custom-call(f32[14,8,128]{2,1,0:T(8,128)S(1)} %collective-permute-do, ...), custom_call_target="tpu_custom_call", output_to_operand_aliasing={{2}: (2, {}), {6}: (3, {})} | custom-call | tf_op jit(solution)/shard_map/pallas_call | solution.py:535
  19.9 2.2 %collective-permute-start.7 = (f32[1,256]{1,0:T(1,128)S(1)}, f32[1,256]{1,0:T(1,128)S(1)}, u32[]{:S(2)}, u32[]{:S(2)}) collective-permute-start(f32[1,256]{1,0:T(1,128)S(1)} %get-tuple-element.41), channel_id=1, source_target_pairs={{0,8},{8,0},{16,24},{24,16},{1,9},{9,1},{17,25},{25,17},{2,10},{10... | collective-permute-start | bytes 3080 | tf_op jit(solution)/shard_map/ppermute | solution.py:567
  22.2 1.5 %collective-permute-done.7 = f32[1,256]{1,0:T(1,128)S(1)} collective-permute-done((f32[1,256]{1,0:T(1,128)S(1)}, f32[1,256]{1,0:T(1,128)S(1)}, u32[]{:S(2)}, u32[]{:S(2)}) %collective-permute-start.7) | collective-permute-done | bytes 1056 | tf_op jit(solution)/shard_map/ppermute | solution.py:567
  23.7 1.6 %collective-permute-start.8 = (f32[1,256]{1,0:T(1,128)S(1)}, f32[1,256]{1,0:T(1,128)S(1)}, u32[]{:S(2)}, u32[]{:S(2)}) collective-permute-start(f32[1,256]{1,0:T(1,128)S(1)} %add.53), channel_id=1, source_target_pairs={{0,16},{8,24},{16,0},{24,8},{1,17},{9,25},{17,1},{25,9},{2,18},{10... | collective-permute-start | bytes 3080 | tf_op jit(solution)/shard_map/ppermute | solution.py:567
  25.3 0.0 copy-done.2
  25.3 0.4 shard_map.124
  25.7 1.6 %collective-permute-done.8 = f32[1,256]{1,0:T(1,128)S(1)} collective-permute-done((f32[1,256]{1,0:T(1,128)S(1)}, f32[1,256]{1,0:T(1,128)S(1)}, u32[]{:S(2)}, u32[]{:S(2)}) %collective-permute-start.8) | collective-permute-done | bytes 1056 | tf_op jit(solution)/shard_map/ppermute | solution.py:567
  27.3 2.4 %shard_map.125 = (f32[8,4,8,128]{3,2,1,0:T(8,128)S(1)}, f32[32,8,128]{2,1,0:T(8,128)S(1)}, f32[320,128]{1,0:T(8,128)S(1)}, f32[80,128]{1,0:T(8,128)S(1)}) custom-call(f32[1,256]{1,0:T(1,128)S(1)} %add.54.picked.misfit, s32[8,512]{1,0:T(8,128)S(1)} %pad.9.spots, ...), custom_call_target="tpu_custom_call", output_to_operand_aliasing={{2}: (2, {}), {3}: (3, {})} | custom-call | tf_op jit(solution)/shard_map/pallas_call | solution.py:570
  29.7 0.1 collective-permute-start.9
  29.8 1.2 %collective-permute-done.9 = f32[4,4,8,128]{3,2,1,0:T(8,128)S(1)} collective-permute-done((f32[4,4,8,128]{3,2,1,0:T(8,128)S(1)}, f32[4,4,8,128]{3,2,1,0:T(8,128)S(1)}, u32[]{:S(2)}, u32[]{:S(2)}) %collective-permute-start.9) | collective-permute-done | bytes 65568 | tf_op jit(solution)/shard_map/ppermute | solution.py:601
  31.1 2.1 %collective-permute-start.10 = (f32[2,4,8,128]{3,2,1,0:T(8,128)S(1)}, f32[2,4,8,128]{3,2,1,0:T(8,128)S(1)}, u32[]{:S(2)}, u32[]{:S(2)}) collective-permute-start(f32[2,4,8,128]{3,2,1,0:T(8,128)S(1)} %slice.35), channel_id=1, source_target_pairs={{0,2},{1,3},{2,0},{3,1},{4,6},{5,7},{6,4},{7,5},{8,10},{9,11},{10,... | collective-permute-start | bytes 98312 | tf_op jit(solution)/shard_map/ppermute | solution.py:601
  33.2 1.9 %collective-permute-done.10 = f32[2,4,8,128]{3,2,1,0:T(8,128)S(1)} collective-permute-done((f32[2,4,8,128]{3,2,1,0:T(8,128)S(1)}, f32[2,4,8,128]{3,2,1,0:T(8,128)S(1)}, u32[]{:S(2)}, u32[]{:S(2)}) %collective-permute-start.10) | collective-permute-done | bytes 32800 | tf_op jit(solution)/shard_map/ppermute | solution.py:601
  35.1 3.1 %collective-permute-start.11 = (f32[4,8,128]{2,1,0:T(8,128)S(1)}, f32[4,8,128]{2,1,0:T(8,128)S(1)}, u32[]{:S(2)}, u32[]{:S(2)}) collective-permute-start(f32[4,8,128]{2,1,0:T(8,128)S(1)} %get-tuple-element.58), channel_id=1, source_target_pairs={{0,4},{1,5},{2,6},{3,7},{4,0},{5,1},{6,2},{7,3},{8,12},{9,13},{10,... | collective-permute-start | bytes 49160 | tf_op jit(solution)/shard_map/ppermute | solution.py:602
  38.2 0.7 %shard_map.126 = (f32[1,32,8,128]{3,2,1,0:T(8,128)}, f32[1,32,8,128]{3,2,1,0:T(8,128)}, f32[1,256]{1,0:T(1,128)}) custom-call(f32[32,8,128]{2,1,0:T(8,128)S(1)} %get-tuple-element.40.field, f32[32,8,128]{2,1,0:T(8,128)S(1)} %get-tuple-element.49.adjoint, f32[1,256]{1,0:T(1,128)S(1)} %add.54.picked.misfit), custom_call_target="tpu_custom_call" | custom-call | bytes 4000000 | tf_op jit(solution)/shard_map/pallas_call | solution.py:589
  38.9 1.0 %collective-permute-done.11.came = f32[4,8,128]{2,1,0:T(8,128)S(1)} collective-permute-done((f32[4,8,128]{2,1,0:T(8,128)S(1)}, f32[4,8,128]{2,1,0:T(8,128)S(1)}, u32[]{:S(2)}, u32[]{:S(2)}) %collective-permute-start.11) | collective-permute-done | bytes 16416 | tf_op jit(solution)/shard_map/ppermute | solution.py:602
  39.9 0.6 %shard_map.127 = f32[4,8,128]{2,1,0:T(8,128)} custom-call(f32[4,8,128]{2,1,0:T(8,128)S(1)} %get-tuple-element.53.scale, f32[4,8,128]{2,1,0:T(8,128)S(1)} %get-tuple-element.54.prior, f32[4,8,128]{2,1,0:T(8,128)S(1)} %get-tuple-element.59.kept, f32[4,8,128]{2,1,0:T(8,128)S(1)} %collective-permute-done.11.came), custom_call_target="tpu_custom_call" | custom-call | tf_op jit(solution)/shard_map/pallas_call | solution.py:603
  (18 shorter events, 0.1 us)
Async XLA Ops:
  0.6 8.0 %copy-start = (f32[1,32,8,128]{3,2,1,0:T(8,128)S(1)}, f32[1,32,8,128]{3,2,1,0:T(8,128)}, u32[]{:S(2)}) copy-start(f32[1,32,8,128]{3,2,1,0:T(8,128)} %param.16) | copy-start | bytes 393220
  0.6 6.0 %collective-permute-start.2 = (f32[1,4,8,128]{3,2,1,0:T(8,128)}, f32[1,4,8,128]{3,2,1,0:T(8,128)S(1)}, u32[]{:S(2)}, u32[]{:S(2)}) collective-permute-start(f32[1,4,8,128]{3,2,1,0:T(8,128)} %bitcast.18), channel_id=1, source_target_pairs={{0,4},{1,5},{2,6},{3,7},{4,0},{5,1},{6,2},{7,3},{8,12},{9,13},{10,... | collective-permute-start | bytes 49160 | tf_op jit(solution)/shard_map/ppermute | solution.py:489
  4.7 3.9 %collective-permute-start = (f32[32,8,128]{2,1,0:T(8,128)}, f32[32,8,128]{2,1,0:T(8,128)S(1)}, u32[]{:S(2)}, u32[]{:S(2)}) collective-permute-start(f32[32,8,128]{2,1,0:T(8,128)} %bitcast.12), channel_id=1, source_target_pairs={{0,1},{1,0},{2,3},{3,2},{4,5},{5,4},{6,7},{7,6},{8,9},{9,8},{10,11... | collective-permute-start | bytes 393224 | tf_op jit(solution)/shard_map/ppermute | solution.py:482
  4.7 3.9 %collective-permute-start.1 = (f32[32,8,128]{2,1,0:T(8,128)}, f32[32,8,128]{2,1,0:T(8,128)S(1)}, u32[]{:S(2)}, u32[]{:S(2)}) collective-permute-start(f32[32,8,128]{2,1,0:T(8,128)} %bitcast.15), channel_id=1, source_target_pairs={{0,1},{1,0},{2,3},{3,2},{4,5},{5,4},{6,7},{7,6},{8,9},{9,8},{10,11... | collective-permute-start | bytes 393224 | tf_op jit(solution)/shard_map/ppermute | solution.py:483
  6.7 2.0 %copy-start.9 = (s32[256,2]{0,1:T(2,128)S(1)}, s32[256,2]{0,1:T(2,128)}, u32[]{:S(2)}) copy-start(s32[256,2]{0,1:T(2,128)} %param.14) | copy-start | bytes 6148
  6.7 4.0 %collective-permute-start.3 = (f32[2,4,8,128]{3,2,1,0:T(8,128)S(1)}, f32[2,4,8,128]{3,2,1,0:T(8,128)S(1)}, u32[]{:S(2)}, u32[]{:S(2)}) collective-permute-start(f32[2,4,8,128]{3,2,1,0:T(8,128)S(1)} %slice.32), channel_id=1, source_target_pairs={{0,2},{1,3},{2,0},{3,1},{4,6},{5,7},{6,4},{7,5},{8,10},{9,11},{10,... | collective-permute-start | bytes 98312 | tf_op jit(solution)/shard_map/ppermute | solution.py:489
  8.7 0.9 %copy-start.1 = (f32[1,32,8,128]{3,2,1,0:T(8,128)S(1)}, f32[1,32,8,128]{3,2,1,0:T(8,128)}, u32[]{:S(2)}) copy-start(f32[1,32,8,128]{3,2,1,0:T(8,128)} %param.17) | copy-start | bytes 393220
  10.7 1.3 %collective-permute-start.4 = (f32[4,4,8,128]{3,2,1,0:T(8,128)S(1)}, f32[4,4,8,128]{3,2,1,0:T(8,128)S(1)}, u32[]{:S(2)}, u32[]{:S(2)}) collective-permute-start(f32[4,4,8,128]{3,2,1,0:T(8,128)S(1)} %slice.33), channel_id=1, source_target_pairs={{0,1},{1,0},{2,3},{3,2},{4,5},{5,4},{6,7},{7,6},{8,9},{9,8},{10,11... | collective-permute-start | bytes 196616 | tf_op jit(solution)/shard_map/ppermute | solution.py:489
  12.0 2.2 %copy-start.3 = (f32[4,8,128]{2,1,0:T(8,128)S(1)}, f32[4,8,128]{2,1,0:T(8,128)}, u32[]{:S(2)}) copy-start(f32[4,8,128]{2,1,0:T(8,128)} %own_model.1) | copy-start | bytes 49156
  12.0 2.2 %copy-start.4 = (s32[4,8,128]{2,1,0:T(8,128)S(1)}, s32[4,8,128]{2,1,0:T(8,128)}, u32[]{:S(2)}) copy-start(s32[4,8,128]{2,1,0:T(8,128)} %labels.1) | copy-start | bytes 49156
  12.0 2.2 %copy-start.7 = (f32[4]{0:T(128)S(1)}, f32[4]{0:T(128)}, u32[]{:S(2)}) copy-start(f32[4]{0:T(128)} %means.1) | copy-start | bytes 52
  12.0 2.2 %copy-start.8 = (f32[4]{0:T(128)S(1)}, f32[4]{0:T(128)}, u32[]{:S(2)}) copy-start(f32[4]{0:T(128)} %variances.1) | copy-start | bytes 52
  12.2 4.4 %collective-permute-start.5 = (f32[14,8,128]{2,1,0:T(8,128)S(1)}, f32[14,8,128]{2,1,0:T(8,128)S(1)}, u32[]{:S(2)}, u32[]{:S(2)}) collective-permute-start(f32[14,8,128]{2,1,0:T(8,128)S(1)} %get-tuple-element.32), channel_id=1, source_target_pairs={{0,8},{1,25},{2,10},{3,27},{4,12},{5,29},{6,14},{7,31},{8,0},{9,17... | collective-permute-start | bytes 172040 | tf_op jit(solution)/shard_map/ppermute | solution.py:514
  14.1 0.7 %copy-start.5 = (f32[1,256]{1,0:T(1,128)S(1)}, f32[1,256]{1,0:T(1,128)}, u32[]{:S(2)}) copy-start(f32[1,256]{1,0:T(1,128)} %observed.1) | copy-start | bytes 3076
  14.2 0.7 %copy-start.6 = (s32[1,2]{1,0:T(1,128)S(1)}, s32[1,2]{1,0:T(1,128)}, u32[]{:S(2)}) copy-start(s32[1,2]{1,0:T(1,128)} %cells.1) | copy-start | bytes 28
  16.6 1.2 %collective-permute-start.6 = (f32[14,8,128]{2,1,0:T(8,128)S(1)}, f32[14,8,128]{2,1,0:T(8,128)S(1)}, u32[]{:S(2)}, u32[]{:S(2)}) collective-permute-start(f32[14,8,128]{2,1,0:T(8,128)S(1)} %broadcast_add_fusion), channel_id=1, source_target_pairs={{0,1},{1,0},{2,3},{3,2},{4,5},{5,4},{6,7},{7,6},{8,9},{9,8},{10,11... | collective-permute-start | bytes 172040 | tf_op jit(solution)/shard_map/ppermute | solution.py:534
  17.9 7.5 %copy-start.2 = (f32[1,32,8,128]{3,2,1,0:T(8,128)S(1)}, f32[1,32,8,128]{3,2,1,0:T(8,128)}, u32[]{:S(2)}) copy-start(f32[1,32,8,128]{3,2,1,0:T(8,128)} %param.17) | copy-start | bytes 393220
  19.9 3.8 %collective-permute-start.7 = (f32[1,256]{1,0:T(1,128)S(1)}, f32[1,256]{1,0:T(1,128)S(1)}, u32[]{:S(2)}, u32[]{:S(2)}) collective-permute-start(f32[1,256]{1,0:T(1,128)S(1)} %get-tuple-element.41), channel_id=1, source_target_pairs={{0,8},{8,0},{16,24},{24,16},{1,9},{9,1},{17,25},{25,17},{2,10},{10... | collective-permute-start | bytes 3080 | tf_op jit(solution)/shard_map/ppermute | solution.py:567
  23.7 3.6 %collective-permute-start.8 = (f32[1,256]{1,0:T(1,128)S(1)}, f32[1,256]{1,0:T(1,128)S(1)}, u32[]{:S(2)}, u32[]{:S(2)}) collective-permute-start(f32[1,256]{1,0:T(1,128)S(1)} %add.53), channel_id=1, source_target_pairs={{0,16},{8,24},{16,0},{24,8},{1,17},{9,25},{17,1},{25,9},{2,18},{10... | collective-permute-start | bytes 3080 | tf_op jit(solution)/shard_map/ppermute | solution.py:567
  29.7 1.3 %collective-permute-start.9 = (f32[4,4,8,128]{3,2,1,0:T(8,128)S(1)}, f32[4,4,8,128]{3,2,1,0:T(8,128)S(1)}, u32[]{:S(2)}, u32[]{:S(2)}) collective-permute-start(f32[4,4,8,128]{3,2,1,0:T(8,128)S(1)} %slice.27), channel_id=1, source_target_pairs={{0,1},{1,0},{2,3},{3,2},{4,5},{5,4},{6,7},{7,6},{8,9},{9,8},{10,11... | collective-permute-start | bytes 196616 | tf_op jit(solution)/shard_map/ppermute | solution.py:601
  31.1 4.0 %collective-permute-start.10 = (f32[2,4,8,128]{3,2,1,0:T(8,128)S(1)}, f32[2,4,8,128]{3,2,1,0:T(8,128)S(1)}, u32[]{:S(2)}, u32[]{:S(2)}) collective-permute-start(f32[2,4,8,128]{3,2,1,0:T(8,128)S(1)} %slice.35), channel_id=1, source_target_pairs={{0,2},{1,3},{2,0},{3,1},{4,6},{5,7},{6,4},{7,5},{8,10},{9,11},{10,... | collective-permute-start | bytes 98312 | tf_op jit(solution)/shard_map/ppermute | solution.py:601
  35.1 4.8 %collective-permute-start.11 = (f32[4,8,128]{2,1,0:T(8,128)S(1)}, f32[4,8,128]{2,1,0:T(8,128)S(1)}, u32[]{:S(2)}, u32[]{:S(2)}) collective-permute-start(f32[4,8,128]{2,1,0:T(8,128)S(1)} %get-tuple-element.58), channel_id=1, source_target_pairs={{0,4},{1,5},{2,6},{3,7},{4,0},{5,1},{6,2},{7,3},{8,12},{9,13},{10,... | collective-permute-start | bytes 49160 | tf_op jit(solution)/shard_map/ppermute | solution.py:602

commit v4 on v3

--- a/solution.py
+++ b/solution.py
@@ -21,6 +21,7 @@
 SLOT = 32
 HALF = SLOT // 2
 PACK_AT = 1
+TOGETHER = 8
 DEPTH = 8
 
 F32 = jnp.float32
@@ -269,17 +270,21 @@
     put_row(main, GROUPS * (per + 2) - 2, jnp.zeros((DEPTH, main.shape[1]), F32))
 
 
-def sweep(old, new, face_m, face_r, b_m, b_r):
+def sweep(old, new, face_m, face_r, b_m, b_r, first):
     per = b_r.shape[0]
-    main_new, rim_new = new
-    above, own = row_set(*old, -1, per), row_set(*old, 0, per)
-    face_above = [face_m[2, (per + 1) * g] for g in range(GROUPS)] + [face_r[2, 0]]
-    for k in range(per):
+    for step in range(per):
+        k = (first + step) % per
+        if step == 0 or k == 0:
+            above, own = row_set(*old, k - 1, per), row_set(*old, k, per)
+            face_above = [face_m[2, (per + 1) * g + k] for g in range(GROUPS)] + [face_r[2, k]]
+        else:
+            above, own = own, below
         below = row_set(*old, k + 1, per)
         before, after = beside(own)
+        done = []
         for g in range(GROUPS + 1):
             n = g // GROUPS
-            field, face, b = (old[n], (face_m, face_r)[n], (b_m, b_r)[n])
+            face, b = ((face_m, face_r)[n], (b_m, b_r)[n])
             y = k if n else k + per * g
             r = k if n else k + (per + 2) * g
             c = k if n else k + (per + 1) * g
@@ -288,9 +293,16 @@
             total = total + (fz * up_depth(own[g]) + down_depth(fz * own[g]))
             total = total + (fy * below[g] + face_above[g] * above[g])
             face_above[g] = fy
-            put_row(new[n], r, total * face[5, c + 1])
-        above, own = own, below
-    wrap(main_new, rim_new, per)
+            done.append(total * face[4, c + 1])
+            put_row(new[n], r, done[g])
+        if k == 0:
+            put_row(new[1], per, turn(done[GROUPS], -SLOT))
+            for g in range(1, GROUPS):
+                put_row(new[0], g * (per + 2) - 2, turn(done[g], -SLOT))
+        if k == per - 1:
+            put_row(new[1], -1, turn(done[GROUPS], SLOT))
+            for g in range(1, GROUPS):
+                put_row(new[0], g * (per + 2) - 1, turn(done[g - 1], SLOT))
 
 
 def relax(first, second, face_m, face_r, b_m, b_r):
@@ -298,12 +310,13 @@
     clear_ends(second[0], per)
     wrap(*first, per)
 
-    def two(_, carry):
-        sweep(first, second, face_m, face_r, b_m, b_r)
-        sweep(second, first, face_m, face_r, b_m, b_r)
+    def some(_, carry):
+        for n in range(TOGETHER):
+            old, new = (first, second) if n % 2 == 0 else (second, first)
+            sweep(old, new, face_m, face_r, b_m, b_r, n)
         return carry
 
-    lax.fori_loop(0, SWEEPS // 2, two, 0)
+    lax.fori_loop(0, SWEEPS // TOGETHER, some, 0)
 
 
 def three_parts(values):
@@ -358,8 +371,7 @@
             if not n and k == 0:
                 face[2, c] = by
             face[3, c + 1] = fz
-            face[4, c + 1] = bz
-            face[5, c + 1] = 1.0 / diagonal
+            face[4, c + 1] = 1.0 / diagonal
     face_r[2, 0] = turn(face_r[2, per], SLOT)
 
 
@@ -539,8 +551,8 @@
             shaped(rows, depth, width),
             shaped(*main_shape),
             shaped(*rim_shape),
-            shaped(6, rows + GROUPS, depth, width),
-            shaped(6, per + 1, depth, width),
+            shaped(5, rows + GROUPS, depth, width),
+            shaped(5, per + 1, depth, width),
             shaped(*main_shape),
         ),
         in_specs=[VMEM] * 8,

time: 40.8 us -> 39.6 us (0.971)
  Pallas kernels: 7.73 us -> 6.45 us
    pallas_call x1, Pallas kernels: 2.42 us -> 1.55 us  [on_device(): pl.pallas_call(functools.partial(adjoint_kernel, total_x, levels), out_sh...]
where the time goes in v4:
time: 39.6 us; the launch traced here: 39.3 us
  starting transfers between devices  17.8 us (45%)
  waiting for transfers between devices  11.8 us (30%)
  Pallas kernels  6.45 us (16%)
  local copies, waits for them, and re-layouts  2.34 us (6%)
  between operations  0.84 us (2%)
    ppermute x3, starting transfers between devices, on_device(): came = lax.ppermute(sent, 'src', xor_pairs(peers, bits[level]))  6.14 us
    ppermute x2, starting transfers between devices, on_device(): picked = picked + lax.ppermute(picked, 'tile', xor_pairs(tiles, step))  3.82 us
    ppermute x2, waiting for transfers between devices, on_device(): picked = picked + lax.ppermute(picked, 'tile', xor_pairs(tiles, step))  3.18 us
    ppermute x2, waiting for transfers between devices, on_device(): lax.ppermute(terms[keep:], 'src', xor_pairs(peers, bits[level]))  3.14 us
    ppermute x1, starting transfers between devices, on_device(): came = lax.ppermute(terms[1], 'src', xor_pairs(peers, bits[-1]))  3.11 us
    ppermute x3, waiting for transfers between devices, on_device(): came = lax.ppermute(sent, 'src', xor_pairs(peers, bits[level]))  2.59 us
    ppermute x2, starting transfers between devices, on_device(): lax.ppermute(terms[keep:], 'src', xor_pairs(peers, bits[level]))  2.19 us
    ppermute x1, starting transfers between devices, on_device(): mine = lax.ppermute(payload, ('tile', 'src'), pairs)  1.9 us
  transfers between devices with their start and end apart: 12, of which 10 were waited for; matrix products, arithmetic and copies ran while one was open for 2% of the time, Pallas kernels for 6%

profile of v4, /device:TPU:0, one launch (start us, length us, event | category | flops | bytes accessed | tf_op | source)
XLA Modules:
  0.0 39.3 jit_solution(16068617653208726695)
XLA Ops:
  0.6 0.0 copy-start
  0.6 4.1 %collective-permute-start.2 = (f32[1,4,8,128]{3,2,1,0:T(8,128)}, f32[1,4,8,128]{3,2,1,0:T(8,128)S(1)}, u32[]{:S(2)}, u32[]{:S(2)}) collective-permute-start(f32[1,4,8,128]{3,2,1,0:T(8,128)} %bitcast.18), channel_id=1, source_target_pairs={{0,4},{1,5},{2,6},{3,7},{4,0},{5,1},{6,2},{7,3},{8,12},{9,13},{10,... | collective-permute-start | bytes 49160 | tf_op jit(solution)/shard_map/ppermute | solution.py:501
  4.7 0.0 collective-permute-start
  4.7 0.5 %collective-permute-start.1 = (f32[32,8,128]{2,1,0:T(8,128)}, f32[32,8,128]{2,1,0:T(8,128)S(1)}, u32[]{:S(2)}, u32[]{:S(2)}) collective-permute-start(f32[32,8,128]{2,1,0:T(8,128)} %bitcast.15), channel_id=1, source_target_pairs={{0,1},{1,0},{2,3},{3,2},{4,5},{5,4},{6,7},{7,6},{8,9},{9,8},{10,11... | collective-permute-start | bytes 393224 | tf_op jit(solution)/shard_map/ppermute | solution.py:495
  5.3 0.7 %pad.8 = f32[8,4,8,128]{3,2,1,0:T(8,128)S(1)} pad(f32[1,4,8,128]{3,2,1,0:T(8,128)} %bitcast.19, f32[]{:T(128)} %constant.28.clone.1), padding=0_7x0_0x0_0x0_0 | pad | bytes 147460 | tf_op jit(solution)/shard_map/jit(_pad)/pad | solution.py:498
  6.0 0.7 %collective-permute-done.2 = f32[1,4,8,128]{3,2,1,0:T(8,128)S(1)} collective-permute-done((f32[1,4,8,128]{3,2,1,0:T(8,128)}, f32[1,4,8,128]{3,2,1,0:T(8,128)S(1)}, u32[]{:S(2)}, u32[]{:S(2)}) %collective-permute-start.2) | collective-permute-done | bytes 16416 | tf_op jit(solution)/shard_map/ppermute | solution.py:501
  6.7 0.0 copy-start.9
  6.7 2.0 %collective-permute-start.3 = (f32[2,4,8,128]{3,2,1,0:T(8,128)S(1)}, f32[2,4,8,128]{3,2,1,0:T(8,128)S(1)}, u32[]{:S(2)}, u32[]{:S(2)}) collective-permute-start(f32[2,4,8,128]{3,2,1,0:T(8,128)S(1)} %slice.32), channel_id=1, source_target_pairs={{0,2},{1,3},{2,0},{3,1},{4,6},{5,7},{6,4},{7,5},{8,10},{9,11},{10,... | collective-permute-start | bytes 98312 | tf_op jit(solution)/shard_map/ppermute | solution.py:501
  8.7 0.0 copy-done.9
  8.7 0.0 collective-permute-done.other_v
  8.7 0.0 collective-permute-done.1.other_a
  8.7 0.0 copy-done
  8.7 0.0 copy-start.1
  8.7 0.9 %copy-done.1 = f32[1,32,8,128]{3,2,1,0:T(8,128)S(1)} copy-done((f32[1,32,8,128]{3,2,1,0:T(8,128)S(1)}, f32[1,32,8,128]{3,2,1,0:T(8,128)}, u32[]{:S(2)}) %copy-start.1) | copy-done | bytes 131096
  9.6 0.4 shard_map.120
  10.0 0.7 %collective-permute-done.3 = f32[2,4,8,128]{3,2,1,0:T(8,128)S(1)} collective-permute-done((f32[2,4,8,128]{3,2,1,0:T(8,128)S(1)}, f32[2,4,8,128]{3,2,1,0:T(8,128)S(1)}, u32[]{:S(2)}, u32[]{:S(2)}) %collective-permute-start.3) | collective-permute-done | bytes 32800 | tf_op jit(solution)/shard_map/ppermute | solution.py:501
  10.7 0.1 collective-permute-start.4
  10.8 1.2 %collective-permute-done.4 = f32[4,4,8,128]{3,2,1,0:T(8,128)S(1)} collective-permute-done((f32[4,4,8,128]{3,2,1,0:T(8,128)S(1)}, f32[4,4,8,128]{3,2,1,0:T(8,128)S(1)}, u32[]{:S(2)}, u32[]{:S(2)}) %collective-permute-start.4) | collective-permute-done | bytes 65568 | tf_op jit(solution)/shard_map/ppermute | solution.py:501
  12.0 0.0 copy-start.3
  12.0 0.0 copy-start.4
  12.0 0.0 copy-start.7
  12.0 0.0 copy-start.8
  12.0 0.2 shard_map.121
  12.2 1.9 %collective-permute-start.5 = (f32[14,8,128]{2,1,0:T(8,128)S(1)}, f32[14,8,128]{2,1,0:T(8,128)S(1)}, u32[]{:S(2)}, u32[]{:S(2)}) collective-permute-start(f32[14,8,128]{2,1,0:T(8,128)S(1)} %get-tuple-element.32), channel_id=1, source_target_pairs={{0,8},{1,25},{2,10},{3,27},{4,12},{5,29},{6,14},{7,31},{8,0},{9,17... | collective-permute-start | bytes 172040 | tf_op jit(solution)/shard_map/ppermute | solution.py:526
  14.1 0.0 copy-start.5
  14.2 0.0 copy-start.6
  14.2 0.0 copy-done.3
  14.2 0.0 copy-done.4
  14.2 0.0 copy-done.7
  14.2 0.0 copy-done.8
  14.2 0.6 %copy-done.5 = f32[1,256]{1,0:T(1,128)S(1)} copy-done((f32[1,256]{1,0:T(1,128)S(1)}, f32[1,256]{1,0:T(1,128)}, u32[]{:S(2)}) %copy-start.5) | copy-done | bytes 1048
  14.8 0.0 copy-done.6
  14.8 1.0 %shard_map.122 = (f32[4,8,128]{2,1,0:T(8,128)S(1)}, f32[4,8,128]{2,1,0:T(8,128)S(1)}, f32[320,128]{1,0:T(8,128)S(1)}, f32[320,128]{1,0:T(8,128)S(1)}, f32[32,8,1...) custom-call(s32[1,2]{1,0:T(1,128)S(1)} %copy-done.6, ...), custom_call_target="tpu_custom_call" | custom-call | bytes 4000000 | tf_op jit(solution)/shard_map/pallas_call | solution.py:528
  15.8 0.8 %collective-permute-done.5.mine = f32[14,8,128]{2,1,0:T(8,128)S(1)} collective-permute-done((f32[14,8,128]{2,1,0:T(8,128)S(1)}, f32[14,8,128]{2,1,0:T(8,128)S(1)}, u32[]{:S(2)}, u32[]{:S(2)}) %collective-permute-start.5) | collective-permute-done | bytes 57376 | tf_op jit(solution)/shard_map/ppermute | solution.py:526
  16.6 0.1 collective-permute-start.6
  16.7 1.1 %collective-permute-done.6.theirs = f32[14,8,128]{2,1,0:T(8,128)S(1)} collective-permute-done((f32[14,8,128]{2,1,0:T(8,128)S(1)}, f32[14,8,128]{2,1,0:T(8,128)S(1)}, u32[]{:S(2)}, u32[]{:S(2)}) %collective-permute-start.6) | collective-permute-done | bytes 57376 | tf_op jit(solution)/shard_map/ppermute | solution.py:546
  17.9 0.0 copy-start.2
  17.9 1.7 %shard_map.123 = (f32[1,256]{1,0:T(1,128)S(1)}, f32[32,8,128]{2,1,0:T(8,128)S(1)}, f32[320,128]{1,0:T(8,128)S(1)}, f32[80,128]{1,0:T(8,128)S(1)}, f32[5,36,8,128...) custom-call(f32[14,8,128]{2,1,0:T(8,128)S(1)} %collective-permute-do, ...), custom_call_target="tpu_custom_call", output_to_operand_aliasing={{2}: (2, {}), {6}: (3, {})} | custom-call | tf_op jit(solution)/shard_map/pallas_call | solution.py:547
  19.5 2.2 %collective-permute-start.7 = (f32[1,256]{1,0:T(1,128)S(1)}, f32[1,256]{1,0:T(1,128)S(1)}, u32[]{:S(2)}, u32[]{:S(2)}) collective-permute-start(f32[1,256]{1,0:T(1,128)S(1)} %get-tuple-element.41), channel_id=1, source_target_pairs={{0,8},{8,0},{16,24},{24,16},{1,9},{9,1},{17,25},{25,17},{2,10},{10... | collective-permute-start | bytes 3080 | tf_op jit(solution)/shard_map/ppermute | solution.py:579
  21.8 1.5 %collective-permute-done.7 = f32[1,256]{1,0:T(1,128)S(1)} collective-permute-done((f32[1,256]{1,0:T(1,128)S(1)}, f32[1,256]{1,0:T(1,128)S(1)}, u32[]{:S(2)}, u32[]{:S(2)}) %collective-permute-start.7) | collective-permute-done | bytes 1056 | tf_op jit(solution)/shard_map/ppermute | solution.py:579
  23.3 1.6 %collective-permute-start.8 = (f32[1,256]{1,0:T(1,128)S(1)}, f32[1,256]{1,0:T(1,128)S(1)}, u32[]{:S(2)}, u32[]{:S(2)}) collective-permute-start(f32[1,256]{1,0:T(1,128)S(1)} %add.53), channel_id=1, source_target_pairs={{0,16},{8,24},{16,0},{24,8},{1,17},{9,25},{17,1},{25,9},{2,18},{10... | collective-permute-start | bytes 3080 | tf_op jit(solution)/shard_map/ppermute | solution.py:579
  24.9 0.0 copy-done.2
  24.9 0.4 shard_map.124
  25.3 1.6 %collective-permute-done.8 = f32[1,256]{1,0:T(1,128)S(1)} collective-permute-done((f32[1,256]{1,0:T(1,128)S(1)}, f32[1,256]{1,0:T(1,128)S(1)}, u32[]{:S(2)}, u32[]{:S(2)}) %collective-permute-start.8) | collective-permute-done | bytes 1056 | tf_op jit(solution)/shard_map/ppermute | solution.py:579
  26.9 1.5 %shard_map.125 = (f32[8,4,8,128]{3,2,1,0:T(8,128)S(1)}, f32[32,8,128]{2,1,0:T(8,128)S(1)}, f32[320,128]{1,0:T(8,128)S(1)}, f32[80,128]{1,0:T(8,128)S(1)}) custom-call(f32[1,256]{1,0:T(1,128)S(1)} %add.54.picked.misfit, s32[8,512]{1,0:T(8,128)S(1)} %pad.9.spots, ...), custom_call_target="tpu_custom_call", output_to_operand_aliasing={{2}: (2, {}), {3}: (3, {})} | custom-call | tf_op jit(solution)/shard_map/pallas_call | solution.py:582
  28.5 0.1 collective-permute-start.9
  28.6 1.2 %collective-permute-done.9 = f32[4,4,8,128]{3,2,1,0:T(8,128)S(1)} collective-permute-done((f32[4,4,8,128]{3,2,1,0:T(8,128)S(1)}, f32[4,4,8,128]{3,2,1,0:T(8,128)S(1)}, u32[]{:S(2)}, u32[]{:S(2)}) %collective-permute-start.9) | collective-permute-done | bytes 65568 | tf_op jit(solution)/shard_map/ppermute | solution.py:613
  29.8 2.1 %collective-permute-start.10 = (f32[2,4,8,128]{3,2,1,0:T(8,128)S(1)}, f32[2,4,8,128]{3,2,1,0:T(8,128)S(1)}, u32[]{:S(2)}, u32[]{:S(2)}) collective-permute-start(f32[2,4,8,128]{3,2,1,0:T(8,128)S(1)} %slice.35), channel_id=1, source_target_pairs={{0,2},{1,3},{2,0},{3,1},{4,6},{5,7},{6,4},{7,5},{8,10},{9,11},{10,... | collective-permute-start | bytes 98312 | tf_op jit(solution)/shard_map/ppermute | solution.py:613
  31.9 1.9 %collective-permute-done.10 = f32[2,4,8,128]{3,2,1,0:T(8,128)S(1)} collective-permute-done((f32[2,4,8,128]{3,2,1,0:T(8,128)S(1)}, f32[2,4,8,128]{3,2,1,0:T(8,128)S(1)}, u32[]{:S(2)}, u32[]{:S(2)}) %collective-permute-start.10) | collective-permute-done | bytes 32800 | tf_op jit(solution)/shard_map/ppermute | solution.py:613
  33.9 3.1 %collective-permute-start.11 = (f32[4,8,128]{2,1,0:T(8,128)S(1)}, f32[4,8,128]{2,1,0:T(8,128)S(1)}, u32[]{:S(2)}, u32[]{:S(2)}) collective-permute-start(f32[4,8,128]{2,1,0:T(8,128)S(1)} %get-tuple-element.58), channel_id=1, source_target_pairs={{0,4},{1,5},{2,6},{3,7},{4,0},{5,1},{6,2},{7,3},{8,12},{9,13},{10,... | collective-permute-start | bytes 49160 | tf_op jit(solution)/shard_map/ppermute | solution.py:614
  37.0 0.7 %shard_map.126 = (f32[1,32,8,128]{3,2,1,0:T(8,128)}, f32[1,32,8,128]{3,2,1,0:T(8,128)}, f32[1,256]{1,0:T(1,128)}) custom-call(f32[32,8,128]{2,1,0:T(8,128)S(1)} %get-tuple-element.40.field, f32[32,8,128]{2,1,0:T(8,128)S(1)} %get-tuple-element.49.adjoint, f32[1,256]{1,0:T(1,128)S(1)} %add.54.picked.misfit), custom_call_target="tpu_custom_call" | custom-call | bytes 4000000 | tf_op jit(solution)/shard_map/pallas_call | solution.py:601
  37.7 1.0 %collective-permute-done.11.came = f32[4,8,128]{2,1,0:T(8,128)S(1)} collective-permute-done((f32[4,8,128]{2,1,0:T(8,128)S(1)}, f32[4,8,128]{2,1,0:T(8,128)S(1)}, u32[]{:S(2)}, u32[]{:S(2)}) %collective-permute-start.11) | collective-permute-done | bytes 16416 | tf_op jit(solution)/shard_map/ppermute | solution.py:614
  38.7 0.6 %shard_map.127 = f32[4,8,128]{2,1,0:T(8,128)} custom-call(f32[4,8,128]{2,1,0:T(8,128)S(1)} %get-tuple-element.53.scale, f32[4,8,128]{2,1,0:T(8,128)S(1)} %get-tuple-element.54.prior, f32[4,8,128]{2,1,0:T(8,128)S(1)} %get-tuple-element.59.kept, f32[4,8,128]{2,1,0:T(8,128)S(1)} %collective-permute-done.11.came), custom_call_target="tpu_custom_call" | custom-call | tf_op jit(solution)/shard_map/pallas_call | solution.py:615
  (18 shorter events, 0.1 us)
Async XLA Ops:
  0.6 8.0 %copy-start = (f32[1,32,8,128]{3,2,1,0:T(8,128)S(1)}, f32[1,32,8,128]{3,2,1,0:T(8,128)}, u32[]{:S(2)}) copy-start(f32[1,32,8,128]{3,2,1,0:T(8,128)} %param.16) | copy-start | bytes 393220
  0.6 6.0 %collective-permute-start.2 = (f32[1,4,8,128]{3,2,1,0:T(8,128)}, f32[1,4,8,128]{3,2,1,0:T(8,128)S(1)}, u32[]{:S(2)}, u32[]{:S(2)}) collective-permute-start(f32[1,4,8,128]{3,2,1,0:T(8,128)} %bitcast.18), channel_id=1, source_target_pairs={{0,4},{1,5},{2,6},{3,7},{4,0},{5,1},{6,2},{7,3},{8,12},{9,13},{10,... | collective-permute-start | bytes 49160 | tf_op jit(solution)/shard_map/ppermute | solution.py:501
  4.7 3.9 %collective-permute-start = (f32[32,8,128]{2,1,0:T(8,128)}, f32[32,8,128]{2,1,0:T(8,128)S(1)}, u32[]{:S(2)}, u32[]{:S(2)}) collective-permute-start(f32[32,8,128]{2,1,0:T(8,128)} %bitcast.12), channel_id=1, source_target_pairs={{0,1},{1,0},{2,3},{3,2},{4,5},{5,4},{6,7},{7,6},{8,9},{9,8},{10,11... | collective-permute-start | bytes 393224 | tf_op jit(solution)/shard_map/ppermute | solution.py:494
  4.7 3.9 %collective-permute-start.1 = (f32[32,8,128]{2,1,0:T(8,128)}, f32[32,8,128]{2,1,0:T(8,128)S(1)}, u32[]{:S(2)}, u32[]{:S(2)}) collective-permute-start(f32[32,8,128]{2,1,0:T(8,128)} %bitcast.15), channel_id=1, source_target_pairs={{0,1},{1,0},{2,3},{3,2},{4,5},{5,4},{6,7},{7,6},{8,9},{9,8},{10,11... | collective-permute-start | bytes 393224 | tf_op jit(solution)/shard_map/ppermute | solution.py:495
  6.7 2.0 %copy-start.9 = (s32[256,2]{0,1:T(2,128)S(1)}, s32[256,2]{0,1:T(2,128)}, u32[]{:S(2)}) copy-start(s32[256,2]{0,1:T(2,128)} %param.14) | copy-start | bytes 6148
  6.7 4.0 %collective-permute-start.3 = (f32[2,4,8,128]{3,2,1,0:T(8,128)S(1)}, f32[2,4,8,128]{3,2,1,0:T(8,128)S(1)}, u32[]{:S(2)}, u32[]{:S(2)}) collective-permute-start(f32[2,4,8,128]{3,2,1,0:T(8,128)S(1)} %slice.32), channel_id=1, source_target_pairs={{0,2},{1,3},{2,0},{3,1},{4,6},{5,7},{6,4},{7,5},{8,10},{9,11},{10,... | collective-permute-start | bytes 98312 | tf_op jit(solution)/shard_map/ppermute | solution.py:501
  8.7 0.9 %copy-start.1 = (f32[1,32,8,128]{3,2,1,0:T(8,128)S(1)}, f32[1,32,8,128]{3,2,1,0:T(8,128)}, u32[]{:S(2)}) copy-start(f32[1,32,8,128]{3,2,1,0:T(8,128)} %param.17) | copy-start | bytes 393220
  10.7 1.3 %collective-permute-start.4 = (f32[4,4,8,128]{3,2,1,0:T(8,128)S(1)}, f32[4,4,8,128]{3,2,1,0:T(8,128)S(1)}, u32[]{:S(2)}, u32[]{:S(2)}) collective-permute-start(f32[4,4,8,128]{3,2,1,0:T(8,128)S(1)} %slice.33), channel_id=1, source_target_pairs={{0,1},{1,0},{2,3},{3,2},{4,5},{5,4},{6,7},{7,6},{8,9},{9,8},{10,11... | collective-permute-start | bytes 196616 | tf_op jit(solution)/shard_map/ppermute | solution.py:501
  12.0 2.2 %copy-start.3 = (f32[4,8,128]{2,1,0:T(8,128)S(1)}, f32[4,8,128]{2,1,0:T(8,128)}, u32[]{:S(2)}) copy-start(f32[4,8,128]{2,1,0:T(8,128)} %own_model.1) | copy-start | bytes 49156
  12.0 2.2 %copy-start.4 = (s32[4,8,128]{2,1,0:T(8,128)S(1)}, s32[4,8,128]{2,1,0:T(8,128)}, u32[]{:S(2)}) copy-start(s32[4,8,128]{2,1,0:T(8,128)} %labels.1) | copy-start | bytes 49156
  12.0 2.2 %copy-start.7 = (f32[4]{0:T(128)S(1)}, f32[4]{0:T(128)}, u32[]{:S(2)}) copy-start(f32[4]{0:T(128)} %means.1) | copy-start | bytes 52
  12.0 2.2 %copy-start.8 = (f32[4]{0:T(128)S(1)}, f32[4]{0:T(128)}, u32[]{:S(2)}) copy-start(f32[4]{0:T(128)} %variances.1) | copy-start | bytes 52
  12.2 4.4 %collective-permute-start.5 = (f32[14,8,128]{2,1,0:T(8,128)S(1)}, f32[14,8,128]{2,1,0:T(8,128)S(1)}, u32[]{:S(2)}, u32[]{:S(2)}) collective-permute-start(f32[14,8,128]{2,1,0:T(8,128)S(1)} %get-tuple-element.32), channel_id=1, source_target_pairs={{0,8},{1,25},{2,10},{3,27},{4,12},{5,29},{6,14},{7,31},{8,0},{9,17... | collective-permute-start | bytes 172040 | tf_op jit(solution)/shard_map/ppermute | solution.py:526
  14.1 0.7 %copy-start.5 = (f32[1,256]{1,0:T(1,128)S(1)}, f32[1,256]{1,0:T(1,128)}, u32[]{:S(2)}) copy-start(f32[1,256]{1,0:T(1,128)} %observed.1) | copy-start | bytes 3076
  14.2 0.7 %copy-start.6 = (s32[1,2]{1,0:T(1,128)S(1)}, s32[1,2]{1,0:T(1,128)}, u32[]{:S(2)}) copy-start(s32[1,2]{1,0:T(1,128)} %cells.1) | copy-start | bytes 28
  16.6 1.2 %collective-permute-start.6 = (f32[14,8,128]{2,1,0:T(8,128)S(1)}, f32[14,8,128]{2,1,0:T(8,128)S(1)}, u32[]{:S(2)}, u32[]{:S(2)}) collective-permute-start(f32[14,8,128]{2,1,0:T(8,128)S(1)} %broadcast_add_fusion), channel_id=1, source_target_pairs={{0,1},{1,0},{2,3},{3,2},{4,5},{5,4},{6,7},{7,6},{8,9},{9,8},{10,11... | collective-permute-start | bytes 172040 | tf_op jit(solution)/shard_map/ppermute | solution.py:546
  17.9 7.1 %copy-start.2 = (f32[1,32,8,128]{3,2,1,0:T(8,128)S(1)}, f32[1,32,8,128]{3,2,1,0:T(8,128)}, u32[]{:S(2)}) copy-start(f32[1,32,8,128]{3,2,1,0:T(8,128)} %param.17) | copy-start | bytes 393220
  19.5 3.8 %collective-permute-start.7 = (f32[1,256]{1,0:T(1,128)S(1)}, f32[1,256]{1,0:T(1,128)S(1)}, u32[]{:S(2)}, u32[]{:S(2)}) collective-permute-start(f32[1,256]{1,0:T(1,128)S(1)} %get-tuple-element.41), channel_id=1, source_target_pairs={{0,8},{8,0},{16,24},{24,16},{1,9},{9,1},{17,25},{25,17},{2,10},{10... | collective-permute-start | bytes 3080 | tf_op jit(solution)/shard_map/ppermute | solution.py:579
  23.3 3.6 %collective-permute-start.8 = (f32[1,256]{1,0:T(1,128)S(1)}, f32[1,256]{1,0:T(1,128)S(1)}, u32[]{:S(2)}, u32[]{:S(2)}) collective-permute-start(f32[1,256]{1,0:T(1,128)S(1)} %add.53), channel_id=1, source_target_pairs={{0,16},{8,24},{16,0},{24,8},{1,17},{9,25},{17,1},{25,9},{2,18},{10... | collective-permute-start | bytes 3080 | tf_op jit(solution)/shard_map/ppermute | solution.py:579
  28.5 1.3 %collective-permute-start.9 = (f32[4,4,8,128]{3,2,1,0:T(8,128)S(1)}, f32[4,4,8,128]{3,2,1,0:T(8,128)S(1)}, u32[]{:S(2)}, u32[]{:S(2)}) collective-permute-start(f32[4,4,8,128]{3,2,1,0:T(8,128)S(1)} %slice.27), channel_id=1, source_target_pairs={{0,1},{1,0},{2,3},{3,2},{4,5},{5,4},{6,7},{7,6},{8,9},{9,8},{10,11... | collective-permute-start | bytes 196616 | tf_op jit(solution)/shard_map/ppermute | solution.py:613
  29.8 4.0 %collective-permute-start.10 = (f32[2,4,8,128]{3,2,1,0:T(8,128)S(1)}, f32[2,4,8,128]{3,2,1,0:T(8,128)S(1)}, u32[]{:S(2)}, u32[]{:S(2)}) collective-permute-start(f32[2,4,8,128]{3,2,1,0:T(8,128)S(1)} %slice.35), channel_id=1, source_target_pairs={{0,2},{1,3},{2,0},{3,1},{4,6},{5,7},{6,4},{7,5},{8,10},{9,11},{10,... | collective-permute-start | bytes 98312 | tf_op jit(solution)/shard_map/ppermute | solution.py:613
  33.9 4.8 %collective-permute-start.11 = (f32[4,8,128]{2,1,0:T(8,128)S(1)}, f32[4,8,128]{2,1,0:T(8,128)S(1)}, u32[]{:S(2)}, u32[]{:S(2)}) collective-permute-start(f32[4,8,128]{2,1,0:T(8,128)S(1)} %get-tuple-element.58), channel_id=1, source_target_pairs={{0,4},{1,5},{2,6},{3,7},{4,0},{5,1},{6,2},{7,3},{8,12},{9,13},{10,... | collective-permute-start | bytes 49160 | tf_op jit(solution)/shard_map/ppermute | solution.py:614

commit v5 on v4

--- a/solution.py
+++ b/solution.py
@@ -196,6 +196,11 @@
         b_r[k] = b_r[k] + jnp.where(at_slot & at_depth, sign, 0.0)
 
 
+def turned_place(spots, first_col, width):
+    x = spots[0:1, :] - first_col
+    return jnp.where((x >= 0) & (x < width), (x + SLOT * spots[2:3, :] + HALF) & 127, -1)
+
+
 def own_adjoint_kernel(mine, theirs, warm, spots, main, rim, hit_x):
     rows, depth, width = warm.shape
     per = rows // GROUPS
@@ -211,17 +216,25 @@
 
     each(per // 2, body, 1)
     clear_ends(main, per)
-    at = depth_of((2 * width, spots.shape[1]))
+    first_col = lax.axis_index("tile") * width
+    at = depth_of((width, spots.shape[1]))
     slot = at % SLOT
-    at = lax.axis_index("tile") * width + jnp.where(at < width, at, HALF - 1 - slot + jnp.where(slot < HALF, width, 0))
-    hit_x[...] = jnp.where(at == spots[0:1, :], 1.0, 0.0).astype(BF16)
-
-
-def save_kernel(field, adjoint, misfit, field_out, adjoint_out, misfit_out, sems):
-    pairs = ((field, field_out.at[0]), (adjoint, adjoint_out.at[0]), (misfit, misfit_out))
-    copies = [pltpu.make_async_copy(a, b, sems.at[n]) for n, (a, b) in enumerate(pairs)]
-    for copy in copies:
-        copy.start()
+    rim_at = first_col + HALF - 1 - slot + jnp.where(slot < HALF, width, 0)
+    hit_x[:width, :] = jnp.where(at == turned_place(spots, first_col, width), 1.0, 0.0).astype(BF16)
+    hit_x[width:, :] = jnp.where(rim_at == spots[0:1, :], 1.0, 0.0).astype(BF16)
+
+
+def save_kernel(field, adjoint, misfit, field_out, adjoint_out, misfit_out, plain_v, plain_a, sems):
+    copies = [pltpu.make_async_copy(misfit, misfit_out, sems.at[2])]
+    copies[0].start()
+    rows = plain_v.shape[0]
+    per = rows // GROUPS
+    for n, (main, plain, out) in enumerate(((field, plain_v, field_out), (adjoint, plain_a, adjoint_out))):
+        for y in range(rows):
+            g = y // per
+            plain[y] = turn(at_row(main, y + 2 * g), -(SLOT * g + HALF))
+        copies.append(pltpu.make_async_copy(plain, out.at[0], sems.at[n]))
+        copies[-1].start()
     for copy in copies:
         copy.wait()
 
@@ -377,10 +390,10 @@
 
 def field_kernel(
     total_x, mine, theirs, main_in, sigma_in, b_m, b_r, spots, measured,
-    picked, plain, main, rim, face_m, face_r, main_2, rim_2,
+    picked, main, rim, face_m, face_r, main_2, rim_2,
 ):
     del main_in, sigma_in
-    rows, depth, width = plain.shape
+    rows, depth, width = b_m.shape
     shape = (depth, width)
     per = rows // GROUPS
     first_col = lax.axis_index("tile") * width
@@ -394,13 +407,12 @@
     wrap(main_2, rim_2, per)
     coefficients(total_x, first_col, main_2, rim_2, face_m, face_r)
     relax((main, rim), (main_2, rim_2), face_m, face_r, b_m, b_r)
-    for y in range(rows):
-        plain[y] = turn(at_row(main, y + 2 * (y // per)), -(SLOT * (y // per) + HALF))
     count = spots.shape[1]
-    x_row = spots[0:1, :] - first_col
     line_row = spots[1:2, :]
-    hit_x = jnp.where(depth_of((width, count)) == x_row, 1.0, 0.0).astype(BF16)
-    flat = plain[...].reshape(rows * depth, width)
+    place = turned_place(spots, first_col, width)
+    hit_x = jnp.where(depth_of((width, count)) == place, 1.0, 0.0).astype(BF16)
+    starts = [(g * (per + 2) + 1) * depth for g in range(GROUPS)]
+    flat = jnp.concatenate([main[start : start + per * depth, :] for start in starts], axis=0)
     lines = sum(jnp.dot(part, hit_x, preferred_element_type=F32) for part in three_parts(flat))
     hit_line = depth_of((rows * depth, count)) == line_row
     got = jnp.sum(jnp.where(hit_line, lines, 0.0), axis=0, keepdims=True)
@@ -409,10 +421,10 @@
 
 def adjoint_kernel(
     total_x, places, picked, spots, main_in, rim_in, hit_x, main_v, rim_v, face_m, face_r,
-    terms, plain, main, rim, main_2, rim_2, b_m, b_r,
+    terms, main, rim, main_2, rim_2, b_m, b_r,
 ):
     del main_in, rim_in
-    rows, depth, width = plain.shape
+    rows, depth, width = b_m.shape
     shape = (depth, width)
     per = rows // GROUPS
     me = lax.axis_index("src")
@@ -427,12 +439,10 @@
         flat = flat + lax.dot_general(left, hit_x[...], (((1,), (1,)), ((), ())), preferred_element_type=F32)
     flat = flat.reshape(rows, depth, 2 * width)
     for y in range(rows):
-        b_m[y] = turn(flat[y, :, :width], SLOT * (y // per) + HALF)
+        b_m[y] = flat[y, :, :width]
     for k in range(per):
         b_r[k] = merge([flat[k + per * g, :, width:] for g in range(GROUPS)])
     relax((main, rim), (main_2, rim_2), face_m, face_r, b_m, b_r)
-    for y in range(rows):
-        plain[y] = turn(at_row(main, y + 2 * (y // per)), -(SLOT * (y // per) + HALF))
     rows_own = terms.shape[1]
     bottom = depth_of(shape) == depth - 1
     for k in range(per):
@@ -484,8 +494,9 @@
     bits = [1 << n for n in range(peers.bit_length() - 1)]
     levels = list(range(len(bits)))
     spots = receiver_cells.T.reshape(1, 2 * receivers)
-    spots = jnp.concatenate([spots % total_x, spots // total_x], axis=0)
-    spots = jnp.pad(spots, ((0, 6), (0, 0)), constant_values=-1)
+    line = spots // total_x
+    spots = jnp.concatenate([spots % total_x, line, line // (depth * per)], axis=0)
+    spots = jnp.pad(spots, ((0, 5), (0, 0)), constant_values=-1)
     start_v, start_a = warm_potential[0], warm_adjoint[0]
 
     def shaped(*sizes):
@@ -544,11 +555,10 @@
         model, start_v, observed,
     )
     theirs = lax.ppermute(mine + nothing, "src", xor_pairs(peers, 1))
-    picked, plain_v, main_v, rim_v, face_m, face_r, _ = pl.pallas_call(
+    picked, main_v, rim_v, face_m, face_r, _ = pl.pallas_call(
         functools.partial(field_kernel, total_x),
         out_shape=(
             shaped(1, receivers),
-            shaped(rows, depth, width),
             shaped(*main_shape),
             shaped(*rim_shape),
             shaped(5, rows + GROUPS, depth, width),
@@ -556,8 +566,8 @@
             shaped(*main_shape),
         ),
         in_specs=[VMEM] * 8,
-        out_specs=(VMEM,) * 7,
-        input_output_aliases={2: 2, 3: 6},
+        out_specs=(VMEM,) * 6,
+        input_output_aliases={2: 1, 3: 5},
         scratch_shapes=[pltpu.VMEM(rim_shape, F32)],
         compiler_params=PARAMS,
     )(mine, theirs, main_v, sigma, b_m, b_r, spots, measured)
@@ -579,17 +589,16 @@
         picked = picked + lax.ppermute(picked, "tile", xor_pairs(tiles, step))
         step *= 2
 
-    terms, plain_a, _, _ = pl.pallas_call(
+    terms, main_a, _ = pl.pallas_call(
         functools.partial(adjoint_kernel, total_x, levels),
         out_shape=(
             shaped(peers, rows_own, depth, width),
-            shaped(rows, depth, width),
             shaped(*main_shape),
             shaped(*rim_shape),
         ),
         in_specs=[VMEM] * 9,
-        out_specs=(VMEM,) * 4,
-        input_output_aliases={2: 2, 3: 3},
+        out_specs=(VMEM,) * 3,
+        input_output_aliases={2: 1, 3: 2},
         scratch_shapes=[
             pltpu.VMEM(main_shape, F32),
             pltpu.VMEM(rim_shape, F32),
@@ -603,10 +612,10 @@
         out_shape=(shaped(*warm_potential.shape), shaped(*warm_adjoint.shape), shaped(*observed.shape)),
         in_specs=[VMEM] * 3,
         out_specs=(HBM,) * 3,
-        scratch_shapes=[pltpu.SemaphoreType.DMA((3,))],
+        scratch_shapes=[pltpu.VMEM((rows, depth, width), F32)] * 2 + [pltpu.SemaphoreType.DMA((3,))],
         cost_estimate=BESIDE,
         compiler_params=PARAMS,
-    )(plain_v, plain_a, picked)
+    )(main_v, main_a, picked)
 
     for level in levels[:-1]:
         keep = terms.shape[0] // 2

time: 39.6 us -> 39.5 us (level)
  no operation moved by 1% of the time
where the time goes in v5:
time: 39.5 us; the launch traced here: 39.2 us
  starting transfers between devices  17.8 us (45%)
  waiting for transfers between devices  11.7 us (30%)
  Pallas kernels  6.44 us (16%)
  local copies, waits for them, and re-layouts  2.33 us (6%)
  between operations  0.86 us (2%)
    ppermute x3, starting transfers between devices, on_device(): came = lax.ppermute(sent, 'src', xor_pairs(peers, bits[level]))  6.14 us
    ppermute x2, starting transfers between devices, on_device(): picked = picked + lax.ppermute(picked, 'tile', xor_pairs(tiles, step))  3.82 us
    ppermute x2, waiting for transfers between devices, on_device(): picked = picked + lax.ppermute(picked, 'tile', xor_pairs(tiles, step))  3.18 us
    ppermute x2, waiting for transfers between devices, on_device(): lax.ppermute(terms[keep:], 'src', xor_pairs(peers, bits[level]))  3.14 us
    ppermute x1, starting transfers between devices, on_device(): came = lax.ppermute(terms[1], 'src', xor_pairs(peers, bits[-1]))  3.11 us
    ppermute x3, waiting for transfers between devices, on_device(): came = lax.ppermute(sent, 'src', xor_pairs(peers, bits[level]))  2.59 us
    ppermute x2, starting transfers between devices, on_device(): lax.ppermute(terms[keep:], 'src', xor_pairs(peers, bits[level]))  2.19 us
    ppermute x1, starting transfers between devices, on_device(): mine = lax.ppermute(payload, ('tile', 'src'), pairs)  1.9 us
  transfers between devices with their start and end apart: 12, of which 10 were waited for; matrix products, arithmetic and copies ran while one was open for 2% of the time, Pallas kernels for 6%

profile of v5, /device:TPU:0, one launch (start us, length us, event | category | flops | bytes accessed | tf_op | source)
XLA Modules:
  0.0 39.2 jit_solution(16663510990959442673)
XLA Ops:
  0.6 0.0 copy-start
  0.6 4.1 %collective-permute-start.2 = (f32[1,4,8,128]{3,2,1,0:T(8,128)}, f32[1,4,8,128]{3,2,1,0:T(8,128)S(1)}, u32[]{:S(2)}, u32[]{:S(2)}) collective-permute-start(f32[1,4,8,128]{3,2,1,0:T(8,128)} %bitcast.18), channel_id=1, source_target_pairs={{0,4},{1,5},{2,6},{3,7},{4,0},{5,1},{6,2},{7,3},{8,12},{9,13},{10,... | collective-permute-start | bytes 49160 | tf_op jit(solution)/shard_map/ppermute | solution.py:512
  4.7 0.0 collective-permute-start
  4.7 0.5 %collective-permute-start.1 = (f32[32,8,128]{2,1,0:T(8,128)}, f32[32,8,128]{2,1,0:T(8,128)S(1)}, u32[]{:S(2)}, u32[]{:S(2)}) collective-permute-start(f32[32,8,128]{2,1,0:T(8,128)} %bitcast.15), channel_id=1, source_target_pairs={{0,1},{1,0},{2,3},{3,2},{4,5},{5,4},{6,7},{7,6},{8,9},{9,8},{10,11... | collective-permute-start | bytes 393224 | tf_op jit(solution)/shard_map/ppermute | solution.py:506
  5.3 0.7 %pad.8 = f32[8,4,8,128]{3,2,1,0:T(8,128)S(1)} pad(f32[1,4,8,128]{3,2,1,0:T(8,128)} %bitcast.19, f32[]{:T(128)} %constant.37.clone.1), padding=0_7x0_0x0_0x0_0 | pad | bytes 147460 | tf_op jit(solution)/shard_map/jit(_pad)/pad | solution.py:509
  6.0 0.7 %collective-permute-done.2 = f32[1,4,8,128]{3,2,1,0:T(8,128)S(1)} collective-permute-done((f32[1,4,8,128]{3,2,1,0:T(8,128)}, f32[1,4,8,128]{3,2,1,0:T(8,128)S(1)}, u32[]{:S(2)}, u32[]{:S(2)}) %collective-permute-start.2) | collective-permute-done | bytes 16416 | tf_op jit(solution)/shard_map/ppermute | solution.py:512
  6.7 0.0 copy-start.9
  6.7 2.0 %collective-permute-start.3 = (f32[2,4,8,128]{3,2,1,0:T(8,128)S(1)}, f32[2,4,8,128]{3,2,1,0:T(8,128)S(1)}, u32[]{:S(2)}, u32[]{:S(2)}) collective-permute-start(f32[2,4,8,128]{3,2,1,0:T(8,128)S(1)} %slice.32), channel_id=1, source_target_pairs={{0,2},{1,3},{2,0},{3,1},{4,6},{5,7},{6,4},{7,5},{8,10},{9,11},{10,... | collective-permute-start | bytes 98312 | tf_op jit(solution)/shard_map/ppermute | solution.py:512
  8.7 0.0 copy-done.9
  8.7 0.0 collective-permute-done.other_v
  8.7 0.0 collective-permute-done.1.other_a
  8.7 0.0 copy-done
  8.7 0.0 copy-start.1
  8.7 0.9 %copy-done.1 = f32[1,32,8,128]{3,2,1,0:T(8,128)S(1)} copy-done((f32[1,32,8,128]{3,2,1,0:T(8,128)S(1)}, f32[1,32,8,128]{3,2,1,0:T(8,128)}, u32[]{:S(2)}) %copy-start.1) | copy-done | bytes 131096
  9.6 0.4 %shard_map.120 = (f32[14,8,128]{2,1,0:T(8,128)S(1)}, f32[8,4,8,128]{3,2,1,0:T(8,128)S(1)}) custom-call(f32[32,8,128]{2,1,0:T(8,128)S(1)} %bitcast.13, f32[32,8,128]{2,1,0:T(8,128)S(1)} %bitcast.16, f32[32,8,128]{2,1,0:T(8,128)S(1)} %collective-permute-done.other_v, ...), custom_call_target="tpu_custom_call", output_to_operand_aliasing={{1}: (4, {})} | custom-call | bytes 4000000 | tf_op jit(solution)/shard_map/pallas_call | solution.py:514
  10.0 0.7 %collective-permute-done.3 = f32[2,4,8,128]{3,2,1,0:T(8,128)S(1)} collective-permute-done((f32[2,4,8,128]{3,2,1,0:T(8,128)S(1)}, f32[2,4,8,128]{3,2,1,0:T(8,128)S(1)}, u32[]{:S(2)}, u32[]{:S(2)}) %collective-permute-start.3) | collective-permute-done | bytes 32800 | tf_op jit(solution)/shard_map/ppermute | solution.py:512
  10.7 0.1 collective-permute-start.4
  10.8 1.2 %collective-permute-done.4 = f32[4,4,8,128]{3,2,1,0:T(8,128)S(1)} collective-permute-done((f32[4,4,8,128]{3,2,1,0:T(8,128)S(1)}, f32[4,4,8,128]{3,2,1,0:T(8,128)S(1)}, u32[]{:S(2)}, u32[]{:S(2)}) %collective-permute-start.4) | collective-permute-done | bytes 65568 | tf_op jit(solution)/shard_map/ppermute | solution.py:512
  12.0 0.0 copy-start.3
  12.0 0.0 copy-start.4
  12.0 0.0 copy-start.7
  12.0 0.0 copy-start.8
  12.0 0.2 shard_map.121
  12.2 1.9 %collective-permute-start.5 = (f32[14,8,128]{2,1,0:T(8,128)S(1)}, f32[14,8,128]{2,1,0:T(8,128)S(1)}, u32[]{:S(2)}, u32[]{:S(2)}) collective-permute-start(f32[14,8,128]{2,1,0:T(8,128)S(1)} %get-tuple-element.31), channel_id=1, source_target_pairs={{0,8},{1,25},{2,10},{3,27},{4,12},{5,29},{6,14},{7,31},{8,0},{9,17... | collective-permute-start | bytes 172040 | tf_op jit(solution)/shard_map/ppermute | solution.py:537
  14.2 0.0 copy-start.5
  14.2 0.0 copy-start.6
  14.2 0.0 copy-done.3
  14.2 0.0 copy-done.4
  14.2 0.0 copy-done.7
  14.2 0.0 copy-done.8
  14.2 0.6 %copy-done.5 = f32[1,256]{1,0:T(1,128)S(1)} copy-done((f32[1,256]{1,0:T(1,128)S(1)}, f32[1,256]{1,0:T(1,128)}, u32[]{:S(2)}) %copy-start.5) | copy-done | bytes 1048
  14.8 0.0 copy-done.6
  14.8 1.0 %shard_map.122 = (f32[4,8,128]{2,1,0:T(8,128)S(1)}, f32[4,8,128]{2,1,0:T(8,128)S(1)}, f32[320,128]{1,0:T(8,128)S(1)}, f32[320,128]{1,0:T(8,128)S(1)}, f32[32,8,1...) custom-call(s32[1,2]{1,0:T(1,128)S(1)} %copy-done.6, ...), custom_call_target="tpu_custom_call" | custom-call | bytes 4000000 | tf_op jit(solution)/shard_map/pallas_call | solution.py:539
  15.8 0.8 %collective-permute-done.5.mine = f32[14,8,128]{2,1,0:T(8,128)S(1)} collective-permute-done((f32[14,8,128]{2,1,0:T(8,128)S(1)}, f32[14,8,128]{2,1,0:T(8,128)S(1)}, u32[]{:S(2)}, u32[]{:S(2)}) %collective-permute-start.5) | collective-permute-done | bytes 57376 | tf_op jit(solution)/shard_map/ppermute | solution.py:537
  16.6 0.1 collective-permute-start.6
  16.7 1.1 %collective-permute-done.6.theirs = f32[14,8,128]{2,1,0:T(8,128)S(1)} collective-permute-done((f32[14,8,128]{2,1,0:T(8,128)S(1)}, f32[14,8,128]{2,1,0:T(8,128)S(1)}, u32[]{:S(2)}, u32[]{:S(2)}) %collective-permute-start.6) | collective-permute-done | bytes 57376 | tf_op jit(solution)/shard_map/ppermute | solution.py:557
  17.9 0.0 copy-start.2
  17.9 1.6 %shard_map.123 = (f32[1,256]{1,0:T(1,128)S(1)}, f32[320,128]{1,0:T(8,128)S(1)}, f32[80,128]{1,0:T(8,128)S(1)}, f32[5,36,8,128]{3,2,1,0:T(8,128)S(1)}, f32[5,9,8,...) custom-call(f32[14,8,128]{2,1,0:T(8,128)S(1)} %collective-permute-done.5.mine, ...), custom_call_target="tpu_custom_call", output_to_operand_aliasing={{1}: (2, {}), {5}: (3, {})} | custom-call | tf_op jit(solution)/shard_map/pallas_call | solution.py:558
  19.5 2.2 %collective-permute-start.7 = (f32[1,256]{1,0:T(1,128)S(1)}, f32[1,256]{1,0:T(1,128)S(1)}, u32[]{:S(2)}, u32[]{:S(2)}) collective-permute-start(f32[1,256]{1,0:T(1,128)S(1)} %get-tuple-element.40), channel_id=1, source_target_pairs={{0,8},{8,0},{16,24},{24,16},{1,9},{9,1},{17,25},{25,17},{2,10},{10... | collective-permute-start | bytes 3080 | tf_op jit(solution)/shard_map/ppermute | solution.py:589
  21.7 1.5 %collective-permute-done.7 = f32[1,256]{1,0:T(1,128)S(1)} collective-permute-done((f32[1,256]{1,0:T(1,128)S(1)}, f32[1,256]{1,0:T(1,128)S(1)}, u32[]{:S(2)}, u32[]{:S(2)}) %collective-permute-start.7) | collective-permute-done | bytes 1056 | tf_op jit(solution)/shard_map/ppermute | solution.py:589
  23.3 1.6 %collective-permute-start.8 = (f32[1,256]{1,0:T(1,128)S(1)}, f32[1,256]{1,0:T(1,128)S(1)}, u32[]{:S(2)}, u32[]{:S(2)}) collective-permute-start(f32[1,256]{1,0:T(1,128)S(1)} %add.66), channel_id=1, source_target_pairs={{0,16},{8,24},{16,0},{24,8},{1,17},{9,25},{17,1},{25,9},{2,18},{10... | collective-permute-start | bytes 3080 | tf_op jit(solution)/shard_map/ppermute | solution.py:589
  24.8 0.0 copy-done.2
  24.8 0.4 shard_map.124
  25.2 1.6 %collective-permute-done.8 = f32[1,256]{1,0:T(1,128)S(1)} collective-permute-done((f32[1,256]{1,0:T(1,128)S(1)}, f32[1,256]{1,0:T(1,128)S(1)}, u32[]{:S(2)}, u32[]{:S(2)}) %collective-permute-start.8) | collective-permute-done | bytes 1056 | tf_op jit(solution)/shard_map/ppermute | solution.py:589
  26.8 1.5 %shard_map.125 = (f32[8,4,8,128]{3,2,1,0:T(8,128)S(1)}, f32[320,128]{1,0:T(8,128)S(1)}, f32[80,128]{1,0:T(8,128)S(1)}) custom-call(f32[1,256]{1,0:T(1,128)S(1)} %add.67.picked.misfit, s32[8,512]{1,0:T(8,128)S(1)} %pad.9.spots, f32[320,128]{1,0:T(8,128)S(1)} %get-tuple-element.41.main_in, ...), custom_call_target="tpu_custom_call", output_to_operand_aliasing={{1}: (2, {}), {2}: (3, {})} | custom-call | tf_op jit(solution)/shard_map/pallas_call | solution.py:592
  28.4 0.1 collective-permute-start.9
  28.5 1.2 %collective-permute-done.9 = f32[4,4,8,128]{3,2,1,0:T(8,128)S(1)} collective-permute-done((f32[4,4,8,128]{3,2,1,0:T(8,128)S(1)}, f32[4,4,8,128]{3,2,1,0:T(8,128)S(1)}, u32[]{:S(2)}, u32[]{:S(2)}) %collective-permute-start.9) | collective-permute-done | bytes 65568 | tf_op jit(solution)/shard_map/ppermute | solution.py:622
  29.7 2.1 %collective-permute-start.10 = (f32[2,4,8,128]{3,2,1,0:T(8,128)S(1)}, f32[2,4,8,128]{3,2,1,0:T(8,128)S(1)}, u32[]{:S(2)}, u32[]{:S(2)}) collective-permute-start(f32[2,4,8,128]{3,2,1,0:T(8,128)S(1)} %slice.35), channel_id=1, source_target_pairs={{0,2},{1,3},{2,0},{3,1},{4,6},{5,7},{6,4},{7,5},{8,10},{9,11},{10,... | collective-permute-start | bytes 98312 | tf_op jit(solution)/shard_map/ppermute | solution.py:622
  31.8 1.9 %collective-permute-done.10 = f32[2,4,8,128]{3,2,1,0:T(8,128)S(1)} collective-permute-done((f32[2,4,8,128]{3,2,1,0:T(8,128)S(1)}, f32[2,4,8,128]{3,2,1,0:T(8,128)S(1)}, u32[]{:S(2)}, u32[]{:S(2)}) %collective-permute-start.10) | collective-permute-done | bytes 32800 | tf_op jit(solution)/shard_map/ppermute | solution.py:622
  33.8 3.1 %collective-permute-start.11 = (f32[4,8,128]{2,1,0:T(8,128)S(1)}, f32[4,8,128]{2,1,0:T(8,128)S(1)}, u32[]{:S(2)}, u32[]{:S(2)}) collective-permute-start(f32[4,8,128]{2,1,0:T(8,128)S(1)} %get-tuple-element.58), channel_id=1, source_target_pairs={{0,4},{1,5},{2,6},{3,7},{4,0},{5,1},{6,2},{7,3},{8,12},{9,13},{10,... | collective-permute-start | bytes 49160 | tf_op jit(solution)/shard_map/ppermute | solution.py:623
  36.9 0.8 %shard_map.126 = (f32[1,32,8,128]{3,2,1,0:T(8,128)}, f32[1,32,8,128]{3,2,1,0:T(8,128)}, f32[1,256]{1,0:T(1,128)}) custom-call(f32[320,128]{1,0:T(8,128)S(1)} %get-tuple-element.39.main_v.field, f32[320,128]{1,0:T(8,128)S(1)} %get-tuple-element.47.adjoint, f32[1,256]{1,0:T(1,128)S(1)} %add.67.picked.misfit), custom_call_target="tpu_custom_call" | custom-call | bytes 4000000 | tf_op jit(solution)/shard_map/pallas_call | solution.py:610
  37.7 0.9 %collective-permute-done.11.came = f32[4,8,128]{2,1,0:T(8,128)S(1)} collective-permute-done((f32[4,8,128]{2,1,0:T(8,128)S(1)}, f32[4,8,128]{2,1,0:T(8,128)S(1)}, u32[]{:S(2)}, u32[]{:S(2)}) %collective-permute-start.11) | collective-permute-done | bytes 16416 | tf_op jit(solution)/shard_map/ppermute | solution.py:623
  38.6 0.6 %shard_map.127 = f32[4,8,128]{2,1,0:T(8,128)} custom-call(f32[4,8,128]{2,1,0:T(8,128)S(1)} %get-tuple-element.51.scale, f32[4,8,128]{2,1,0:T(8,128)S(1)} %get-tuple-element.52.prior, f32[4,8,128]{2,1,0:T(8,128)S(1)} %get-tuple-element.59.kept, f32[4,8,128]{2,1,0:T(8,128)S(1)} %collective-permute-done.11.came), custom_call_target="tpu_custom_call" | custom-call | tf_op jit(solution)/shard_map/pallas_call | solution.py:624
  (18 shorter events, 0.1 us)
Async XLA Ops:
  0.6 8.0 %copy-start = (f32[1,32,8,128]{3,2,1,0:T(8,128)S(1)}, f32[1,32,8,128]{3,2,1,0:T(8,128)}, u32[]{:S(2)}) copy-start(f32[1,32,8,128]{3,2,1,0:T(8,128)} %param.16) | copy-start | bytes 393220
  0.6 6.0 %collective-permute-start.2 = (f32[1,4,8,128]{3,2,1,0:T(8,128)}, f32[1,4,8,128]{3,2,1,0:T(8,128)S(1)}, u32[]{:S(2)}, u32[]{:S(2)}) collective-permute-start(f32[1,4,8,128]{3,2,1,0:T(8,128)} %bitcast.18), channel_id=1, source_target_pairs={{0,4},{1,5},{2,6},{3,7},{4,0},{5,1},{6,2},{7,3},{8,12},{9,13},{10,... | collective-permute-start | bytes 49160 | tf_op jit(solution)/shard_map/ppermute | solution.py:512
  4.7 3.9 %collective-permute-start = (f32[32,8,128]{2,1,0:T(8,128)}, f32[32,8,128]{2,1,0:T(8,128)S(1)}, u32[]{:S(2)}, u32[]{:S(2)}) collective-permute-start(f32[32,8,128]{2,1,0:T(8,128)} %bitcast.12), channel_id=1, source_target_pairs={{0,1},{1,0},{2,3},{3,2},{4,5},{5,4},{6,7},{7,6},{8,9},{9,8},{10,11... | collective-permute-start | bytes 393224 | tf_op jit(solution)/shard_map/ppermute | solution.py:505
  4.7 3.9 %collective-permute-start.1 = (f32[32,8,128]{2,1,0:T(8,128)}, f32[32,8,128]{2,1,0:T(8,128)S(1)}, u32[]{:S(2)}, u32[]{:S(2)}) collective-permute-start(f32[32,8,128]{2,1,0:T(8,128)} %bitcast.15), channel_id=1, source_target_pairs={{0,1},{1,0},{2,3},{3,2},{4,5},{5,4},{6,7},{7,6},{8,9},{9,8},{10,11... | collective-permute-start | bytes 393224 | tf_op jit(solution)/shard_map/ppermute | solution.py:506
  6.7 2.0 %copy-start.9 = (s32[256,2]{0,1:T(2,128)S(1)}, s32[256,2]{0,1:T(2,128)}, u32[]{:S(2)}) copy-start(s32[256,2]{0,1:T(2,128)} %param.14) | copy-start | bytes 6148
  6.7 4.0 %collective-permute-start.3 = (f32[2,4,8,128]{3,2,1,0:T(8,128)S(1)}, f32[2,4,8,128]{3,2,1,0:T(8,128)S(1)}, u32[]{:S(2)}, u32[]{:S(2)}) collective-permute-start(f32[2,4,8,128]{3,2,1,0:T(8,128)S(1)} %slice.32), channel_id=1, source_target_pairs={{0,2},{1,3},{2,0},{3,1},{4,6},{5,7},{6,4},{7,5},{8,10},{9,11},{10,... | collective-permute-start | bytes 98312 | tf_op jit(solution)/shard_map/ppermute | solution.py:512
  8.7 0.9 %copy-start.1 = (f32[1,32,8,128]{3,2,1,0:T(8,128)S(1)}, f32[1,32,8,128]{3,2,1,0:T(8,128)}, u32[]{:S(2)}) copy-start(f32[1,32,8,128]{3,2,1,0:T(8,128)} %param.17) | copy-start | bytes 393220
  10.7 1.3 %collective-permute-start.4 = (f32[4,4,8,128]{3,2,1,0:T(8,128)S(1)}, f32[4,4,8,128]{3,2,1,0:T(8,128)S(1)}, u32[]{:S(2)}, u32[]{:S(2)}) collective-permute-start(f32[4,4,8,128]{3,2,1,0:T(8,128)S(1)} %slice.33), channel_id=1, source_target_pairs={{0,1},{1,0},{2,3},{3,2},{4,5},{5,4},{6,7},{7,6},{8,9},{9,8},{10,11... | collective-permute-start | bytes 196616 | tf_op jit(solution)/shard_map/ppermute | solution.py:512
  12.0 2.2 %copy-start.3 = (f32[4,8,128]{2,1,0:T(8,128)S(1)}, f32[4,8,128]{2,1,0:T(8,128)}, u32[]{:S(2)}) copy-start(f32[4,8,128]{2,1,0:T(8,128)} %own_model.1) | copy-start | bytes 49156
  12.0 2.2 %copy-start.4 = (s32[4,8,128]{2,1,0:T(8,128)S(1)}, s32[4,8,128]{2,1,0:T(8,128)}, u32[]{:S(2)}) copy-start(s32[4,8,128]{2,1,0:T(8,128)} %labels.1) | copy-start | bytes 49156
  12.0 2.2 %copy-start.7 = (f32[4]{0:T(128)S(1)}, f32[4]{0:T(128)}, u32[]{:S(2)}) copy-start(f32[4]{0:T(128)} %means.1) | copy-start | bytes 52
  12.0 2.2 %copy-start.8 = (f32[4]{0:T(128)S(1)}, f32[4]{0:T(128)}, u32[]{:S(2)}) copy-start(f32[4]{0:T(128)} %variances.1) | copy-start | bytes 52
  12.2 4.4 %collective-permute-start.5 = (f32[14,8,128]{2,1,0:T(8,128)S(1)}, f32[14,8,128]{2,1,0:T(8,128)S(1)}, u32[]{:S(2)}, u32[]{:S(2)}) collective-permute-start(f32[14,8,128]{2,1,0:T(8,128)S(1)} %get-tuple-element.31), channel_id=1, source_target_pairs={{0,8},{1,25},{2,10},{3,27},{4,12},{5,29},{6,14},{7,31},{8,0},{9,17... | collective-permute-start | bytes 172040 | tf_op jit(solution)/shard_map/ppermute | solution.py:537
  14.2 0.7 %copy-start.5 = (f32[1,256]{1,0:T(1,128)S(1)}, f32[1,256]{1,0:T(1,128)}, u32[]{:S(2)}) copy-start(f32[1,256]{1,0:T(1,128)} %observed.1) | copy-start | bytes 3076
  14.2 0.7 %copy-start.6 = (s32[1,2]{1,0:T(1,128)S(1)}, s32[1,2]{1,0:T(1,128)}, u32[]{:S(2)}) copy-start(s32[1,2]{1,0:T(1,128)} %cells.1) | copy-start | bytes 28
  16.6 1.2 %collective-permute-start.6 = (f32[14,8,128]{2,1,0:T(8,128)S(1)}, f32[14,8,128]{2,1,0:T(8,128)S(1)}, u32[]{:S(2)}, u32[]{:S(2)}) collective-permute-start(f32[14,8,128]{2,1,0:T(8,128)S(1)} %broadcast_add_fusion), channel_id=1, source_target_pairs={{0,1},{1,0},{2,3},{3,2},{4,5},{5,4},{6,7},{7,6},{8,9},{9,8},{10,11... | collective-permute-start | bytes 172040 | tf_op jit(solution)/shard_map/ppermute | solution.py:557
  17.9 7.0 %copy-start.2 = (f32[1,32,8,128]{3,2,1,0:T(8,128)S(1)}, f32[1,32,8,128]{3,2,1,0:T(8,128)}, u32[]{:S(2)}) copy-start(f32[1,32,8,128]{3,2,1,0:T(8,128)} %param.17) | copy-start | bytes 393220
  19.5 3.8 %collective-permute-start.7 = (f32[1,256]{1,0:T(1,128)S(1)}, f32[1,256]{1,0:T(1,128)S(1)}, u32[]{:S(2)}, u32[]{:S(2)}) collective-permute-start(f32[1,256]{1,0:T(1,128)S(1)} %get-tuple-element.40), channel_id=1, source_target_pairs={{0,8},{8,0},{16,24},{24,16},{1,9},{9,1},{17,25},{25,17},{2,10},{10... | collective-permute-start | bytes 3080 | tf_op jit(solution)/shard_map/ppermute | solution.py:589
  23.3 3.6 %collective-permute-start.8 = (f32[1,256]{1,0:T(1,128)S(1)}, f32[1,256]{1,0:T(1,128)S(1)}, u32[]{:S(2)}, u32[]{:S(2)}) collective-permute-start(f32[1,256]{1,0:T(1,128)S(1)} %add.66), channel_id=1, source_target_pairs={{0,16},{8,24},{16,0},{24,8},{1,17},{9,25},{17,1},{25,9},{2,18},{10... | collective-permute-start | bytes 3080 | tf_op jit(solution)/shard_map/ppermute | solution.py:589
  28.4 1.3 %collective-permute-start.9 = (f32[4,4,8,128]{3,2,1,0:T(8,128)S(1)}, f32[4,4,8,128]{3,2,1,0:T(8,128)S(1)}, u32[]{:S(2)}, u32[]{:S(2)}) collective-permute-start(f32[4,4,8,128]{3,2,1,0:T(8,128)S(1)} %slice.27), channel_id=1, source_target_pairs={{0,1},{1,0},{2,3},{3,2},{4,5},{5,4},{6,7},{7,6},{8,9},{9,8},{10,11... | collective-permute-start | bytes 196616 | tf_op jit(solution)/shard_map/ppermute | solution.py:622
  29.7 4.0 %collective-permute-start.10 = (f32[2,4,8,128]{3,2,1,0:T(8,128)S(1)}, f32[2,4,8,128]{3,2,1,0:T(8,128)S(1)}, u32[]{:S(2)}, u32[]{:S(2)}) collective-permute-start(f32[2,4,8,128]{3,2,1,0:T(8,128)S(1)} %slice.35), channel_id=1, source_target_pairs={{0,2},{1,3},{2,0},{3,1},{4,6},{5,7},{6,4},{7,5},{8,10},{9,11},{10,... | collective-permute-start | bytes 98312 | tf_op jit(solution)/shard_map/ppermute | solution.py:622
  33.8 4.8 %collective-permute-start.11 = (f32[4,8,128]{2,1,0:T(8,128)S(1)}, f32[4,8,128]{2,1,0:T(8,128)S(1)}, u32[]{:S(2)}, u32[]{:S(2)}) collective-permute-start(f32[4,8,128]{2,1,0:T(8,128)S(1)} %get-tuple-element.58), channel_id=1, source_target_pairs={{0,4},{1,5},{2,6},{3,7},{4,0},{5,1},{6,2},{7,3},{8,12},{9,13},{10,... | collective-permute-start | bytes 49160 | tf_op jit(solution)/shard_map/ppermute | solution.py:623

commit v6 on v5

--- a/solution.py
+++ b/solution.py
@@ -21,7 +21,6 @@
 SLOT = 32
 HALF = SLOT // 2
 PACK_AT = 1
-TOGETHER = 8
 DEPTH = 8
 
 F32 = jnp.float32
@@ -201,7 +200,7 @@
     return jnp.where((x >= 0) & (x < width), (x + SLOT * spots[2:3, :] + HALF) & 127, -1)
 
 
-def own_adjoint_kernel(mine, theirs, warm, spots, main, rim, hit_x):
+def own_adjoint_kernel(mine, theirs, warm, spots, face_m, face_r, swept, swept_rim, hit_x, main, rim):
     rows, depth, width = warm.shape
     per = rows // GROUPS
     mask = window(1 - facing(), 0, (depth, width))
@@ -216,6 +215,9 @@
 
     each(per // 2, body, 1)
     clear_ends(main, per)
+    clear_ends(swept, per)
+    wrap(main, rim, per)
+    sweep((main, rim), (swept, swept_rim), face_m, face_r, None, None, 0)
     first_col = lax.axis_index("tile") * width
     at = depth_of((width, spots.shape[1]))
     slot = at % SLOT
@@ -284,7 +286,7 @@
 
 
 def sweep(old, new, face_m, face_r, b_m, b_r, first):
-    per = b_r.shape[0]
+    per = face_r.shape[1] - 1
     for step in range(per):
         k = (first + step) % per
         if step == 0 or k == 0:
@@ -302,7 +304,9 @@
             r = k if n else k + (per + 2) * g
             c = k if n else k + (per + 1) * g
             fy, fz = face[2, c + 1], face[3, c + 1]
-            total = b[y] + face[0, c + 1] * after[g] + face[1, c + 1] * before[g]
+            total = face[0, c + 1] * after[g] + face[1, c + 1] * before[g]
+            if b is not None:
+                total = b[y] + total
             total = total + (fz * up_depth(own[g]) + down_depth(fz * own[g]))
             total = total + (fy * below[g] + face_above[g] * above[g])
             face_above[g] = fy
@@ -318,18 +322,14 @@
                 put_row(new[0], g * (per + 2) - 1, turn(done[g - 1], SLOT))
 
 
-def relax(first, second, face_m, face_r, b_m, b_r):
-    per = b_r.shape[0]
+def relax(first, second, face_m, face_r, b_m, b_r, start=0):
+    per = face_r.shape[1] - 1
     clear_ends(second[0], per)
     wrap(*first, per)
-
-    def some(_, carry):
-        for n in range(TOGETHER):
-            old, new = (first, second) if n % 2 == 0 else (second, first)
-            sweep(old, new, face_m, face_r, b_m, b_r, n)
-        return carry
-
-    lax.fori_loop(0, SWEEPS // TOGETHER, some, 0)
+    for n in range(start, SWEEPS):
+        sweep(first, second, face_m, face_r, b_m, b_r, n)
+        first, second = second, first
+    return first
 
 
 def three_parts(values):
@@ -421,7 +421,7 @@
 
 def adjoint_kernel(
     total_x, places, picked, spots, main_in, rim_in, hit_x, main_v, rim_v, face_m, face_r,
-    terms, main, rim, main_2, rim_2, b_m, b_r,
+    terms, main_2, main_1, rim_1, rim_2, b_m, b_r,
 ):
     del main_in, rim_in
     rows, depth, width = b_m.shape
@@ -442,7 +442,12 @@
         b_m[y] = flat[y, :, :width]
     for k in range(per):
         b_r[k] = merge([flat[k + per * g, :, width:] for g in range(GROUPS)])
-    relax((main, rim), (main_2, rim_2), face_m, face_r, b_m, b_r)
+    for y in range(rows):
+        r = y + 2 * (y // per)
+        put_row(main_1, r, at_row(main_1, r) + b_m[y] * face_m[4, y + y // per + 1])
+    for k in range(per):
+        put_row(rim_1, k, at_row(rim_1, k) + b_r[k] * face_r[4, k + 1])
+    main, rim = relax((main_1, rim_1), (main_2, rim_2), face_m, face_r, b_m, b_r, 1)
     rows_own = terms.shape[1]
     bottom = depth_of(shape) == depth - 1
     for k in range(per):
@@ -578,29 +583,30 @@
             shaped(*rim_shape),
             jax.ShapeDtypeStruct((2 * width, 2 * receivers), BF16),
         ),
-        in_specs=[VMEM] * 4,
+        in_specs=[VMEM] * 6,
         out_specs=(VMEM,) * 3,
+        scratch_shapes=[pltpu.VMEM(main_shape, F32), pltpu.VMEM(rim_shape, F32)],
         cost_estimate=BESIDE,
         compiler_params=PARAMS,
-    )(mine, theirs, start_a, spots)
+    )(mine, theirs, start_a, spots, face_m, face_r)
 
     step = 1
     while step < tiles:
         picked = picked + lax.ppermute(picked, "tile", xor_pairs(tiles, step))
         step *= 2
 
-    terms, main_a, _ = pl.pallas_call(
+    terms, main_a, _, _ = pl.pallas_call(
         functools.partial(adjoint_kernel, total_x, levels),
         out_shape=(
             shaped(peers, rows_own, depth, width),
             shaped(*main_shape),
+            shaped(*main_shape),
             shaped(*rim_shape),
         ),
         in_specs=[VMEM] * 9,
-        out_specs=(VMEM,) * 3,
-        input_output_aliases={2: 1, 3: 2},
+        out_specs=(VMEM,) * 4,
+        input_output_aliases={2: 2, 3: 3},
         scratch_shapes=[
-            pltpu.VMEM(main_shape, F32),
             pltpu.VMEM(rim_shape, F32),
             pltpu.VMEM((rows, depth, width), F32),
             pltpu.VMEM((per, depth, width), F32),

time: 39.5 us -> 39.4 us (level)
  transfers between devices with their start and end apart: 12 -> 12, of which waited for: 10 -> 10; matrix products, arithmetic and copies ran while one was open for 2% -> 2% of each run, Pallas kernels for 6% -> 7%
where the time goes in v6:
time: 39.4 us; the launch traced here: 39.1 us
  starting transfers between devices  17.8 us (45%)
  waiting for transfers between devices  11.5 us (29%)
  Pallas kernels  6.54 us (17%)
  local copies, waits for them, and re-layouts  2.33 us (6%)
  between operations  0.86 us (2%)
    ppermute x3, starting transfers between devices, on_device(): came = lax.ppermute(sent, 'src', xor_pairs(peers, bits[level]))  6.14 us
    ppermute x2, starting transfers between devices, on_device(): picked = picked + lax.ppermute(picked, 'tile', xor_pairs(tiles, step))  3.83 us
    ppermute x2, waiting for transfers between devices, on_device(): lax.ppermute(terms[keep:], 'src', xor_pairs(peers, bits[level]))  3.14 us
    ppermute x1, starting transfers between devices, on_device(): came = lax.ppermute(terms[1], 'src', xor_pairs(peers, bits[-1]))  3.12 us
    ppermute x2, waiting for transfers between devices, on_device(): picked = picked + lax.ppermute(picked, 'tile', xor_pairs(tiles, step))  3 us
    ppermute x3, waiting for transfers between devices, on_device(): came = lax.ppermute(sent, 'src', xor_pairs(peers, bits[level]))  2.59 us
    ppermute x2, starting transfers between devices, on_device(): lax.ppermute(terms[keep:], 'src', xor_pairs(peers, bits[level]))  2.18 us
    ppermute x1, starting transfers between devices, on_device(): mine = lax.ppermute(payload, ('tile', 'src'), pairs)  1.9 us
  transfers between devices with their start and end apart: 12, of which 10 were waited for; matrix products, arithmetic and copies ran while one was open for 2% of the time, Pallas kernels for 7%

profile of v6, /device:TPU:0, one launch (start us, length us, event | category | flops | bytes accessed | tf_op | source)
XLA Modules:
  0.0 39.1 jit_solution(13368675482643069020)
XLA Ops:
  0.6 0.0 copy-start
  0.6 4.1 %collective-permute-start.2 = (f32[1,4,8,128]{3,2,1,0:T(8,128)}, f32[1,4,8,128]{3,2,1,0:T(8,128)S(1)}, u32[]{:S(2)}, u32[]{:S(2)}) collective-permute-start(f32[1,4,8,128]{3,2,1,0:T(8,128)} %bitcast.18), channel_id=1, source_target_pairs={{0,4},{1,5},{2,6},{3,7},{4,0},{5,1},{6,2},{7,3},{8,12},{9,13},{10,... | collective-permute-start | bytes 49160 | tf_op jit(solution)/shard_map/ppermute | solution.py:517
  4.7 0.0 collective-permute-start
  4.7 0.5 %collective-permute-start.1 = (f32[32,8,128]{2,1,0:T(8,128)}, f32[32,8,128]{2,1,0:T(8,128)S(1)}, u32[]{:S(2)}, u32[]{:S(2)}) collective-permute-start(f32[32,8,128]{2,1,0:T(8,128)} %bitcast.15), channel_id=1, source_target_pairs={{0,1},{1,0},{2,3},{3,2},{4,5},{5,4},{6,7},{7,6},{8,9},{9,8},{10,11... | collective-permute-start | bytes 393224 | tf_op jit(solution)/shard_map/ppermute | solution.py:511
  5.3 0.7 %pad.8 = f32[8,4,8,128]{3,2,1,0:T(8,128)S(1)} pad(f32[1,4,8,128]{3,2,1,0:T(8,128)} %bitcast.19, f32[]{:T(128)} %constant.37.clone.1), padding=0_7x0_0x0_0x0_0 | pad | bytes 147460 | tf_op jit(solution)/shard_map/jit(_pad)/pad | solution.py:514
  6.0 0.7 %collective-permute-done.2 = f32[1,4,8,128]{3,2,1,0:T(8,128)S(1)} collective-permute-done((f32[1,4,8,128]{3,2,1,0:T(8,128)}, f32[1,4,8,128]{3,2,1,0:T(8,128)S(1)}, u32[]{:S(2)}, u32[]{:S(2)}) %collective-permute-start.2) | collective-permute-done | bytes 16416 | tf_op jit(solution)/shard_map/ppermute | solution.py:517
  6.7 0.0 copy-start.9
  6.7 2.0 %collective-permute-start.3 = (f32[2,4,8,128]{3,2,1,0:T(8,128)S(1)}, f32[2,4,8,128]{3,2,1,0:T(8,128)S(1)}, u32[]{:S(2)}, u32[]{:S(2)}) collective-permute-start(f32[2,4,8,128]{3,2,1,0:T(8,128)S(1)} %slice.32), channel_id=1, source_target_pairs={{0,2},{1,3},{2,0},{3,1},{4,6},{5,7},{6,4},{7,5},{8,10},{9,11},{10,... | collective-permute-start | bytes 98312 | tf_op jit(solution)/shard_map/ppermute | solution.py:517
  8.7 0.0 copy-done.9
  8.7 0.0 collective-permute-done.other_v
  8.7 0.0 collective-permute-done.1.other_a
  8.7 0.0 copy-done
  8.7 0.0 copy-start.1
  8.7 0.9 %copy-done.1 = f32[1,32,8,128]{3,2,1,0:T(8,128)S(1)} copy-done((f32[1,32,8,128]{3,2,1,0:T(8,128)S(1)}, f32[1,32,8,128]{3,2,1,0:T(8,128)}, u32[]{:S(2)}) %copy-start.1) | copy-done | bytes 131096
  9.6 0.4 %shard_map.120 = (f32[14,8,128]{2,1,0:T(8,128)S(1)}, f32[8,4,8,128]{3,2,1,0:T(8,128)S(1)}) custom-call(f32[32,8,128]{2,1,0:T(8,128)S(1)} %bitcast.13, f32[32,8,128]{2,1,0:T(8,128)S(1)} %bitcast.16, f32[32,8,128]{2,1,0:T(8,128)S(1)} %collective-permute-done.other_v, ...), custom_call_target="tpu_custom_call", output_to_operand_aliasing={{1}: (4, {})} | custom-call | bytes 4000000 | tf_op jit(solution)/shard_map/pallas_call | solution.py:519
  10.0 0.7 %collective-permute-done.3 = f32[2,4,8,128]{3,2,1,0:T(8,128)S(1)} collective-permute-done((f32[2,4,8,128]{3,2,1,0:T(8,128)S(1)}, f32[2,4,8,128]{3,2,1,0:T(8,128)S(1)}, u32[]{:S(2)}, u32[]{:S(2)}) %collective-permute-start.3) | collective-permute-done | bytes 32800 | tf_op jit(solution)/shard_map/ppermute | solution.py:517
  10.7 0.1 collective-permute-start.4
  10.8 1.2 %collective-permute-done.4 = f32[4,4,8,128]{3,2,1,0:T(8,128)S(1)} collective-permute-done((f32[4,4,8,128]{3,2,1,0:T(8,128)S(1)}, f32[4,4,8,128]{3,2,1,0:T(8,128)S(1)}, u32[]{:S(2)}, u32[]{:S(2)}) %collective-permute-start.4) | collective-permute-done | bytes 65568 | tf_op jit(solution)/shard_map/ppermute | solution.py:517
  12.0 0.0 copy-start.3
  12.0 0.0 copy-start.4
  12.0 0.0 copy-start.7
  12.0 0.0 copy-start.8
  12.0 0.2 shard_map.121
  12.2 1.9 %collective-permute-start.5 = (f32[14,8,128]{2,1,0:T(8,128)S(1)}, f32[14,8,128]{2,1,0:T(8,128)S(1)}, u32[]{:S(2)}, u32[]{:S(2)}) collective-permute-start(f32[14,8,128]{2,1,0:T(8,128)S(1)} %get-tuple-element.31), channel_id=1, source_target_pairs={{0,8},{1,25},{2,10},{3,27},{4,12},{5,29},{6,14},{7,31},{8,0},{9,17... | collective-permute-start | bytes 172040 | tf_op jit(solution)/shard_map/ppermute | solution.py:542
  14.2 0.0 copy-start.5
  14.2 0.0 copy-start.6
  14.2 0.0 copy-done.3
  14.2 0.0 copy-done.4
  14.2 0.0 copy-done.7
  14.2 0.0 copy-done.8
  14.2 0.6 %copy-done.5 = f32[1,256]{1,0:T(1,128)S(1)} copy-done((f32[1,256]{1,0:T(1,128)S(1)}, f32[1,256]{1,0:T(1,128)}, u32[]{:S(2)}) %copy-start.5) | copy-done | bytes 1048
  14.8 0.0 copy-done.6
  14.8 1.0 %shard_map.122 = (f32[4,8,128]{2,1,0:T(8,128)S(1)}, f32[4,8,128]{2,1,0:T(8,128)S(1)}, f32[320,128]{1,0:T(8,128)S(1)}, f32[320,128]{1,0:T(8,128)S(1)}, f32[32,8,1...) custom-call(s32[1,2]{1,0:T(1,128)S(1)} %copy-done.6, ...), custom_call_target="tpu_custom_call" | custom-call | bytes 4000000 | tf_op jit(solution)/shard_map/pallas_call | solution.py:544
  15.8 0.8 %collective-permute-done.5.mine = f32[14,8,128]{2,1,0:T(8,128)S(1)} collective-permute-done((f32[14,8,128]{2,1,0:T(8,128)S(1)}, f32[14,8,128]{2,1,0:T(8,128)S(1)}, u32[]{:S(2)}, u32[]{:S(2)}) %collective-permute-start.5) | collective-permute-done | bytes 57376 | tf_op jit(solution)/shard_map/ppermute | solution.py:542
  16.6 0.1 collective-permute-start.6
  16.7 1.1 %collective-permute-done.6.theirs = f32[14,8,128]{2,1,0:T(8,128)S(1)} collective-permute-done((f32[14,8,128]{2,1,0:T(8,128)S(1)}, f32[14,8,128]{2,1,0:T(8,128)S(1)}, u32[]{:S(2)}, u32[]{:S(2)}) %collective-permute-start.6) | collective-permute-done | bytes 57376 | tf_op jit(solution)/shard_map/ppermute | solution.py:562
  17.9 0.0 copy-start.2
  17.9 1.6 %shard_map.123 = (f32[1,256]{1,0:T(1,128)S(1)}, f32[320,128]{1,0:T(8,128)S(1)}, f32[80,128]{1,0:T(8,128)S(1)}, f32[5,36,8,128]{3,2,1,0:T(8,128)S(1)}, f32[5,9,8,...) custom-call(f32[14,8,128]{2,1,0:T(8,128)S(1)} %collective-permute-done.5.mine, ...), custom_call_target="tpu_custom_call", output_to_operand_aliasing={{1}: (2, {}), {5}: (3, {})} | custom-call | tf_op jit(solution)/shard_map/pallas_call | solution.py:563
  19.5 2.3 %collective-permute-start.7 = (f32[1,256]{1,0:T(1,128)S(1)}, f32[1,256]{1,0:T(1,128)S(1)}, u32[]{:S(2)}, u32[]{:S(2)}) collective-permute-start(f32[1,256]{1,0:T(1,128)S(1)} %get-tuple-element.40), channel_id=1, source_target_pairs={{0,8},{8,0},{16,24},{24,16},{1,9},{9,1},{17,25},{25,17},{2,10},{10... | collective-permute-start | bytes 3080 | tf_op jit(solution)/shard_map/ppermute | solution.py:595
  21.7 1.5 %collective-permute-done.7 = f32[1,256]{1,0:T(1,128)S(1)} collective-permute-done((f32[1,256]{1,0:T(1,128)S(1)}, f32[1,256]{1,0:T(1,128)S(1)}, u32[]{:S(2)}, u32[]{:S(2)}) %collective-permute-start.7) | collective-permute-done | bytes 1056 | tf_op jit(solution)/shard_map/ppermute | solution.py:595
  23.3 1.6 %collective-permute-start.8 = (f32[1,256]{1,0:T(1,128)S(1)}, f32[1,256]{1,0:T(1,128)S(1)}, u32[]{:S(2)}, u32[]{:S(2)}) collective-permute-start(f32[1,256]{1,0:T(1,128)S(1)} %add.66), channel_id=1, source_target_pairs={{0,16},{8,24},{16,0},{24,8},{1,17},{9,25},{17,1},{25,9},{2,18},{10... | collective-permute-start | bytes 3080 | tf_op jit(solution)/shard_map/ppermute | solution.py:595
  24.9 0.0 copy-done.2
  24.9 0.5 %shard_map.124 = (f32[320,128]{1,0:T(8,128)S(1)}, f32[80,128]{1,0:T(8,128)S(1)}, bf16[256,512]{1,0:T(8,128)(2,1)S(1)}) custom-call(f32[14,8,128]{2,1,0:T(8,128)S(1)} %collective-permute-done.5.mine, f32[14,8,128]{2,1,0:T(8,128)S(1)} %collective-permute-done.6.theirs, f32[32,8,128]{2,1,0:T(8,128)S(1)} %bitcast.17, s32[8,512]{1,0:T(8,128)S(1)} %pad.9.spots, ...), custom_call_target="tpu_custom_call" | custom-call | bytes 4000000 | tf_op jit(solution)/shard_map/pallas_call | solution.py:579
  25.4 1.5 %collective-permute-done.8 = f32[1,256]{1,0:T(1,128)S(1)} collective-permute-done((f32[1,256]{1,0:T(1,128)S(1)}, f32[1,256]{1,0:T(1,128)S(1)}, u32[]{:S(2)}, u32[]{:S(2)}) %collective-permute-start.8) | collective-permute-done | bytes 1056 | tf_op jit(solution)/shard_map/ppermute | solution.py:595
  26.9 1.4 %shard_map.125 = (f32[8,4,8,128]{3,2,1,0:T(8,128)S(1)}, f32[320,128]{1,0:T(8,128)S(1)}, f32[320,128]{1,0:T(8,128)S(1)}, f32[80,128]{1,0:T(8,128)S(1)}) custom-call(f32[1,256]{1,0:T(1,128)S(1)} %add.67.picked.misfit, s32[8,512]{1,0:T(8,128)S(1)} %pad.9.spots, f32[320,128]{1,0:T(8,128)S(1)} %get-tuple-element.43.main_in, ...), custom_call_target="tpu_custom_call", output_to_operand_aliasing={{2}: (2, {}), {3}: (3, {})} | custom-call | tf_op jit(solution)/shard_map/pallas_call | solution.py:598
  28.3 0.1 collective-permute-start.9
  28.4 1.2 %collective-permute-done.9 = f32[4,4,8,128]{3,2,1,0:T(8,128)S(1)} collective-permute-done((f32[4,4,8,128]{3,2,1,0:T(8,128)S(1)}, f32[4,4,8,128]{3,2,1,0:T(8,128)S(1)}, u32[]{:S(2)}, u32[]{:S(2)}) %collective-permute-start.9) | collective-permute-done | bytes 65568 | tf_op jit(solution)/shard_map/ppermute | solution.py:628
  29.6 2.1 %collective-permute-start.10 = (f32[2,4,8,128]{3,2,1,0:T(8,128)S(1)}, f32[2,4,8,128]{3,2,1,0:T(8,128)S(1)}, u32[]{:S(2)}, u32[]{:S(2)}) collective-permute-start(f32[2,4,8,128]{3,2,1,0:T(8,128)S(1)} %slice.35), channel_id=1, source_target_pairs={{0,2},{1,3},{2,0},{3,1},{4,6},{5,7},{6,4},{7,5},{8,10},{9,11},{10,... | collective-permute-start | bytes 98312 | tf_op jit(solution)/shard_map/ppermute | solution.py:628
  31.8 1.9 %collective-permute-done.10 = f32[2,4,8,128]{3,2,1,0:T(8,128)S(1)} collective-permute-done((f32[2,4,8,128]{3,2,1,0:T(8,128)S(1)}, f32[2,4,8,128]{3,2,1,0:T(8,128)S(1)}, u32[]{:S(2)}, u32[]{:S(2)}) %collective-permute-start.10) | collective-permute-done | bytes 32800 | tf_op jit(solution)/shard_map/ppermute | solution.py:628
  33.7 3.1 %collective-permute-start.11 = (f32[4,8,128]{2,1,0:T(8,128)S(1)}, f32[4,8,128]{2,1,0:T(8,128)S(1)}, u32[]{:S(2)}, u32[]{:S(2)}) collective-permute-start(f32[4,8,128]{2,1,0:T(8,128)S(1)} %get-tuple-element.58), channel_id=1, source_target_pairs={{0,4},{1,5},{2,6},{3,7},{4,0},{5,1},{6,2},{7,3},{8,12},{9,13},{10,... | collective-permute-start | bytes 49160 | tf_op jit(solution)/shard_map/ppermute | solution.py:629
  36.8 0.8 %shard_map.126 = (f32[1,32,8,128]{3,2,1,0:T(8,128)}, f32[1,32,8,128]{3,2,1,0:T(8,128)}, f32[1,256]{1,0:T(1,128)}) custom-call(f32[320,128]{1,0:T(8,128)S(1)} %get-tuple-element.39.main_v.field, f32[320,128]{1,0:T(8,128)S(1)} %get-tuple-element.47.adjoint, f32[1,256]{1,0:T(1,128)S(1)} %add.67.picked.misfit), custom_call_target="tpu_custom_call" | custom-call | bytes 4000000 | tf_op jit(solution)/shard_map/pallas_call | solution.py:616
  37.6 0.9 %collective-permute-done.11.came = f32[4,8,128]{2,1,0:T(8,128)S(1)} collective-permute-done((f32[4,8,128]{2,1,0:T(8,128)S(1)}, f32[4,8,128]{2,1,0:T(8,128)S(1)}, u32[]{:S(2)}, u32[]{:S(2)}) %collective-permute-start.11) | collective-permute-done | bytes 16416 | tf_op jit(solution)/shard_map/ppermute | solution.py:629
  38.5 0.6 %shard_map.127 = f32[4,8,128]{2,1,0:T(8,128)} custom-call(f32[4,8,128]{2,1,0:T(8,128)S(1)} %get-tuple-element.51.scale, f32[4,8,128]{2,1,0:T(8,128)S(1)} %get-tuple-element.52.prior, f32[4,8,128]{2,1,0:T(8,128)S(1)} %get-tuple-element.59.kept, f32[4,8,128]{2,1,0:T(8,128)S(1)} %collective-permute-done.11.came), custom_call_target="tpu_custom_call" | custom-call | tf_op jit(solution)/shard_map/pallas_call | solution.py:630
  (18 shorter events, 0.1 us)
Async XLA Ops:
  0.6 8.0 %copy-start = (f32[1,32,8,128]{3,2,1,0:T(8,128)S(1)}, f32[1,32,8,128]{3,2,1,0:T(8,128)}, u32[]{:S(2)}) copy-start(f32[1,32,8,128]{3,2,1,0:T(8,128)} %param.16) | copy-start | bytes 393220
  0.6 6.0 %collective-permute-start.2 = (f32[1,4,8,128]{3,2,1,0:T(8,128)}, f32[1,4,8,128]{3,2,1,0:T(8,128)S(1)}, u32[]{:S(2)}, u32[]{:S(2)}) collective-permute-start(f32[1,4,8,128]{3,2,1,0:T(8,128)} %bitcast.18), channel_id=1, source_target_pairs={{0,4},{1,5},{2,6},{3,7},{4,0},{5,1},{6,2},{7,3},{8,12},{9,13},{10,... | collective-permute-start | bytes 49160 | tf_op jit(solution)/shard_map/ppermute | solution.py:517
  4.7 3.9 %collective-permute-start = (f32[32,8,128]{2,1,0:T(8,128)}, f32[32,8,128]{2,1,0:T(8,128)S(1)}, u32[]{:S(2)}, u32[]{:S(2)}) collective-permute-start(f32[32,8,128]{2,1,0:T(8,128)} %bitcast.12), channel_id=1, source_target_pairs={{0,1},{1,0},{2,3},{3,2},{4,5},{5,4},{6,7},{7,6},{8,9},{9,8},{10,11... | collective-permute-start | bytes 393224 | tf_op jit(solution)/shard_map/ppermute | solution.py:510
  4.7 3.9 %collective-permute-start.1 = (f32[32,8,128]{2,1,0:T(8,128)}, f32[32,8,128]{2,1,0:T(8,128)S(1)}, u32[]{:S(2)}, u32[]{:S(2)}) collective-permute-start(f32[32,8,128]{2,1,0:T(8,128)} %bitcast.15), channel_id=1, source_target_pairs={{0,1},{1,0},{2,3},{3,2},{4,5},{5,4},{6,7},{7,6},{8,9},{9,8},{10,11... | collective-permute-start | bytes 393224 | tf_op jit(solution)/shard_map/ppermute | solution.py:511
  6.7 2.0 %copy-start.9 = (s32[256,2]{0,1:T(2,128)S(1)}, s32[256,2]{0,1:T(2,128)}, u32[]{:S(2)}) copy-start(s32[256,2]{0,1:T(2,128)} %param.14) | copy-start | bytes 6148
  6.7 4.0 %collective-permute-start.3 = (f32[2,4,8,128]{3,2,1,0:T(8,128)S(1)}, f32[2,4,8,128]{3,2,1,0:T(8,128)S(1)}, u32[]{:S(2)}, u32[]{:S(2)}) collective-permute-start(f32[2,4,8,128]{3,2,1,0:T(8,128)S(1)} %slice.32), channel_id=1, source_target_pairs={{0,2},{1,3},{2,0},{3,1},{4,6},{5,7},{6,4},{7,5},{8,10},{9,11},{10,... | collective-permute-start | bytes 98312 | tf_op jit(solution)/shard_map/ppermute | solution.py:517
  8.7 0.9 %copy-start.1 = (f32[1,32,8,128]{3,2,1,0:T(8,128)S(1)}, f32[1,32,8,128]{3,2,1,0:T(8,128)}, u32[]{:S(2)}) copy-start(f32[1,32,8,128]{3,2,1,0:T(8,128)} %param.17) | copy-start | bytes 393220
  10.7 1.3 %collective-permute-start.4 = (f32[4,4,8,128]{3,2,1,0:T(8,128)S(1)}, f32[4,4,8,128]{3,2,1,0:T(8,128)S(1)}, u32[]{:S(2)}, u32[]{:S(2)}) collective-permute-start(f32[4,4,8,128]{3,2,1,0:T(8,128)S(1)} %slice.33), channel_id=1, source_target_pairs={{0,1},{1,0},{2,3},{3,2},{4,5},{5,4},{6,7},{7,6},{8,9},{9,8},{10,11... | collective-permute-start | bytes 196616 | tf_op jit(solution)/shard_map/ppermute | solution.py:517
  12.0 2.2 %copy-start.3 = (f32[4,8,128]{2,1,0:T(8,128)S(1)}, f32[4,8,128]{2,1,0:T(8,128)}, u32[]{:S(2)}) copy-start(f32[4,8,128]{2,1,0:T(8,128)} %own_model.1) | copy-start | bytes 49156
  12.0 2.2 %copy-start.4 = (s32[4,8,128]{2,1,0:T(8,128)S(1)}, s32[4,8,128]{2,1,0:T(8,128)}, u32[]{:S(2)}) copy-start(s32[4,8,128]{2,1,0:T(8,128)} %labels.1) | copy-start | bytes 49156
  12.0 2.2 %copy-start.7 = (f32[4]{0:T(128)S(1)}, f32[4]{0:T(128)}, u32[]{:S(2)}) copy-start(f32[4]{0:T(128)} %means.1) | copy-start | bytes 52
  12.0 2.2 %copy-start.8 = (f32[4]{0:T(128)S(1)}, f32[4]{0:T(128)}, u32[]{:S(2)}) copy-start(f32[4]{0:T(128)} %variances.1) | copy-start | bytes 52
  12.2 4.4 %collective-permute-start.5 = (f32[14,8,128]{2,1,0:T(8,128)S(1)}, f32[14,8,128]{2,1,0:T(8,128)S(1)}, u32[]{:S(2)}, u32[]{:S(2)}) collective-permute-start(f32[14,8,128]{2,1,0:T(8,128)S(1)} %get-tuple-element.31), channel_id=1, source_target_pairs={{0,8},{1,25},{2,10},{3,27},{4,12},{5,29},{6,14},{7,31},{8,0},{9,17... | collective-permute-start | bytes 172040 | tf_op jit(solution)/shard_map/ppermute | solution.py:542
  14.2 0.7 %copy-start.5 = (f32[1,256]{1,0:T(1,128)S(1)}, f32[1,256]{1,0:T(1,128)}, u32[]{:S(2)}) copy-start(f32[1,256]{1,0:T(1,128)} %observed.1) | copy-start | bytes 3076
  14.2 0.7 %copy-start.6 = (s32[1,2]{1,0:T(1,128)S(1)}, s32[1,2]{1,0:T(1,128)}, u32[]{:S(2)}) copy-start(s32[1,2]{1,0:T(1,128)} %cells.1) | copy-start | bytes 28
  16.6 1.2 %collective-permute-start.6 = (f32[14,8,128]{2,1,0:T(8,128)S(1)}, f32[14,8,128]{2,1,0:T(8,128)S(1)}, u32[]{:S(2)}, u32[]{:S(2)}) collective-permute-start(f32[14,8,128]{2,1,0:T(8,128)S(1)} %broadcast_add_fusion), channel_id=1, source_target_pairs={{0,1},{1,0},{2,3},{3,2},{4,5},{5,4},{6,7},{7,6},{8,9},{9,8},{10,11... | collective-permute-start | bytes 172040 | tf_op jit(solution)/shard_map/ppermute | solution.py:562
  17.9 7.0 %copy-start.2 = (f32[1,32,8,128]{3,2,1,0:T(8,128)S(1)}, f32[1,32,8,128]{3,2,1,0:T(8,128)}, u32[]{:S(2)}) copy-start(f32[1,32,8,128]{3,2,1,0:T(8,128)} %param.17) | copy-start | bytes 393220
  19.5 3.8 %collective-permute-start.7 = (f32[1,256]{1,0:T(1,128)S(1)}, f32[1,256]{1,0:T(1,128)S(1)}, u32[]{:S(2)}, u32[]{:S(2)}) collective-permute-start(f32[1,256]{1,0:T(1,128)S(1)} %get-tuple-element.40), channel_id=1, source_target_pairs={{0,8},{8,0},{16,24},{24,16},{1,9},{9,1},{17,25},{25,17},{2,10},{10... | collective-permute-start | bytes 3080 | tf_op jit(solution)/shard_map/ppermute | solution.py:595
  23.3 3.6 %collective-permute-start.8 = (f32[1,256]{1,0:T(1,128)S(1)}, f32[1,256]{1,0:T(1,128)S(1)}, u32[]{:S(2)}, u32[]{:S(2)}) collective-permute-start(f32[1,256]{1,0:T(1,128)S(1)} %add.66), channel_id=1, source_target_pairs={{0,16},{8,24},{16,0},{24,8},{1,17},{9,25},{17,1},{25,9},{2,18},{10... | collective-permute-start | bytes 3080 | tf_op jit(solution)/shard_map/ppermute | solution.py:595
  28.3 1.3 %collective-permute-start.9 = (f32[4,4,8,128]{3,2,1,0:T(8,128)S(1)}, f32[4,4,8,128]{3,2,1,0:T(8,128)S(1)}, u32[]{:S(2)}, u32[]{:S(2)}) collective-permute-start(f32[4,4,8,128]{3,2,1,0:T(8,128)S(1)} %slice.27), channel_id=1, source_target_pairs={{0,1},{1,0},{2,3},{3,2},{4,5},{5,4},{6,7},{7,6},{8,9},{9,8},{10,11... | collective-permute-start | bytes 196616 | tf_op jit(solution)/shard_map/ppermute | solution.py:628
  29.6 4.0 %collective-permute-start.10 = (f32[2,4,8,128]{3,2,1,0:T(8,128)S(1)}, f32[2,4,8,128]{3,2,1,0:T(8,128)S(1)}, u32[]{:S(2)}, u32[]{:S(2)}) collective-permute-start(f32[2,4,8,128]{3,2,1,0:T(8,128)S(1)} %slice.35), channel_id=1, source_target_pairs={{0,2},{1,3},{2,0},{3,1},{4,6},{5,7},{6,4},{7,5},{8,10},{9,11},{10,... | collective-permute-start | bytes 98312 | tf_op jit(solution)/shard_map/ppermute | solution.py:628
  33.7 4.8 %collective-permute-start.11 = (f32[4,8,128]{2,1,0:T(8,128)S(1)}, f32[4,8,128]{2,1,0:T(8,128)S(1)}, u32[]{:S(2)}, u32[]{:S(2)}) collective-permute-start(f32[4,8,128]{2,1,0:T(8,128)S(1)} %get-tuple-element.58), channel_id=1, source_target_pairs={{0,4},{1,5},{2,6},{3,7},{4,0},{5,1},{6,2},{7,3},{8,12},{9,13},{10,... | collective-permute-start | bytes 49160 | tf_op jit(solution)/shard_map/ppermute | solution.py:629
